TPU v7x, 512 devices: a whole 4x8x8 slice. The times are simulated.
512 devices in a mesh: row: 8 (over z), col: 16 (over y, core), layer: 4 (over x).
Axes of the slice: x: 4, y: 8, z: 8, core: 2. Of those that a mesh axis runs over, the one named last changes fastest.
Arguments:
- matrix: bfloat16 [8192, 8192], P('row', ('col', 'layer')), may hold values from -6 to 6
- list_x: int32 [256, 40], P('row'), may hold values from 0 to 255, all different within a row; in each aligned block of 32 rows (0 to 31, 32 to 63, ...) at most 10 rows name the same one
- list_sq: int32 [256, 60], P('row'), may hold values from 0 to 255, all different within a row
- list_out: int32 [256, 40], P('row'), may hold values from 0 to 255, all different within a row
Outputs:
- updated: bfloat16 [8192, 8192], P('row', ('col', 'layer'))
Inputs may be any that keep to these rules, and one draw needn't show every extreme that they name: `list_x`: each row holds distinct block column numbers; within each aligned group of 32 block rows (the rows of one device along row) no block column appears in more than 10 rows. `list_sq`: each row holds distinct block column numbers. `list_out`: each row holds distinct block column numbers.
All inputs are finite; a program needn't handle non-finite values.
Results may differ from a plain program's by a relative error of at most 0.004.
Values may be sent and summed in bfloat16 or wider, within the bound.
No kernel may reach another device: no remote copies, remote signals or barrier semaphores. Data moves between devices by JAX's collectives and lax.ppermute only.
A program may use at most 128 MiB of HBM per device.

v0:
```python
import jax
import jax.numpy as jnp
from jax import lax
from jax.sharding import PartitionSpec as P

B = 32
NB = 256
KX = 40
KSQ = 60


def block_hits(lists, column_ids):
    return jnp.any(lists[:, :, None] == column_ids[None, None, :], axis=1)


def local(matrix, list_x, list_sq, list_out):
    scale_square = (NB / (KX * KX * B)) ** 0.5
    scale_cube = (NB / (KX * KSQ * B)) ** 0.5
    local_rows = list_x.shape[0]
    width = matrix.shape[1]
    tile_blocks = width // B
    layer_count = lax.axis_size("layer")
    layer_index = lax.axis_index("layer")
    col_base = (lax.axis_index("col") * layer_count + layer_index) * tile_blocks
    own_ids = col_base + jnp.arange(tile_blocks, dtype=jnp.int32)

    def tile_mask(lists):
        hit = block_hits(lists, own_ids)
        return jnp.broadcast_to(hit[:, None, :, None], (local_rows, B, tile_blocks, B)).reshape(
            local_rows * B, width
        )

    sparse = jnp.where(tile_mask(list_x), matrix, jnp.zeros_like(matrix))

    def right_factor(tile):
        units = tile.shape[0] // width
        shaped = tile.reshape(units // layer_count, layer_count, width, width)
        swapped = lax.all_to_all(shaped, "layer", split_axis=1, concat_axis=3, tiled=True)
        swapped = swapped.reshape(units // layer_count * width, layer_count * width)
        return lax.all_gather(swapped, "row", axis=0, tiled=True)

    def product(tile):
        right_side = right_factor(tile)
        partial_value = jnp.dot(
            lax.all_gather(sparse, "col", axis=1, tiled=True),
            right_side,
            preferred_element_type=jnp.float32,
        )
        return lax.psum_scatter(partial_value, "layer", scatter_dimension=1, tiled=True)

    square = jnp.where(tile_mask(list_sq), product(sparse) * scale_square, jnp.float32(0.0)).astype(
        jnp.bfloat16
    )
    cube = product(square) * scale_cube
    result = 1.5 * sparse.astype(jnp.float32) - 0.5 * cube
    return jnp.where(tile_mask(list_out), result, jnp.float32(0.0)).astype(jnp.bfloat16)


def solution(mesh):
    placed = (P("row", ("col", "layer")), P("row", None), P("row", None), P("row", None))
    return jax.shard_map(
        local, mesh=mesh, in_specs=placed, out_specs=P("row", ("col", "layer")), check_vma=False
    )
```

profile of v0, /device:TPU:1, one launch (start us, length us, event | category | flops | bytes accessed | tf_op | source)
XLA Modules:
  0.0 266.4 jit_solution(12621094748157483494)
XLA Ops:
  6.5 1.0 compare_reduce_fusion.1
  7.7 0.3 broadcast_in_dim.13
  8.0 0.6 reshape.34
  8.7 1.0 broadcast_select_fusion
  9.7 10.2 %all_to_all.30 = bf16[2,4,128,128]{3,2,0,1:T(8,128)(2,1)S(1)} all-to-all(bf16[2,4,128,128]{3,2,0,1:T(8,128)(2,1)S(1)} %copy.14), channel_id=1, replica_groups=mesh['row'=8,'col'=16,'layer'=4] {'layer'}, dimensions={1} | all-to-all | bytes 524288 | tf_op jit(solution)/shard_map/all_to_all | solution.py:38
  20.1 0.7 copy.23
  20.9 0.7 all-gather.4.cloned.1.call-update
  21.6 44.2 %all-gather.6.cloned.1.call-done = bf16[2048,512]{1,0:T(8,128)(2,1)} async-done(((bf16[256,512]{1,0:T(8,128)(2,1)}), bf16[2048,512]{1,0:T(8,128)(2,1)}) %all-gather.6.cloned.1.call-update) | async-done | bytes 2097168 | tf_op jit(solution)/shard_map/all_gather | solution.py:40
  65.8 57.3 %all-gather.4.cloned.1.call-done = bf16[1024,2048]{1,0:T(8,128)(2,1)} async-done(((bf16[1024,128]{1,0:T(8,128)(2,1)}), bf16[1024,2048]{1,0:T(8,128)(2,1)}) %all-gather.4.cloned.1.call-update) | async-done | bytes 4194320 | tf_op jit(solution)/shard_map/all_gather | solution.py:45
  123.1 6.5 %fusion = f32[1024,512]{1,0:T(8,128)} fusion(bf16[1024,2048]{1,0:T(8,128)(2,1)} %all-gather.4.cloned.1.call-done, bf16[2048,512]{1,0:T(8,128)(2,1)} %all-gather.6.cloned.1.call-done), kind=kOutput, calls=%fused_computation.9 | convolution fusion | flops 2147483648 | bytes 8388608 | tf_op jit(solution)/shard_map/dot_general | solution.py:44
  129.7 0.6 copy-done.2
  130.3 0.2 compare_reduce_fusion
  130.7 0.3 broadcast_in_dim.16
  131.0 0.6 reshape.35
  131.6 30.7 %reduce-scatter.3.cloned.1.call-done = f32[1024,128]{1,0:T(8,128)} async-done(((f32[1024,512]{1,0:T(8,128)}), f32[1024,128]{1,0:T(8,128)}) %reduce-scatter.3.cloned.1.call-update) | async-done | bytes 524304 | tf_op jit(solution)/shard_map/reduce_scatter | solution.py:49
  162.4 1.1 select_convert_fusion.1
  163.5 8.1 %all_to_all.31 = bf16[2,4,128,128]{3,2,0,1:T(8,128)(2,1)S(1)} all-to-all(bf16[2,4,128,128]{3,2,0,1:T(8,128)(2,1)S(1)} %copy.16), channel_id=1, replica_groups=mesh['row'=8,'col'=16,'layer'=4] {'layer'}, dimensions={1} | all-to-all | bytes 524288 | tf_op jit(solution)/shard_map/all_to_all | solution.py:38
  171.8 0.7 copy.22
  172.6 41.4 %all-gather.8.cloned.1.call-done = bf16[2048,512]{1,0:T(8,128)(2,1)} async-done(((bf16[256,512]{1,0:T(8,128)(2,1)}), bf16[2048,512]{1,0:T(8,128)(2,1)}) %all-gather.8.cloned.1.call-update) | async-done | bytes 2097168 | tf_op jit(solution)/shard_map/all_gather | solution.py:40
  214.1 6.5 %fusion.1 = f32[1024,512]{1,0:T(8,128)} fusion(bf16[1024,2048]{1,0:T(8,128)(2,1)} %all-gather.4.cloned.1.call-done, bf16[2048,512]{1,0:T(8,128)(2,1)} %all-gather.8.cloned.1.call-done), kind=kOutput, calls=%fused_computation.10 | convolution fusion | flops 2147483648 | bytes 8388608 | tf_op jit(solution)/shard_map/dot_general | solution.py:44
  220.7 0.3 broadcast_in_dim.12
  221.1 0.6 reshape.33
  221.7 36.3 %reduce-scatter.5.cloned.1.call-done = f32[1024,128]{1,0:T(8,128)} async-done(((f32[1024,512]{1,0:T(8,128)}), f32[1024,128]{1,0:T(8,128)}) %reduce-scatter.5.cloned.1.call-update) | async-done | bytes 524304 | tf_op jit(solution)/shard_map/reduce_scatter | solution.py:49
  257.9 1.9 select_convert_fusion
  (22 shorter events, 1.0 us)
Async XLA Ops:
  6.5 59.3 %all-gather.6.cloned.1.call-start = ((), (), s32[]{:S(2)}) async-start(), calls=%async_computation.5 | async-start | bytes 2359296 | tf_op jit(solution)/shard_map/all_gather | solution.py:40
  9.6 11.2 %copy-start = (bf16[1024,128]{1,0:T(8,128)(2,1)}, bf16[1024,128]{1,0:T(8,128)(2,1)S(1)}, u32[]{:S(2)}) copy-start(bf16[1024,128]{1,0:T(8,128)(2,1)S(1)} %broadcast_select_fusion) | copy-start | bytes 786436
  20.8 102.3 %all-gather.4.cloned.1.call-start = ((), (), s32[]{:S(2)}) async-start(), calls=%async_computation.4 | async-start | bytes 4456448 | tf_op jit(solution)/shard_map/all_gather | solution.py:45
  21.6 140.8 %reduce-scatter.3.cloned.1.call-start = ((), (), s32[]{:S(2)}) async-start(), calls=%async_computation.6 | async-start | bytes 2621440 | tf_op jit(solution)/shard_map/reduce_scatter | solution.py:49
  129.6 0.7 copy-start.2
  129.6 84.4 %all-gather.8.cloned.1.call-start = ((), (), s32[]{:S(2)}) async-start(), calls=%async_computation.7 | async-start | bytes 2359296 | tf_op jit(solution)/shard_map/all_gather | solution.py:40
  172.6 85.4 %reduce-scatter.5.cloned.1.call-start = ((), (), s32[]{:S(2)}) async-start(), calls=%async_computation.8 | async-start | bytes 2621440 | tf_op jit(solution)/shard_map/reduce_scatter | solution.py:49
  220.6 37.4 %copy-start.1 = (bf16[1024,128]{1,0:T(8,128)(2,1)S(1)}, bf16[1024,128]{1,0:T(8,128)(2,1)}, u32[]{:S(2)}) copy-start(bf16[1024,128]{1,0:T(8,128)(2,1)} %copy-done) | copy-start | bytes 786436
Sparse Core Ops, SparseCore 0:
  20.9 44.8 all-gather.5
  67.8 55.1 all-gather.3
  129.8 32.5 reduce-scatter.2
  172.7 41.3 all-gather.7
  220.7 37.1 reduce-scatter.4
where the time goes:
time: 267 us; the launch traced here: 266 us
  waiting for transfers between devices  211 us (79%)
  blocking collectives  18.3 us (7%)
  between operations  13.2 us (5%)
  matrix products  13.1 us (5%)
  local copies, waits for them, and re-layouts  5.81 us (2%)
  other arithmetic  5.23 us (2%)
    all_gather x2, waiting for transfers between devices, right_factor(): return lax.all_gather(swapped, 'row', axis=0, tiled=True)  85.6 us
    reduce_scatter x2, waiting for transfers between devices, product(): lax.psum_scatter(partial_value, 'layer', scatter_dimension=1, tiled=True)  67 us
    all_gather x1, waiting for transfers between devices, product(): lax.all_gather(sparse, 'col', axis=1, tiled=True)  57.3 us
    all_to_all x2, blocking collectives, right_factor(): lax.all_to_all(shaped, 'layer', split_axis=1, concat_axis=3, tiled=True)  18.3 us
    dot_general x2, matrix products, product(): jnp.dot(lax.all_gather(sparse, 'col', axis=1, tiled=True), right_side, pr...  13.1 us
  transfers between devices with their start and end apart: 5, of which 5 were waited for; matrix products, arithmetic and copies ran while one was open for 1% of the time, Pallas kernels for 0%

commit v1 on v0

v1 whole, which is shorter than its diff:
```python
import functools

import jax
import jax.numpy as jnp
from jax import lax
from jax.experimental import pallas as pl
from jax.experimental.pallas import tpu as pltpu
from jax.sharding import PartitionSpec as P

B = 32
NB = 256
KX = 40
KSQ = 60
CAP = 10
ROWS = 1024
W = 128
BR = ROWS // B
GROUPS = 8
PER = 8
F32 = jnp.float32
BF16 = jnp.bfloat16
MIB = 1 << 20


def lane_hits(lists, base):
    ids = base + lax.broadcasted_iota(jnp.int32, (BR, W), 1) // B
    hit = jnp.zeros((BR, W), F32)
    for t in range(lists.shape[1]):
        hit = jnp.where(lists[:, t : t + 1] == ids, 1.0, hit)
    return hit


def slots_of(hit):
    below = lax.broadcasted_iota(jnp.int32, (BR, BR), 1) < lax.broadcasted_iota(
        jnp.int32, (BR, BR), 0
    )
    rank = jnp.dot(
        jnp.where(below, 1.0, 0.0).astype(BF16), hit.astype(BF16), preferred_element_type=F32
    )
    return jnp.where(hit > 0.0, rank, float(CAP))


def pack_kernel(base_ref, list_ref, tile_ref, pay_ref, left_ref, table_ref):
    lists = list_ref[...]
    hit = lane_hits(lists, base_ref[0])
    slot = slots_of(hit)
    slot_int = slot.astype(jnp.int32)
    packed = [jnp.zeros((B, W), F32) for _ in range(CAP)]
    for i in range(BR):
        block = tile_ref[pl.ds(i * B, B), :].astype(F32)
        row = jnp.broadcast_to(slot_int[i : i + 1, :], (B, W))
        for s in range(min(i + 1, CAP)):
            packed[s] = jnp.where(row == s, block, packed[s])
    for s in range(CAP):
        value = packed[s].astype(BF16)
        pay_ref[pl.ds(s * B, B), :] = value
        left_ref[pl.ds(s * B, B), :] = value
    pay_ref[pl.ds(CAP * B, B), :] = slot.astype(BF16)

    ids = lax.broadcasted_iota(jnp.int32, (BR, NB), 1)
    every = jnp.zeros((BR, NB), F32)
    for t in range(KX):
        every = jnp.where(lists[:, t : t + 1] == ids, 1.0, every)
    table_ref[...] = slots_of(every).astype(jnp.int32) * B


def pack(base, list_x, tile):
    return pl.pallas_call(
        pack_kernel,
        out_shape=(
            jax.ShapeDtypeStruct(((CAP + 1) * B, W), BF16),
            jax.ShapeDtypeStruct((CAP * B, W), BF16),
            jax.ShapeDtypeStruct((BR, NB), jnp.int32),
        ),
        in_specs=[
            pl.BlockSpec(memory_space=pltpu.SMEM),
            pl.BlockSpec(memory_space=pltpu.VMEM),
            pl.BlockSpec(memory_space=pltpu.VMEM),
        ],
        out_specs=(pl.BlockSpec(memory_space=pltpu.VMEM),) * 3,
        compiler_params=pltpu.CompilerParams(vmem_limit_bytes=8 * MIB),
        cost_estimate=pl.CostEstimate(flops=10_000_000, bytes_accessed=500_000, transcendentals=0),
        name="pack",
    )(base, list_x, tile)


def right_kernel(at_ref, base_ref, lx_ref, lsq_ref, lout_ref, *refs):
    pays, (right_ref, masks_ref) = refs[:9], refs[9:]
    masks_ref[0] = lane_hits(lx_ref[...], base_ref[0])
    masks_ref[1] = lane_hits(lsq_ref[...], base_ref[0])
    masks_ref[2] = lane_hits(lout_ref[...], base_ref[0])
    for p in range(GROUPS):
        if p < GROUPS - 1:
            part = [pays[p][pl.ds(s * B, B), :].astype(F32) for s in range(CAP + 1)]
        else:
            half = pays[p].shape[0]
            part = [pays[p][pl.ds(s * B, B), :].astype(F32) for s in range(half // B)]
            part += [pays[p + 1][pl.ds(s * B, B), :].astype(F32) for s in range(CAP + 1 - half // B)]
        slot = part[CAP].astype(jnp.int32)
        g = at_ref[p]
        for i in range(BR):
            row = jnp.broadcast_to(slot[i : i + 1, :], (B, W))
            value = jnp.zeros((B, W), F32)
            for s in range(min(i + 1, CAP)):
                value = jnp.where(row == s, part[s], value)
            right_ref[g, pl.ds(i * B, B), :] = value.astype(BF16)


def right(at, base, list_x, list_sq, list_out, pays):
    smem = pl.BlockSpec(memory_space=pltpu.SMEM)
    vmem = pl.BlockSpec(memory_space=pltpu.VMEM)
    return pl.pallas_call(
        right_kernel,
        out_shape=(
            jax.ShapeDtypeStruct((GROUPS, ROWS, W), BF16),
            jax.ShapeDtypeStruct((3, BR, W), F32),
        ),
        in_specs=[smem, smem] + [vmem] * (3 + len(pays)),
        out_specs=(vmem, vmem),
        compiler_params=pltpu.CompilerParams(vmem_limit_bytes=16 * MIB),
        cost_estimate=pl.CostEstimate(flops=30_000_000, bytes_accessed=3_000_000, transcendentals=0),
        name="right",
    )(at, base, list_x, list_sq, list_out, *pays)


def square_kernel(
    scale, slots_ref, left_ref, right_ref, masks_ref, square_ref, dense_ref, held, dense, acc, in_sems, out_sems
):
    def fetch(g):
        return pltpu.make_async_copy(
            left_ref.at[pl.ds(g * PER, PER)],
            held.at[pl.ds(g * PER, PER), pl.ds(0, CAP * B)],
            in_sems.at[g],
        )

    def put(g):
        return pltpu.make_async_copy(dense.at[g % 2], dense_ref.at[g], out_sems.at[g % 2])

    for g in range(GROUPS):
        fetch(g).start()
    held[:, pl.ds(CAP * B, B), :] = jnp.zeros((GROUPS * PER, B, W), BF16)
    lane = lax.broadcasted_iota(jnp.int32, (B, W), 1)
    for g in range(GROUPS):
        fetch(g).wait()
        if g >= 2:
            put(g - 2).wait()

        @pl.loop(0, BR)
        def _(i):
            for q in range(PER):
                d = g * PER + q
                blocks = [
                    held[d, pl.ds(pl.multiple_of(slots_ref[i, d * 4 + c], B), B), :] for c in range(4)
                ]
                value = jnp.where(
                    lane < 2 * B,
                    jnp.where(lane < B, blocks[0], blocks[1]),
                    jnp.where(lane < 3 * B, blocks[2], blocks[3]),
                )
                dense[g % 2, pl.ds(pl.multiple_of(i * B, B), B), pl.ds(q * W, W)] = value

        put(g).start()
        part = jnp.dot(dense[g % 2], right_ref[g], preferred_element_type=F32)
        acc[...] = part if g == 0 else acc[...] + part
    for i in range(BR):
        keep = jnp.broadcast_to(masks_ref[1, i : i + 1, :], (B, W))
        value = acc[pl.ds(i * B, B), :] * scale
        square_ref[pl.ds(i * B, B), :] = jnp.where(keep > 0.0, value, 0.0).astype(BF16)
    put(GROUPS - 2).wait()
    put(GROUPS - 1).wait()


def square_of(slots, left, right_side, masks):
    scale = (NB / (KX * KX * B)) ** 0.5
    smem = pl.BlockSpec(memory_space=pltpu.SMEM)
    vmem = pl.BlockSpec(memory_space=pltpu.VMEM)
    hbm = pl.BlockSpec(memory_space=pl.ANY)
    return pl.pallas_call(
        functools.partial(square_kernel, scale),
        out_shape=(
            jax.ShapeDtypeStruct((ROWS, W), BF16),
            jax.ShapeDtypeStruct((GROUPS, ROWS, GROUPS * W), BF16),
        ),
        in_specs=[smem, hbm, vmem, vmem],
        out_specs=(vmem, hbm),
        scratch_shapes=[
            pltpu.VMEM((GROUPS * PER, (CAP + 1) * B, W), BF16),
            pltpu.VMEM((2, ROWS, PER * W), BF16),
            pltpu.VMEM((ROWS, W), F32),
            pltpu.SemaphoreType.DMA((GROUPS,)),
            pltpu.SemaphoreType.DMA((2,)),
        ],
        compiler_params=pltpu.CompilerParams(vmem_limit_bytes=32 * MIB),
        cost_estimate=pl.CostEstimate(
            flops=2 * ROWS * GROUPS * ROWS * W, bytes_accessed=24 * MIB, transcendentals=0
        ),
        name="square",
    )(slots, left, right_side, masks)


STEP = 256


def cube_part(at, dense, pieces, acc=None, last=None):
    scale = (NB / (KX * KSQ * B)) ** 0.5
    count = len(pieces)
    spans = [piece[0].shape[0] for piece in pieces]

    def kernel(at_ref, *refs):
        refs = list(refs)
        total = refs.pop(0)[...] if acc is not None else None
        for p in range(count):
            left_ref = refs.pop(0)
            start = 0
            for _ in pieces[p]:
                piece_ref = refs.pop(0)
                size = piece_ref.shape[0]
                term = jnp.dot(
                    left_ref[0, :, pl.ds(start, size)], piece_ref[...], preferred_element_type=F32
                )
                total = term if total is None else total + term
                start += size
        out_ref = refs[-1]
        if last is None:
            out_ref[...] = total
            return
        tile_ref, masks_ref = refs[0], refs[1]
        for k in range(STEP // B):
            rows = pl.ds(k * B, B)
            keep_x = jnp.broadcast_to(masks_ref[0, k : k + 1, :], (B, W))
            keep_out = jnp.broadcast_to(masks_ref[2, k : k + 1, :], (B, W))
            sparse = jnp.where(keep_x > 0.0, tile_ref[rows, :].astype(F32), 0.0)
            cube = total[k * B : (k + 1) * B, :] * scale
            result = 1.5 * sparse - 0.5 * cube
            out_ref[rows, :] = jnp.where(keep_out > 0.0, result, 0.0).astype(BF16)

    operands, specs = [], []
    rows_spec = pl.BlockSpec((STEP, W), lambda i, at_ref: (i, 0))
    if acc is not None:
        operands.append(acc)
        specs.append(rows_spec)
    for p in range(count):
        operands.append(dense)
        specs.append(
            pl.BlockSpec((1, STEP, GROUPS * W), lambda i, at_ref, p=p: (at_ref[p], i, 0))
        )
        for piece in pieces[p]:
            operands.append(piece)
            specs.append(pl.BlockSpec(piece.shape, lambda i, at_ref: (0, 0)))
    if last is not None:
        tile, masks = last
        operands += [tile, masks]
        specs += [rows_spec, pl.BlockSpec((3, STEP // B, W), lambda i, at_ref: (0, i, 0))]
    del spans
    return pl.pallas_call(
        kernel,
        out_shape=jax.ShapeDtypeStruct((ROWS, W), F32 if last is None else BF16),
        grid_spec=pltpu.PrefetchScalarGridSpec(
            num_scalar_prefetch=1,
            grid=(ROWS // STEP,),
            in_specs=specs,
            out_specs=rows_spec,
        ),
        compiler_params=pltpu.CompilerParams(vmem_limit_bytes=24 * MIB),
        cost_estimate=pl.CostEstimate(
            flops=2 * ROWS * ROWS * W * count,
            bytes_accessed=count * 3 * MIB + MIB,
            transcendentals=0,
        ),
        name="cube_last" if last is not None else "cube_part",
    )(at, *operands)


def ring_steps(own, cut):
    ahead = [(i, (i + 1) % GROUPS) for i in range(GROUPS)]
    back = [(i, (i - 1) % GROUPS) for i in range(GROUPS)]
    steps, down, up = [], own, own
    for distance in range(1, GROUPS // 2 + 1):
        if distance == GROUPS // 2:
            down, up = down[:cut], up[cut:]
        down = lax.ppermute(down, "row", ahead)
        up = lax.ppermute(up, "row", back)
        steps.append((down, up))
    return steps


def local(matrix, list_x, list_sq, list_out):
    layers = lax.axis_size("layer")
    tile = lax.axis_index("col") * layers + lax.axis_index("layer")
    base = jnp.reshape(tile * (W // B), (1,)).astype(jnp.int32)
    row = lax.axis_index("row").astype(jnp.int32)
    near = jnp.stack([row, row - 1, row + 1, row - 2, row + 2, row - 3, row + 3, row + 4])
    near = jnp.bitwise_and(near, GROUPS - 1)

    pay, left, slots = pack(base, list_x, matrix)
    lefts = lax.all_gather(left, ("col", "layer"), axis=0, tiled=False)
    hops = ring_steps(pay, 6 * B)
    pays = [pay] + [piece for hop in hops for piece in hop]
    right_side, masks = right(near, base, list_x, list_sq, list_out, pays)

    square, dense = square_of(slots, lefts, right_side, masks)

    hops = ring_steps(square, ROWS // 2)
    acc = cube_part(near[0:1], dense, [(square,)])
    for distance in range(1, GROUPS // 2):
        down, up = hops[distance - 1]
        acc = cube_part(near[2 * distance - 1 : 2 * distance + 1], dense, [(down,), (up,)], acc)
    down, up = hops[-1]
    return cube_part(near[7:8], dense, [(down, up)], acc, (matrix, masks))


def solution(mesh):
    placed = (P("row", ("col", "layer")), P("row", None), P("row", None), P("row", None))
    return jax.shard_map(
        local, mesh=mesh, in_specs=placed, out_specs=P("row", ("col", "layer")), check_vma=False
    )
```

time: 267 us -> 193 us (0.72)
  the two profiles are of different devices: /device:TPU:1 before, /device:TPU:2 now
where the time goes in v1:
time: 193 us; the launch traced here: 192 us
  starting transfers between devices  63.2 us (33%)
  waiting for transfers between devices  59.3 us (31%)
  Pallas kernels  42.8 us (22%)
  between operations  13.7 us (7%)
  local copies, waits for them, and re-layouts  12.9 us (7%)
    all_gather x1, waiting for transfers between devices, local(): lefts = lax.all_gather(left, ('col', 'layer'), axis=0, tiled=False)  47.1 us
    ppermute x8, starting transfers between devices, ring_steps(): up = lax.ppermute(up, 'row', back)  43.5 us
    pallas_call x1, Pallas kernels, square_of(): pl.pallas_call(functools.partial(square_kernel, scale), out_shape=(jax.Sh...  26.9 us
    ppermute x8, starting transfers between devices, ring_steps(): down = lax.ppermute(down, 'row', ahead)  19.7 us
    unnamed x18, local copies, waits for them, and re-layouts  12.1 us
    pallas_call x5, Pallas kernels, cube_part(): pl.pallas_call(kernel, out_shape=jax.ShapeDtypeStruct((ROWS, W), F32 if l...  11.7 us
    ppermute x8, waiting for transfers between devices, ring_steps(): down = lax.ppermute(down, 'row', ahead)  10.5 us
  transfers between devices with their start and end apart: 17, of which 7 were waited for; matrix products, arithmetic and copies ran while one was open for 0% of the time, Pallas kernels for 6%

profile of v1, /device:TPU:2, one launch (start us, length us, event | category | flops | bytes accessed | tf_op | source)
XLA Modules:
  0.0 191.9 jit_solution(16590683777640792840)
XLA Ops:
  9.5 4.3 %collective-permute-start = (bf16[352,128]{1,0:T(8,128)(2,1)S(1)}, bf16[352,128]{1,0:T(8,128)(2,1)S(1)}, u32[]{:S(2)}, u32[]{:S(2)}) collective-permute-start(bf16[352,128]{1,0:T(8,128)(2,1)S(1)} %get-tuple-element.14.refs_0_), channel_id=1, source_target_pairs={{0,64},{64,128},{128,192},{192,256},{256,320},{320,384},{384,448},... | collective-permute-start | bytes 270344 | tf_op jit(solution)/shard_map/ppermute | solution.py:281
  13.8 8.6 %collective-permute-start.1 = (bf16[352,128]{1,0:T(8,128)(2,1)S(1)}, bf16[352,128]{1,0:T(8,128)(2,1)S(1)}, u32[]{:S(2)}, u32[]{:S(2)}) collective-permute-start(bf16[352,128]{1,0:T(8,128)(2,1)S(1)} %get-tuple-element.14.refs_0_), channel_id=1, source_target_pairs={{0,448},{64,0},{128,64},{192,128},{256,192},{320,256},{384,320},{4... | collective-permute-start | bytes 270344 | tf_op jit(solution)/shard_map/ppermute | solution.py:282
  25.0 5.1 %collective-permute-start.3 = (bf16[352,128]{1,0:T(8,128)(2,1)S(1)}, bf16[352,128]{1,0:T(8,128)(2,1)S(1)}, u32[]{:S(2)}, u32[]{:S(2)}) collective-permute-start(bf16[352,128]{1,0:T(8,128)(2,1)S(1)} %collective-permute-done.1.refs_2_), channel_id=1, source_target_pairs={{0,448},{64,0},{128,64},{192,128},{256,192},{320,256},{384,320},{4... | collective-permute-start | bytes 270344 | tf_op jit(solution)/shard_map/ppermute | solution.py:282
  32.6 5.1 %collective-permute-start.5 = (bf16[352,128]{1,0:T(8,128)(2,1)S(1)}, bf16[352,128]{1,0:T(8,128)(2,1)S(1)}, u32[]{:S(2)}, u32[]{:S(2)}) collective-permute-start(bf16[352,128]{1,0:T(8,128)(2,1)S(1)} %collective-permute-done.3.refs_4_), channel_id=1, source_target_pairs={{0,448},{64,0},{128,64},{192,128},{256,192},{320,256},{384,320},{4... | collective-permute-start | bytes 270344 | tf_op jit(solution)/shard_map/ppermute | solution.py:282
  38.3 1.9 collective-permute-start.6
  40.3 5.1 %collective-permute-start.7 = (bf16[160,128]{1,0:T(8,128)(2,1)S(1)}, bf16[160,128]{1,0:T(8,128)(2,1)S(1)}, u32[]{:S(2)}, u32[]{:S(2)}) collective-permute-start(bf16[160,128]{1,0:T(8,128)(2,1)S(1)} %slice.37), channel_id=1, source_target_pairs={{0,448},{64,0},{128,64},{192,128},{256,192},{320,256},{384,320},{4... | collective-permute-start | bytes 122888 | tf_op jit(solution)/shard_map/ppermute | solution.py:282
  49.2 3.0 %right.1 = (bf16[8,1024,128]{2,1,0:T(8,128)(2,1)S(1)}, f32[3,32,128]{2,1,0:T(8,128)S(1)}) custom-call(s32[8]{0:T(128)S(1)} %broadcast_and_fusion.at_ref, s32[1]{0:T(128)} %bitcast.8.base_ref, s32[32,40]{1,0:T(8,128)S(1)} %copy-done.5, s32[32,60]{1,0:T(8,128)S(1)} %copy-done.6, s32[32,40]{1,0:T(8,128)S(1)} %copy-done.7, ...), custom_call_target="tpu_custom_call" | custom-call | flops 30000000 | bytes 3000000 | tf_op jit(solution)/shard_map/right/pallas_call | solution.py:112
  52.2 47.1 %all-gather.3.cloned.1.call-done = bf16[20480,128]{1,0:T(8,128)(2,1)} async-done(((bf16[320,128]{1,0:T(8,128)(2,1)}), bf16[20480,128]{1,0:T(8,128)(2,1)}) %all-gather.3.cloned.1.call-update) | async-done | bytes 5242896 | tf_op jit(solution)/shard_map/all_gather | solution.py:296
  99.3 2.5 %copy-done.8 = bf16[20480,128]{1,0:T(8,128)(2,1)S(1)} copy-done((bf16[20480,128]{1,0:T(8,128)(2,1)S(1)}, bf16[20480,128]{1,0:T(8,128)(2,1)}, u32[]{:S(2)}) %copy-start.8) | copy-done | bytes 5242904
  101.8 26.9 %square.1 = (bf16[1024,128]{1,0:T(8,128)(2,1)S(1)}, bf16[8,1024,1024]{2,1,0:T(8,128)(2,1)}) custom-call(s32[32,256]{1,0:T(8,128)S(1)} %get-tuple-element.12.slots_ref, bf16[64,320,128]{2,1,0:T(8,128)(2,1)S(1)} %bitcast.10, bf16[8,1024,128]{2,1,0:T(8,128)(2,1)S(1)} %get-tuple-element.15.right_ref, f32[3,32,128]{2,1,0:T(8,128)S(1)} %get-tuple-element.16.masks_ref.refs_5_), custom_call_target="tpu_custom_call" | custom-call | flops 2147483648 | bytes 25165824 | tf_op jit(solution)/shard_map/square/pallas_call | solution.py:178
  128.7 3.6 %collective-permute-start.8 = (bf16[1024,128]{1,0:T(8,128)(2,1)S(1)}, bf16[1024,128]{1,0:T(8,128)(2,1)S(1)}, u32[]{:S(2)}, u32[]{:S(2)}) collective-permute-start(bf16[1024,128]{1,0:T(8,128)(2,1)S(1)} %get-tuple-element.18.refs_1_), channel_id=1, source_target_pairs={{0,64},{64,128},{128,192},{192,256},{256,320},{320,384},{384,448},... | collective-permute-start | bytes 786440 | tf_op jit(solution)/shard_map/ppermute | solution.py:281
  132.3 4.2 %collective-permute-start.9 = (bf16[1024,128]{1,0:T(8,128)(2,1)S(1)}, bf16[1024,128]{1,0:T(8,128)(2,1)S(1)}, u32[]{:S(2)}, u32[]{:S(2)}) collective-permute-start(bf16[1024,128]{1,0:T(8,128)(2,1)S(1)} %get-tuple-element.18.refs_1_), channel_id=1, source_target_pairs={{0,448},{64,0},{128,64},{192,128},{256,192},{320,256},{384,320},{4... | collective-permute-start | bytes 786440 | tf_op jit(solution)/shard_map/ppermute | solution.py:282
  136.5 4.8 %collective-permute-done.8.refs_2_ = bf16[1024,128]{1,0:T(8,128)(2,1)S(1)} collective-permute-done((bf16[1024,128]{1,0:T(8,128)(2,1)S(1)}, bf16[1024,128]{1,0:T(8,128)(2,1)S(1)}, u32[]{:S(2)}, u32[]{:S(2)}) %collective-permute-start.8) | collective-permute-done | bytes 262176 | tf_op jit(solution)/shard_map/ppermute | solution.py:281
  143.2 5.1 %collective-permute-start.11 = (bf16[1024,128]{1,0:T(8,128)(2,1)S(1)}, bf16[1024,128]{1,0:T(8,128)(2,1)S(1)}, u32[]{:S(2)}, u32[]{:S(2)}) collective-permute-start(bf16[1024,128]{1,0:T(8,128)(2,1)S(1)} %collective-permute-done.9.refs_4_), channel_id=1, source_target_pairs={{0,448},{64,0},{128,64},{192,128},{256,192},{320,256},{384,320},{4... | collective-permute-start | bytes 786440 | tf_op jit(solution)/shard_map/ppermute | solution.py:282
  148.4 4.0 %collective-permute-done.10.refs_2_ = bf16[1024,128]{1,0:T(8,128)(2,1)S(1)} collective-permute-done((bf16[1024,128]{1,0:T(8,128)(2,1)S(1)}, bf16[1024,128]{1,0:T(8,128)(2,1)S(1)}, u32[]{:S(2)}, u32[]{:S(2)}) %collective-permute-start.10) | collective-permute-done | bytes 262176 | tf_op jit(solution)/shard_map/ppermute | solution.py:281
  154.3 5.1 %collective-permute-start.13 = (bf16[1024,128]{1,0:T(8,128)(2,1)S(1)}, bf16[1024,128]{1,0:T(8,128)(2,1)S(1)}, u32[]{:S(2)}, u32[]{:S(2)}) collective-permute-start(bf16[1024,128]{1,0:T(8,128)(2,1)S(1)} %collective-permute-done.11.refs_4_), channel_id=1, source_target_pairs={{0,448},{64,0},{128,64},{192,128},{256,192},{320,256},{384,320},{4... | collective-permute-start | bytes 786440 | tf_op jit(solution)/shard_map/ppermute | solution.py:282
  160.2 5.8 %copy-done = bf16[8,1024,1024]{2,1,0:T(8,128)(2,1)S(1)} copy-done((bf16[8,1024,1024]{2,1,0:T(8,128)(2,1)S(1)}, bf16[8,1024,1024]{2,1,0:T(8,128)(2,1)}, u32[]{:S(2)}) %copy-start) | copy-done | bytes 16777240
  165.9 2.0 %cube_part.4.refs_0_ = f32[1024,128]{1,0:T(8,128)S(1)} custom-call(s32[1]{0:T(128)} %get-tuple-element.19.at_ref, bf16[8,1024,1024]{2,1,0:T(8,128)(2,1)S(1)} %copy-done, bf16[1024,128]{1,0:T(8,128)(2,1)S(1)} %get-tuple-element.18.refs_1_), custom_call_target="tpu_custom_call" | custom-call | flops 268435456 | bytes 4194304 | tf_op jit(solution)/shard_map/cube_part/pallas_call | solution.py:255
  168.0 2.3 %collective-permute-start.14 = (bf16[512,128]{1,0:T(8,128)(2,1)S(1)}, bf16[512,128]{1,0:T(8,128)(2,1)S(1)}, u32[]{:S(2)}, u32[]{:S(2)}) collective-permute-start(bf16[512,128]{1,0:T(8,128)(2,1)S(1)} %slice.38), channel_id=1, source_target_pairs={{0,64},{64,128},{128,192},{192,256},{256,320},{320,384},{384,448},... | collective-permute-start | bytes 393224 | tf_op jit(solution)/shard_map/ppermute | solution.py:281
  170.3 5.0 %collective-permute-start.15 = (bf16[512,128]{1,0:T(8,128)(2,1)S(1)}, bf16[512,128]{1,0:T(8,128)(2,1)S(1)}, u32[]{:S(2)}, u32[]{:S(2)}) collective-permute-start(bf16[512,128]{1,0:T(8,128)(2,1)S(1)} %slice.39), channel_id=1, source_target_pairs={{0,448},{64,0},{128,64},{192,128},{256,192},{320,256},{384,320},{4... | collective-permute-start | bytes 393224 | tf_op jit(solution)/shard_map/ppermute | solution.py:282
  175.3 2.3 %cube_part.5.refs_0_ = f32[1024,128]{1,0:T(8,128)S(1)} custom-call(s32[2]{0:T(128)S(1)} %get-tuple-element.21.at_ref, f32[1024,128]{1,0:T(8,128)S(1)} %cube_part.4.refs_0_, bf16[8,1024,1024]{2,1,0:T(8,128)(2,1)S(1)} %copy-done.1, bf16[1024,128]{1,0:T(8,128)(2,1)S(1)} %collective-permute-done.8.refs_2_, bf16[8,1024,1024]{2,1,0:T(8,128)(2,1)S(1)} %copy-done.1, ...), custom_call_target="tpu_custom_call" | custom-call | flops 536870912 | bytes 7340032 | tf_op jit(solution)/shard_map/cube_part/pallas_call | solution.py:255
  177.6 2.3 %cube_part.6.refs_0_ = f32[1024,128]{1,0:T(8,128)S(1)} custom-call(s32[2]{0:T(128)S(1)} %get-tuple-element.22.at_ref, f32[1024,128]{1,0:T(8,128)S(1)} %cube_part.5.refs_0_, bf16[8,1024,1024]{2,1,0:T(8,128)(2,1)S(1)} %copy-done.1, bf16[1024,128]{1,0:T(8,128)(2,1)S(1)} %collective-permute-done.10.refs_2_, bf16[8,1024,1024]{2,1,0:T(8,128)(2,1)S(1)} %copy-done.1, ...), custom_call_target="tpu_custom_call" | custom-call | flops 536870912 | bytes 7340032 | tf_op jit(solution)/shard_map/cube_part/pallas_call | solution.py:255
  179.9 2.3 %cube_part.7.refs_0_ = f32[1024,128]{1,0:T(8,128)S(1)} custom-call(s32[2]{0:T(128)S(1)} %get-tuple-element.23.at_ref, f32[1024,128]{1,0:T(8,128)S(1)} %cube_part.6.refs_0_, bf16[8,1024,1024]{2,1,0:T(8,128)(2,1)S(1)} %copy-done.1, bf16[1024,128]{1,0:T(8,128)(2,1)S(1)} %collective-permute-done.12.refs_2_, bf16[8,1024,1024]{2,1,0:T(8,128)(2,1)S(1)} %copy-done.1, ...), custom_call_target="tpu_custom_call" | custom-call | flops 536870912 | bytes 7340032 | tf_op jit(solution)/shard_map/cube_part/pallas_call | solution.py:255
  182.2 2.9 %cube_last.1 = bf16[1024,128]{1,0:T(8,128)(2,1)} custom-call(s32[1]{0:T(128)} %get-tuple-element.20.at_ref, f32[1024,128]{1,0:T(8,128)S(1)} %cube_part.7.refs_0_, bf16[8,1024,1024]{2,1,0:T(8,128)(2,1)S(1)} %copy-done.1, bf16[512,128]{1,0:T(8,128)(2,1)S(1)} %collective-permute-done.14.refs_2_, bf16[512,128]{1,0:T(8,128)(2,1)S(1)} %collective-permute-done.15.refs_3_, ...), custom_call_target="tpu_custom_call" | custom-call | flops 268435456 | bytes 4194304 | tf_op jit(solution)/shard_map/cube_last/pallas_call | solution.py:255
  (45 shorter events, 17.0 us)
Async XLA Ops:
  6.5 92.8 %all-gather.3.cloned.1.call-start = ((), (), s32[]{:S(2)}) async-start(), calls=%async_computation | async-start | bytes 5324800 | tf_op jit(solution)/shard_map/all_gather | solution.py:296
  6.5 0.9 copy-start.2
  9.5 13.6 %collective-permute-start = (bf16[352,128]{1,0:T(8,128)(2,1)S(1)}, bf16[352,128]{1,0:T(8,128)(2,1)S(1)}, u32[]{:S(2)}, u32[]{:S(2)}) collective-permute-start(bf16[352,128]{1,0:T(8,128)(2,1)S(1)} %get-tuple-element.14.refs_0_), channel_id=1, source_target_pairs={{0,64},{64,128},{128,192},{192,256},{256,320},{320,384},{384,448},... | collective-permute-start | bytes 270344 | tf_op jit(solution)/shard_map/ppermute | solution.py:281
  13.8 11.2 %collective-permute-start.1 = (bf16[352,128]{1,0:T(8,128)(2,1)S(1)}, bf16[352,128]{1,0:T(8,128)(2,1)S(1)}, u32[]{:S(2)}, u32[]{:S(2)}) collective-permute-start(bf16[352,128]{1,0:T(8,128)(2,1)S(1)} %get-tuple-element.14.refs_0_), channel_id=1, source_target_pairs={{0,448},{64,0},{128,64},{192,128},{256,192},{320,256},{384,320},{4... | collective-permute-start | bytes 270344 | tf_op jit(solution)/shard_map/ppermute | solution.py:282
  23.1 7.6 %collective-permute-start.2 = (bf16[352,128]{1,0:T(8,128)(2,1)S(1)}, bf16[352,128]{1,0:T(8,128)(2,1)S(1)}, u32[]{:S(2)}, u32[]{:S(2)}) collective-permute-start(bf16[352,128]{1,0:T(8,128)(2,1)S(1)} %collective-permute-done.refs_1_), channel_id=1, source_target_pairs={{0,64},{64,128},{128,192},{192,256},{256,320},{320,384},{384,448},... | collective-permute-start | bytes 270344 | tf_op jit(solution)/shard_map/ppermute | solution.py:281
  25.0 7.6 %collective-permute-start.3 = (bf16[352,128]{1,0:T(8,128)(2,1)S(1)}, bf16[352,128]{1,0:T(8,128)(2,1)S(1)}, u32[]{:S(2)}, u32[]{:S(2)}) collective-permute-start(bf16[352,128]{1,0:T(8,128)(2,1)S(1)} %collective-permute-done.1.refs_2_), channel_id=1, source_target_pairs={{0,448},{64,0},{128,64},{192,128},{256,192},{320,256},{384,320},{4... | collective-permute-start | bytes 270344 | tf_op jit(solution)/shard_map/ppermute | solution.py:282
  30.7 7.6 %collective-permute-start.4 = (bf16[352,128]{1,0:T(8,128)(2,1)S(1)}, bf16[352,128]{1,0:T(8,128)(2,1)S(1)}, u32[]{:S(2)}, u32[]{:S(2)}) collective-permute-start(bf16[352,128]{1,0:T(8,128)(2,1)S(1)} %collective-permute-done.2.refs_3_), channel_id=1, source_target_pairs={{0,64},{64,128},{128,192},{192,256},{256,320},{320,384},{384,448},... | collective-permute-start | bytes 270344 | tf_op jit(solution)/shard_map/ppermute | solution.py:281
  32.6 7.6 %collective-permute-start.5 = (bf16[352,128]{1,0:T(8,128)(2,1)S(1)}, bf16[352,128]{1,0:T(8,128)(2,1)S(1)}, u32[]{:S(2)}, u32[]{:S(2)}) collective-permute-start(bf16[352,128]{1,0:T(8,128)(2,1)S(1)} %collective-permute-done.3.refs_4_), channel_id=1, source_target_pairs={{0,448},{64,0},{128,64},{192,128},{256,192},{320,256},{384,320},{4... | collective-permute-start | bytes 270344 | tf_op jit(solution)/shard_map/ppermute | solution.py:282
  38.3 8.7 %collective-permute-start.6 = (bf16[192,128]{1,0:T(8,128)(2,1)S(1)}, bf16[192,128]{1,0:T(8,128)(2,1)S(1)}, u32[]{:S(2)}, u32[]{:S(2)}) collective-permute-start(bf16[192,128]{1,0:T(8,128)(2,1)S(1)} %slice.36), channel_id=1, source_target_pairs={{0,64},{64,128},{128,192},{192,256},{256,320},{320,384},{384,448},... | collective-permute-start | bytes 147464 | tf_op jit(solution)/shard_map/ppermute | solution.py:281
  40.3 6.8 %collective-permute-start.7 = (bf16[160,128]{1,0:T(8,128)(2,1)S(1)}, bf16[160,128]{1,0:T(8,128)(2,1)S(1)}, u32[]{:S(2)}, u32[]{:S(2)}) collective-permute-start(bf16[160,128]{1,0:T(8,128)(2,1)S(1)} %slice.37), channel_id=1, source_target_pairs={{0,448},{64,0},{128,64},{192,128},{256,192},{320,256},{384,320},{4... | collective-permute-start | bytes 122888 | tf_op jit(solution)/shard_map/ppermute | solution.py:282
  47.1 0.7 copy-start.5
  48.5 0.7 copy-start.7
  99.3 2.5 %copy-start.8 = (bf16[20480,128]{1,0:T(8,128)(2,1)S(1)}, bf16[20480,128]{1,0:T(8,128)(2,1)}, u32[]{:S(2)}) copy-start(bf16[20480,128]{1,0:T(8,128)(2,1)} %all-gather.3.cloned.1.call-done) | copy-start | bytes 15728644
  128.7 12.6 %collective-permute-start.8 = (bf16[1024,128]{1,0:T(8,128)(2,1)S(1)}, bf16[1024,128]{1,0:T(8,128)(2,1)S(1)}, u32[]{:S(2)}, u32[]{:S(2)}) collective-permute-start(bf16[1024,128]{1,0:T(8,128)(2,1)S(1)} %get-tuple-element.18.refs_1_), channel_id=1, source_target_pairs={{0,64},{64,128},{128,192},{192,256},{256,320},{320,384},{384,448},... | collective-permute-start | bytes 786440 | tf_op jit(solution)/shard_map/ppermute | solution.py:281
  132.3 10.9 %collective-permute-start.9 = (bf16[1024,128]{1,0:T(8,128)(2,1)S(1)}, bf16[1024,128]{1,0:T(8,128)(2,1)S(1)}, u32[]{:S(2)}, u32[]{:S(2)}) collective-permute-start(bf16[1024,128]{1,0:T(8,128)(2,1)S(1)} %get-tuple-element.18.refs_1_), channel_id=1, source_target_pairs={{0,448},{64,0},{128,64},{192,128},{256,192},{320,256},{384,320},{4... | collective-permute-start | bytes 786440 | tf_op jit(solution)/shard_map/ppermute | solution.py:282
  141.3 11.1 %collective-permute-start.10 = (bf16[1024,128]{1,0:T(8,128)(2,1)S(1)}, bf16[1024,128]{1,0:T(8,128)(2,1)S(1)}, u32[]{:S(2)}, u32[]{:S(2)}) collective-permute-start(bf16[1024,128]{1,0:T(8,128)(2,1)S(1)} %collective-permute-done.8.refs_2_), channel_id=1, source_target_pairs={{0,64},{64,128},{128,192},{192,256},{256,320},{320,384},{384,448},... | collective-permute-start | bytes 786440 | tf_op jit(solution)/shard_map/ppermute | solution.py:281
  143.2 11.1 %collective-permute-start.11 = (bf16[1024,128]{1,0:T(8,128)(2,1)S(1)}, bf16[1024,128]{1,0:T(8,128)(2,1)S(1)}, u32[]{:S(2)}, u32[]{:S(2)}) collective-permute-start(bf16[1024,128]{1,0:T(8,128)(2,1)S(1)} %collective-permute-done.9.refs_4_), channel_id=1, source_target_pairs={{0,448},{64,0},{128,64},{192,128},{256,192},{320,256},{384,320},{4... | collective-permute-start | bytes 786440 | tf_op jit(solution)/shard_map/ppermute | solution.py:282
  152.4 15.6 %collective-permute-start.12 = (bf16[1024,128]{1,0:T(8,128)(2,1)S(1)}, bf16[1024,128]{1,0:T(8,128)(2,1)S(1)}, u32[]{:S(2)}, u32[]{:S(2)}) collective-permute-start(bf16[1024,128]{1,0:T(8,128)(2,1)S(1)} %collective-permute-done.10.refs_2_), channel_id=1, source_target_pairs={{0,64},{64,128},{128,192},{192,256},{256,320},{320,384},{384,448},... | collective-permute-start | bytes 786440 | tf_op jit(solution)/shard_map/ppermute | solution.py:281
  154.3 16.0 %collective-permute-start.13 = (bf16[1024,128]{1,0:T(8,128)(2,1)S(1)}, bf16[1024,128]{1,0:T(8,128)(2,1)S(1)}, u32[]{:S(2)}, u32[]{:S(2)}) collective-permute-start(bf16[1024,128]{1,0:T(8,128)(2,1)S(1)} %collective-permute-done.11.refs_4_), channel_id=1, source_target_pairs={{0,448},{64,0},{128,64},{192,128},{256,192},{320,256},{384,320},{4... | collective-permute-start | bytes 786440 | tf_op jit(solution)/shard_map/ppermute | solution.py:282
  160.2 5.8 %copy-start = (bf16[8,1024,1024]{2,1,0:T(8,128)(2,1)S(1)}, bf16[8,1024,1024]{2,1,0:T(8,128)(2,1)}, u32[]{:S(2)}) copy-start(bf16[8,1024,1024]{2,1,0:T(8,128)(2,1)} %get-tuple-element.17.refs_0_.refs_1_.refs_3_) | copy-start | bytes 50331652
  165.9 9.4 %copy-start.1 = (bf16[8,1024,1024]{2,1,0:T(8,128)(2,1)S(1)}, bf16[8,1024,1024]{2,1,0:T(8,128)(2,1)}, u32[]{:S(2)}) copy-start(bf16[8,1024,1024]{2,1,0:T(8,128)(2,1)} %get-tuple-element.17.refs_0_.refs_1_.refs_3_) | copy-start | bytes 50331652
  168.0 14.2 %collective-permute-start.14 = (bf16[512,128]{1,0:T(8,128)(2,1)S(1)}, bf16[512,128]{1,0:T(8,128)(2,1)S(1)}, u32[]{:S(2)}, u32[]{:S(2)}) collective-permute-start(bf16[512,128]{1,0:T(8,128)(2,1)S(1)} %slice.38), channel_id=1, source_target_pairs={{0,64},{64,128},{128,192},{192,256},{256,320},{320,384},{384,448},... | collective-permute-start | bytes 393224 | tf_op jit(solution)/shard_map/ppermute | solution.py:281
  170.3 11.9 %collective-permute-start.15 = (bf16[512,128]{1,0:T(8,128)(2,1)S(1)}, bf16[512,128]{1,0:T(8,128)(2,1)S(1)}, u32[]{:S(2)}, u32[]{:S(2)}) collective-permute-start(bf16[512,128]{1,0:T(8,128)(2,1)S(1)} %slice.39), channel_id=1, source_target_pairs={{0,448},{64,0},{128,64},{192,128},{256,192},{320,256},{384,320},{4... | collective-permute-start | bytes 393224 | tf_op jit(solution)/shard_map/ppermute | solution.py:282
  179.9 2.3 %copy-start.3 = (bf16[1024,128]{1,0:T(8,128)(2,1)S(1)}, bf16[1024,128]{1,0:T(8,128)(2,1)}, u32[]{:S(2)}) copy-start(bf16[1024,128]{1,0:T(8,128)(2,1)} %refs_4_.1) | copy-start | bytes 786436
  (2 other events, 1.4 us)
Sparse Core Ops, SparseCore 0:
  10.7 88.5 all-gather.2

commit v2 on v0

v2 whole, which is shorter than its diff:
```python
import jax
import jax.numpy as jnp
from jax import lax
from jax.experimental import pallas as pl
from jax.experimental.pallas import tpu as pltpu
from jax.sharding import PartitionSpec as P

B = 32
NB = 256
KX = 40
KSQ = 60
CAP = 10
ROWS = 1024
W = 128
BR = ROWS // B
GROUPS = 8
TILES = 4
HALF = TILES * W
PAY = 576
F32 = jnp.float32
BF16 = jnp.bfloat16
MIB = 1 << 20
SMEM = pl.BlockSpec(memory_space=pltpu.SMEM)
VMEM = pl.BlockSpec(memory_space=pltpu.VMEM)
HBM = pl.BlockSpec(memory_space=pl.ANY)


def params(limit):
    return pltpu.CompilerParams(vmem_limit_bytes=limit * MIB)


def cost(flops, size):
    return pl.CostEstimate(flops=flops, bytes_accessed=size, transcendentals=0)


def copies_in(pairs, sems):
    copies = [pltpu.make_async_copy(a, b, sems.at[k]) for k, (a, b) in enumerate(pairs)]
    for copy in copies:
        copy.start()
    for copy in copies:
        copy.wait()


def lane_hits(lists, base):
    ids = base + lax.broadcasted_iota(jnp.int32, (BR, W), 1) // B
    hit = jnp.zeros((BR, W), F32)
    for t in range(lists.shape[1]):
        hit = jnp.where(lists[:, t : t + 1] == ids, 1.0, hit)
    return hit


def slots_of(hit):
    below = lax.broadcasted_iota(jnp.int32, (BR, BR), 1) < lax.broadcasted_iota(
        jnp.int32, (BR, BR), 0
    )
    rank = jnp.dot(
        jnp.where(below, 1.0, 0.0).astype(BF16), hit.astype(BF16), preferred_element_type=F32
    )
    return jnp.where(hit > 0.0, rank, float(CAP))


def pack_kernel(base_ref, list_hbm, tile_hbm, pay_ref, left_ref, slots_ref, list_ref, tile_ref, sems):
    copies_in([(list_hbm, list_ref), (tile_hbm, tile_ref)], sems)
    lists = list_ref[...]
    hit = lane_hits(lists, base_ref[0])
    slot = slots_of(hit)
    slot_int = slot.astype(jnp.int32)
    packed = [jnp.zeros((B, W), F32) for _ in range(CAP)]
    for i in range(BR):
        block = tile_ref[pl.ds(i * B, B), :].astype(F32)
        row = jnp.broadcast_to(slot_int[i : i + 1, :], (B, W))
        for s in range(min(i + 1, CAP)):
            packed[s] = jnp.where(row == s, block, packed[s])
    for s in range(CAP):
        value = packed[s].astype(BF16)
        pay_ref[pl.ds(s * B, B), :] = value
        left_ref[s] = value
    pay_ref[pl.ds(CAP * B, B), :] = slot.astype(BF16)
    pay_ref[pl.ds((CAP + 1) * B, PAY - (CAP + 1) * B), :] = jnp.zeros(
        (PAY - (CAP + 1) * B, W), BF16
    )

    ids = lax.broadcasted_iota(jnp.int32, (BR, NB), 1)
    every = jnp.zeros((BR, NB), F32)
    for t in range(KX):
        every = jnp.where(lists[:, t : t + 1] == ids, 1.0, every)
    slots_ref[...] = slots_of(every).astype(jnp.int32)


def pack(base, list_x, tile):
    return pl.pallas_call(
        pack_kernel,
        out_shape=(
            jax.ShapeDtypeStruct((PAY, W), BF16),
            jax.ShapeDtypeStruct((CAP, B, W), BF16),
            jax.ShapeDtypeStruct((BR, NB), jnp.int32),
        ),
        in_specs=[SMEM, HBM, HBM],
        out_specs=(VMEM,) * 3,
        scratch_shapes=[
            pltpu.VMEM((BR, KX), jnp.int32),
            pltpu.VMEM((ROWS, W), BF16),
            pltpu.SemaphoreType.DMA((2,)),
        ],
        compiler_params=params(48),
        cost_estimate=cost(10_000_000, 500_000),
        name="pack",
    )(base, list_x, tile)


def order_kernel(table_ref, *refs):
    tiles, out_ref, sems = refs[:TILES], refs[TILES], refs[TILES + 1]
    copies_in([(tile, out_ref.at[table_ref[k]]) for k, tile in enumerate(tiles)], sems)


def order(table, tiles):
    return pl.pallas_call(
        order_kernel,
        out_shape=jax.ShapeDtypeStruct((TILES, CAP, B, W), BF16),
        in_specs=[SMEM] + [HBM] * TILES,
        out_specs=HBM,
        scratch_shapes=[pltpu.SemaphoreType.DMA((TILES,))],
        cost_estimate=cost(0, 700_000),
        name="order",
    )(table, *tiles)


def right_kernel(table_ref, base_ref, *refs):
    lists_hbm, mine_hbm, other_hbm, right_ref, masks_ref = refs[:3], *refs[3:7]
    lists, pays_ref, sems = refs[7:10], refs[10], refs[11]
    rows = pl.ds(0, (CAP + 1) * B)
    pairs = list(zip(lists_hbm, lists))
    pairs += [(ref.at[:, rows], pays_ref.at[k]) for k, ref in enumerate((mine_hbm, other_hbm))]
    copies_in(pairs, sems)
    for k in range(3):
        masks_ref[k] = lane_hits(lists[k][...], base_ref[0])

    @pl.loop(0, 2 * TILES)
    def _(h):
        g, core = table_ref[TILES + 2 * h], table_ref[TILES + 2 * h + 1]
        first = pl.multiple_of(CAP * B + core * (BR // 2), BR // 2)
        for k in range(2):
            part = [pays_ref[k, g, pl.ds(s * B, B), :].astype(F32) for s in range(CAP)]
            slot = pays_ref[k, g, pl.ds(first, BR // 2), :].astype(F32).astype(jnp.int32)
            for t in range(BR // 2):
                row = jnp.broadcast_to(slot[t : t + 1, :], (B, W))
                value = jnp.zeros((B, W), F32)
                for s in range(CAP):
                    value = jnp.where(row == s, part[s], value)
                right_ref[h, pl.ds(t * B, B), pl.ds(k * W, W)] = value.astype(BF16)


def right(table, base, lists, mine, other):
    return pl.pallas_call(
        right_kernel,
        out_shape=(
            jax.ShapeDtypeStruct((2 * TILES, HALF, 2 * W), BF16),
            jax.ShapeDtypeStruct((3, BR, W), F32),
        ),
        in_specs=[SMEM, SMEM] + [HBM] * 5,
        out_specs=(VMEM, VMEM),
        scratch_shapes=[pltpu.VMEM(a.shape, jnp.int32) for a in lists]
        + [
            pltpu.VMEM((2, GROUPS, (CAP + 1) * B, W), BF16),
            pltpu.SemaphoreType.DMA((5,)),
        ],
        compiler_params=params(48),
        cost_estimate=cost(40_000_000, 4 * MIB),
        name="right",
    )(table, base, *lists, mine, other)


def grow(halves, places, table, slots, dense=None, right_side=None, acc=None, split=False):
    count = len(halves)

    def kernel(table_ref, slots_ref, *refs):
        refs = list(refs)
        packed = [refs.pop(0) for _ in halves]
        right_ref = refs.pop(0) if right_side is not None else None
        acc_ref = refs.pop(0) if acc is not None else None
        if dense is not None:
            refs.pop(0)
        held, wide, sems = refs[-3:]
        dense_ref, outs = refs[0], refs[1:-3]

        held[:, :, CAP] = jnp.zeros((count, TILES, B, W), F32)
        lane = lax.broadcasted_iota(jnp.int32, (B, W), 1)
        puts = []
        total = None
        for k in range(count):
            for q in range(TILES):
                for s in range(CAP):
                    held[k, q, s] = packed[k][q, s].astype(F32)
            g, core = table_ref[places[k]], table_ref[places[k] + 1]
            first = (g * 2 + core) * TILES * (W // B)

            @pl.loop(0, BR)
            def _(i):
                for q in range(TILES):
                    part = [held[k, q, slots_ref[i, first + 4 * q + c]] for c in range(4)]
                    value = jnp.where(
                        lane < 2 * B,
                        jnp.where(lane < B, part[0], part[1]),
                        jnp.where(lane < 3 * B, part[2], part[3]),
                    )
                    wide[k, pl.ds(pl.multiple_of(i * B, B), B), pl.ds(q * W, W)] = value.astype(BF16)

            put = pltpu.make_async_copy(wide.at[k], dense_ref.at[g, core], sems.at[k])
            put.start()
            puts.append(put)
            if right_ref is not None:
                at = (places[k] - TILES) // 2
                term = jnp.dot(wide[k], right_ref[at], preferred_element_type=F32)
                total = term if total is None else total + term
        if right_ref is not None:
            if acc_ref is not None:
                total = total + acc_ref[...]
            if split:
                outs[0][...] = total[:, :W]
                outs[1][...] = total[:, W:]
            else:
                outs[0][...] = total
        for put in puts:
            put.wait()

    operands, specs = [table, slots, *halves], [SMEM, SMEM] + [VMEM] * count
    shapes = [jax.ShapeDtypeStruct((GROUPS, 2, ROWS, HALF), BF16)]
    if right_side is not None:
        operands.append(right_side)
        specs.append(VMEM)
        shapes += [jax.ShapeDtypeStruct((ROWS, W), F32)] * 2 if split else [
            jax.ShapeDtypeStruct((ROWS, 2 * W), F32)
        ]
    if acc is not None:
        operands.append(acc)
        specs.append(VMEM)
    aliases = {}
    if dense is not None:
        aliases = {len(operands): 0}
        operands.append(dense)
        specs.append(HBM)
    return pl.pallas_call(
        kernel,
        out_shape=tuple(shapes),
        in_specs=specs,
        out_specs=(HBM,) + (VMEM,) * (len(shapes) - 1),
        scratch_shapes=[
            pltpu.VMEM((count, TILES, CAP + 1, B, W), F32),
            pltpu.VMEM((count, ROWS, HALF), BF16),
            pltpu.SemaphoreType.DMA((count,)),
        ],
        input_output_aliases=aliases,
        compiler_params=params(50),
        cost_estimate=cost(4 * ROWS * HALF * W * count, count * 3 * MIB),
        name="grow" if right_side is not None else "widen",
    )(*operands)


def finish_kernel(mine_ref, other_ref, masks_ref, square_ref):
    scale = (NB / (KX * KX * B)) ** 0.5
    for i in range(BR):
        rows = pl.ds(i * B, B)
        keep = jnp.broadcast_to(masks_ref[1, i : i + 1, :], (B, W))
        value = (mine_ref[rows, :] + other_ref[rows, :]) * scale
        square_ref[rows, :] = jnp.where(keep > 0.0, value, 0.0).astype(BF16)


def finish(mine, other, masks):
    return pl.pallas_call(
        finish_kernel,
        out_shape=jax.ShapeDtypeStruct((ROWS, W), BF16),
        in_specs=[VMEM] * 3,
        out_specs=VMEM,
        cost_estimate=cost(400_000, MIB),
        name="finish",
    )(mine, other, masks)


STEP = 256


def cube_part(places, table, dense, pieces, acc=None, last=None):
    scale = (NB / (KX * KSQ * B)) ** 0.5
    count = len(pieces)

    def kernel(table_ref, *refs):
        refs = list(refs)
        total = refs.pop(0)[...] if acc is not None else None
        for p in range(count):
            left_ref, piece_ref = refs.pop(0), refs.pop(0)
            for core in range(2):
                term = jnp.dot(
                    left_ref[0, core],
                    piece_ref[pl.ds(core * HALF, HALF), :],
                    preferred_element_type=F32,
                )
                total = term if total is None else total + term
        out_ref = refs[-1]
        if last is None:
            out_ref[...] = total
            return
        tile_ref, masks_ref = refs[0], refs[1]
        for k in range(STEP // B):
            rows = pl.ds(k * B, B)
            keep_x = jnp.broadcast_to(masks_ref[0, k : k + 1, :], (B, W))
            keep_out = jnp.broadcast_to(masks_ref[2, k : k + 1, :], (B, W))
            sparse = jnp.where(keep_x > 0.0, tile_ref[rows, :].astype(F32), 0.0)
            cube = total[k * B : (k + 1) * B, :] * scale
            result = 1.5 * sparse - 0.5 * cube
            out_ref[rows, :] = jnp.where(keep_out > 0.0, result, 0.0).astype(BF16)

    operands, specs = [], []
    rows_spec = pl.BlockSpec((STEP, W), lambda i, table_ref: (i, 0))
    if acc is not None:
        operands.append(acc)
        specs.append(rows_spec)
    for p in range(count):
        operands += [dense, pieces[p]]
        if last is None:
            place = lambda i, table_ref, p=p: (table_ref[places[p]], 0, i, 0)
        else:
            place = lambda i, table_ref: (0, 0, i, 0)
        specs.append(pl.BlockSpec((1, 2, STEP, HALF), place))
        specs.append(pl.BlockSpec((ROWS, W), lambda i, table_ref: (0, 0)))
    if last is not None:
        tile, masks = last
        operands += [tile, masks]
        specs += [rows_spec, pl.BlockSpec((3, STEP // B, W), lambda i, table_ref: (0, i, 0))]
    return pl.pallas_call(
        kernel,
        out_shape=jax.ShapeDtypeStruct((ROWS, W), F32 if last is None else BF16),
        grid_spec=pltpu.PrefetchScalarGridSpec(
            num_scalar_prefetch=1,
            grid=(ROWS // STEP,),
            in_specs=specs,
            out_specs=rows_spec,
        ),
        compiler_params=params(50 if last is None else 16),
        cost_estimate=cost(2 * ROWS * ROWS * W * count, count * 3 * MIB + MIB),
        name="cube_last" if last is not None else "cube_part",
    )(table, *operands)


def local(matrix, list_x, list_sq, list_out):
    layers = lax.axis_size("layer")
    col = lax.axis_index("col").astype(jnp.int32)
    row = lax.axis_index("row").astype(jnp.int32)
    layer = lax.axis_index("layer").astype(jnp.int32)
    y, core = col // 2, col % 2
    sign = 1 - 2 * core
    base = jnp.reshape((col * layers + layer) * (W // B), (1,))

    def group(at, distance):
        return jnp.bitwise_and(at + sign * distance, GROUPS - 1)

    table = [jnp.bitwise_and(layer + d, TILES - 1) for d in (0, -1, 1, 2)]
    for turn, own in ((-1, core), (1, 1 - core)):
        for d, which in ((0, own), (1, own), (1, 1 - own), (2, own), (2, 1 - own), (3, own), (3, 1 - own), (4, own)):
            table += [group(y, turn * d), which]
    table += [group(row, d) for d in (0, -1, 1, -2, 2, -3, 3, 4)]
    table = jnp.stack(table)
    mine_at, other_at, z_at = 4, 20, 36

    cols = 2 * GROUPS
    swap = [(c, c ^ 1) for c in range(cols)]
    turn_y = [(c, (c + (2 if c % 2 == 0 else -2)) % cols) for c in range(cols)]
    turn_z = [
        (r * cols + c, (r + (1 if c % 2 == 0 else -1)) % GROUPS * cols + c)
        for r in range(GROUPS)
        for c in range(cols)
    ]

    def along_x(piece, step):
        return lax.ppermute(piece, "layer", [(x, (x + step) % layers) for x in range(layers)])

    def along_y(piece):
        return lax.ppermute(piece, "col", turn_y)

    def along_z(piece):
        return lax.ppermute(piece, ("row", "col"), turn_z)

    def across(piece):
        return lax.ppermute(piece, "col", swap)

    def after(piece, *done):
        return lax.optimization_barrier((piece, *done))[0]

    pay, left, slots = pack(base, list_x, matrix)
    pays = lax.all_gather(pay, "row", axis=0, tiled=False)
    a0 = order(table, [left, along_x(left, 1), along_x(left, -1), along_x(left, 2)])
    b0 = across(a0)

    def places(start, *which):
        return [start + 2 * k for k in which]

    a1, b1 = along_y(a0), along_y(b0)
    a2, b2 = along_y(a1), along_y(b1)
    a3, b3 = along_y(a2), along_y(b2)
    pays = after(pays, a2)
    right_side, masks = right(table, base, (list_x, list_sq, list_out), pays, across(pays))
    dense, acc = grow([a0, a1, b1], places(mine_at, 0, 1, 2), table, slots, None, right_side)
    a4 = along_y(after(a3, acc))
    dense, acc = grow([a2, b2], places(mine_at, 3, 4), table, slots, dense, right_side, acc)
    dense, acc = grow([a3, b3], places(mine_at, 5, 6), table, slots, dense, right_side, acc)
    dense, mine, other = grow(
        [a4], places(mine_at, 7), table, slots, dense, right_side, acc, split=True
    )
    square = finish(mine, across(other), masks)

    theirs = jnp.concatenate([a1, b1, a2, b2, a3, b3, a4], axis=0)
    theirs = across(after(theirs, other))
    c0, d0 = square, across(square)
    c1, d1 = along_z(c0), along_z(d0)
    (dense,) = grow(
        [b0] + [theirs[k * TILES : (k + 1) * TILES] for k in range(7)],
        places(other_at, *range(8)),
        table,
        slots,
        dense,
    )
    acc = cube_part([z_at], table, dense, [c0])
    c1, d1 = lax.optimization_barrier((c1, d1, acc))[:2]
    c2, d2 = along_z(c1), along_z(d1)
    acc = cube_part([z_at + 1, z_at + 2], table, dense, [c1, across(d1)], acc)
    c2, d2 = lax.optimization_barrier((c2, d2, acc))[:2]
    c3, d3 = along_z(c2), along_z(d2)
    acc = cube_part([z_at + 3, z_at + 4], table, dense, [c2, across(d2)], acc)
    c4 = along_z(after(c3, acc))
    acc = cube_part([z_at + 5, z_at + 6], table, dense, [c3, across(d3)], acc)
    far = lax.dynamic_slice_in_dim(dense, group(row, 4), 1, 0)
    return cube_part([0], table, far, [c4], acc, (matrix, masks))


def solution(mesh):
    placed = (P("row", ("col", "layer")), P("row", None), P("row", None), P("row", None))
    return jax.shard_map(
        local, mesh=mesh, in_specs=placed, out_specs=P("row", ("col", "layer")), check_vma=False
    )
```

time: 267 us -> 220 us (0.82)
  the two profiles are of different devices: /device:TPU:1 before, /device:TPU:16 now
where the time goes in v2:
time: 220 us; the launch traced here: 219 us
  Pallas kernels  78.9 us (36%)
  starting transfers between devices  77.9 us (35%)
  waiting for transfers between devices  33.9 us (15%)
  local copies, waits for them, and re-layouts  14 us (6%)
  between operations  14 us (6%)
    pallas_call x5, Pallas kernels, grow(): pl.pallas_call(kernel, out_shape=tuple(shapes), in_specs=specs, out_specs...  40.5 us
    ppermute x7, starting transfers between devices, along_z(): return lax.ppermute(piece, ('row', 'col'), turn_z)  26.7 us
    ppermute x7, waiting for transfers between devices, along_y(): return lax.ppermute(piece, 'col', turn_y)  22.9 us
    ppermute x7, starting transfers between devices, along_y(): return lax.ppermute(piece, 'col', turn_y)  22.7 us
    pallas_call x5, Pallas kernels, cube_part(): pl.pallas_call(kernel, out_shape=jax.ShapeDtypeStruct((ROWS, W), F32 if l...  19.6 us
    ppermute x8, starting transfers between devices, across(): return lax.ppermute(piece, 'col', swap)  17.8 us
    pallas_call x1, Pallas kernels, order(): pl.pallas_call(order_kernel, out_shape=jax.ShapeDtypeStruct((TILES, CAP,...  11.7 us
    ppermute x3, starting transfers between devices, along_x(): lax.ppermute(piece, 'layer', [(x, (x + step) % layers) for x in range(lay...  10.8 us
  transfers between devices with their start and end apart: 26, of which 9 were waited for; matrix products, arithmetic and copies ran while one was open for 3% of the time, Pallas kernels for 32%

profile of v2, /device:TPU:16, one launch (start us, length us, event | category | flops | bytes accessed | tf_op | source)
XLA Modules:
  0.0 218.7 jit_solution(11719113130297165208)
XLA Ops:
  13.0 3.7 %collective-permute-start.1 = (bf16[10,32,128]{2,1,0:T(8,128)(2,1)S(1)}, bf16[10,32,128]{2,1,0:T(8,128)(2,1)S(1)}, u32[]{:S(2)}, u32[]{:S(2)}) collective-permute-start(bf16[10,32,128]{2,1,0:T(8,128)(2,1)S(1)} %get-tuple-element.28.refs_0_), channel_id=1, source_target_pairs={{0,3},{1,0},{2,1},{3,2},{4,7},{5,4},{6,5},{7,6},{8,11},{9,8},{10,9... | collective-permute-start | bytes 245768 | tf_op jit(solution)/shard_map/ppermute | solution.py:374
  16.7 3.7 %collective-permute-start.2 = (bf16[10,32,128]{2,1,0:T(8,128)(2,1)S(1)}, bf16[10,32,128]{2,1,0:T(8,128)(2,1)S(1)}, u32[]{:S(2)}, u32[]{:S(2)}) collective-permute-start(bf16[10,32,128]{2,1,0:T(8,128)(2,1)S(1)} %get-tuple-element.28.refs_0_), channel_id=1, source_target_pairs={{0,2},{1,3},{2,0},{3,1},{4,6},{5,7},{6,4},{7,5},{8,10},{9,11},{10,... | collective-permute-start | bytes 245768 | tf_op jit(solution)/shard_map/ppermute | solution.py:374
  25.2 11.7 %order.1.refs_0_ = bf16[4,10,32,128]{3,2,1,0:T(8,128)(2,1)} custom-call(s32[44]{0:T(128)} %stack.116.table_ref, bf16[10,32,128]{2,1,0:T(8,128)(2,1)} %copy-done.10, bf16[10,32,128]{2,1,0:T(8,128)(2,1)} %copy-done.16, bf16[10,32,128]{2,1,0:T(8,128)(2,1)} %copy-done.17, bf16[10,32,128]{2,1,0:T(8,128)(2,1)} %copy-done.18), custom_call_target="tpu_custom_call" | custom-call | bytes 700000 | tf_op jit(solution)/shard_map/order/pallas_call | solution.py:117
  36.9 3.5 %collective-permute-start.4 = (bf16[4,10,32,128]{3,2,1,0:T(8,128)(2,1)}, bf16[4,10,32,128]{3,2,1,0:T(8,128)(2,1)S(1)}, u32[]{:S(2)}, u32[]{:S(2)}) collective-permute-start(bf16[4,10,32,128]{3,2,1,0:T(8,128)(2,1)} %order.1.refs_0_), channel_id=1, source_target_pairs={{0,8},{4,60},{8,16},{12,4},{16,24},{20,12},{24,32},{28,20},{32,40}... | collective-permute-start | bytes 983048 | tf_op jit(solution)/shard_map/ppermute | solution.py:377
  40.4 5.7 %collective-permute-done.4.refs_1_ = bf16[4,10,32,128]{3,2,1,0:T(8,128)(2,1)S(1)} collective-permute-done((bf16[4,10,32,128]{3,2,1,0:T(8,128)(2,1)}, bf16[4,10,32,128]{3,2,1,0:T(8,128)(2,1)S(1)}, u32[]{:S(2)}, u32[]{:S(2)}) %collective-permute-start.4) | collective-permute-done | bytes 327712 | tf_op jit(solution)/shard_map/ppermute | solution.py:377
  46.1 3.9 %collective-permute-start.6 = (bf16[4,10,32,128]{3,2,1,0:T(8,128)(2,1)S(1)}, bf16[4,10,32,128]{3,2,1,0:T(8,128)(2,1)S(1)}, u32[]{:S(2)}, u32[]{:S(2)}) collective-permute-start(bf16[4,10,32,128]{3,2,1,0:T(8,128)(2,1)S(1)} %collective-permute-done.4.refs_1_), channel_id=1, source_target_pairs={{0,8},{4,60},{8,16},{12,4},{16,24},{20,12},{24,32},{28,20},{32,40}... | collective-permute-start | bytes 983048 | tf_op jit(solution)/shard_map/ppermute | solution.py:377
  51.9 7.1 %collective-permute-done.6.refs_0_ = bf16[4,10,32,128]{3,2,1,0:T(8,128)(2,1)S(1)} collective-permute-done((bf16[4,10,32,128]{3,2,1,0:T(8,128)(2,1)S(1)}, bf16[4,10,32,128]{3,2,1,0:T(8,128)(2,1)S(1)}, u32[]{:S(2)}, u32[]{:S(2)}) %collective-permute-start.6) | collective-permute-done | bytes 327712 | tf_op jit(solution)/shard_map/ppermute | solution.py:377
  63.0 8.3 %collective-permute-done.5.refs_2_ = bf16[4,10,32,128]{3,2,1,0:T(8,128)(2,1)S(1)} collective-permute-done((bf16[4,10,32,128]{3,2,1,0:T(8,128)(2,1)S(1)}, bf16[4,10,32,128]{3,2,1,0:T(8,128)(2,1)S(1)}, u32[]{:S(2)}, u32[]{:S(2)}) %collective-permute-start.5) | collective-permute-done | bytes 327712 | tf_op jit(solution)/shard_map/ppermute | solution.py:377
  73.9 4.8 %collective-permute-start.8 = (bf16[4,10,32,128]{3,2,1,0:T(8,128)(2,1)S(1)}, bf16[4,10,32,128]{3,2,1,0:T(8,128)(2,1)S(1)}, u32[]{:S(2)}, u32[]{:S(2)}) collective-permute-start(bf16[4,10,32,128]{3,2,1,0:T(8,128)(2,1)S(1)} %collective-permute-done.6.refs_0_), channel_id=1, source_target_pairs={{0,8},{4,60},{8,16},{12,4},{16,24},{20,12},{24,32},{28,20},{32,40}... | collective-permute-start | bytes 983048 | tf_op jit(solution)/shard_map/ppermute | solution.py:377
  84.9 3.7 %right.1 = (bf16[8,512,256]{2,1,0:T(8,128)(2,1)S(1)}, f32[3,32,128]{2,1,0:T(8,128)S(1)}) custom-call(s32[44]{0:T(128)S(1)} %copy-done.9, s32[1]{0:T(128)} %bitcast.23.base_ref, s32[32,40]{1,0:T(8,128)S(1)} %copy-done.12, s32[32,60]{1,0:T(8,128)S(1)} %copy-done.13, s32[32,40]{1,0:T(8,128)S(1)} %copy-done.14, bf16[8,576,128]{2,1,0:T(8,128)(2,1)S(1)} %bitcast.26, ...), custom_call_target="tpu_custom_call" | custom-call | flops 40000000 | bytes 4194304 | tf_op jit(solution)/shard_map/right/pallas_call | solution.py:154
  90.6 8.6 %grow.4 = (bf16[8,2,1024,512]{3,2,1,0:T(8,128)(2,1)}, f32[1024,256]{1,0:T(8,128)S(1)}) custom-call(s32[44]{0:T(128)S(1)} %copy-done.9, s32[32,256]{1,0:T(8,128)S(1)} %get-tuple-element.27.slots_ref, bf16[4,10,32,128]{3,2,1,0:T(8,128)(2,1)S(1)} %copy-done.1, bf16[4,10,32,128]{3,2,1,0:T(8,128)(2,1)S(1)} %collective-permute-done.4.refs_1_, ...), custom_call_target="tpu_custom_call" | custom-call | flops 805306368 | bytes 9437184 | tf_op jit(solution)/shard_map/grow/pallas_call | solution.py:242
  99.2 4.7 %collective-permute-start.11 = (bf16[4,10,32,128]{3,2,1,0:T(8,128)(2,1)S(1)}, bf16[4,10,32,128]{3,2,1,0:T(8,128)(2,1)S(1)}, u32[]{:S(2)}, u32[]{:S(2)}) collective-permute-start(bf16[4,10,32,128]{3,2,1,0:T(8,128)(2,1)S(1)} %collective-permute-done.8.refs_0_), channel_id=1, source_target_pairs={{0,8},{4,60},{8,16},{12,4},{16,24},{20,12},{24,32},{28,20},{32,40}... | collective-permute-start | bytes 983048 | tf_op jit(solution)/shard_map/ppermute | solution.py:377
  105.5 6.0 %grow.5 = (bf16[8,2,1024,512]{3,2,1,0:T(8,128)(2,1)}, f32[1024,256]{1,0:T(8,128)S(1)}) custom-call(s32[44]{0:T(128)S(1)} %copy-done.9, s32[32,256]{1,0:T(8,128)S(1)} %get-tuple-element.27.slots_ref, bf16[4,10,32,128]{3,2,1,0:T(8,128)(2,1)S(1)} %collective-permute-done.6.refs_0_, ...), custom_call_target="tpu_custom_call", output_to_operand_aliasing={{0}: (6, {})} | custom-call | flops 536870912 | bytes 6291456 | tf_op jit(solution)/shard_map/grow/pallas_call | solution.py:242
  111.5 6.1 %grow.6 = (bf16[8,2,1024,512]{3,2,1,0:T(8,128)(2,1)}, f32[1024,256]{1,0:T(8,128)S(1)}) custom-call(s32[44]{0:T(128)S(1)} %copy-done.9, s32[32,256]{1,0:T(8,128)S(1)} %get-tuple-element.27.slots_ref, bf16[4,10,32,128]{3,2,1,0:T(8,128)(2,1)S(1)} %collective-permute-done.8.refs_0_, ...), custom_call_target="tpu_custom_call", output_to_operand_aliasing={{0}: (6, {})} | custom-call | flops 536870912 | bytes 6291456 | tf_op jit(solution)/shard_map/grow/pallas_call | solution.py:242
  118.4 4.2 %grow.7 = (bf16[8,2,1024,512]{3,2,1,0:T(8,128)(2,1)}, f32[1024,128]{1,0:T(8,128)S(1)}, f32[1024,128]{1,0:T(8,128)S(1)}) custom-call(s32[44]{0:T(128)S(1)} %copy-done.9, s32[32,256]{1,0:T(8,128)S(1)} %get-tuple-element.27.slots_ref, bf16[4,10,32,128]{3,2,1,0:T(8,128)(2,1)S(1)} %collective-permute-done.11.refs_0_, ...), custom_call_target="tpu_custom_call", output_to_operand_aliasing={{0}: (5, {})} | custom-call | flops 268435456 | bytes 3145728 | tf_op jit(solution)/shard_map/grow/pallas_call | solution.py:242
  135.3 4.3 %collective-permute-start.14 = (bf16[1024,128]{1,0:T(8,128)(2,1)}, bf16[1024,128]{1,0:T(8,128)(2,1)S(1)}, u32[]{:S(2)}, u32[]{:S(2)}) collective-permute-start(bf16[1024,128]{1,0:T(8,128)(2,1)} %finish.1.refs_1_), channel_id=1, source_target_pairs={{0,64},{4,452},{8,72},{12,460},{16,80},{20,468},{24,88},{28,476},{... | collective-permute-start | bytes 786440 | tf_op jit(solution)/shard_map/ppermute | solution.py:380
  139.6 8.6 %collective-permute-start.16 = (bf16[1024,128]{1,0:T(8,128)(2,1)S(1)}, bf16[1024,128]{1,0:T(8,128)(2,1)S(1)}, u32[]{:S(2)}, u32[]{:S(2)}) collective-permute-start(bf16[1024,128]{1,0:T(8,128)(2,1)S(1)} %collective-permute-done.15), channel_id=1, source_target_pairs={{0,64},{4,452},{8,72},{12,460},{16,80},{20,468},{24,88},{28,476},{... | collective-permute-start | bytes 786440 | tf_op jit(solution)/shard_map/ppermute | solution.py:380
  148.6 15.6 %widen.1.refs_0_.refs_1_.refs_3_ = bf16[8,2,1024,512]{3,2,1,0:T(8,128)(2,1)} custom-call(s32[44]{0:T(128)S(1)} %copy-done.9, s32[32,256]{1,0:T(8,128)S(1)} %get-tuple-element.27.slots_ref, bf16[4,10,32,128]{3,2,1,0:T(8,128)(2,1)S(1)} %collective-permute-done.3.refs_0_, ...), custom_call_target="tpu_custom_call", output_to_operand_aliasing={{}: (10, {})} | custom-call | flops 2147483648 | bytes 25165824 | tf_op jit(solution)/shard_map/widen/pallas_call | solution.py:242
  164.2 3.6 %cube_part.4.refs_0_ = f32[1024,128]{1,0:T(8,128)S(1)} custom-call(s32[44]{0:T(128)S(1)} %copy-done.9, bf16[8,2,1024,512]{3,2,1,0:T(8,128)(2,1)} %widen.1.refs_0_.refs_1_.refs_3_, bf16[1024,128]{1,0:T(8,128)(2,1)S(1)} %copy-done.3), custom_call_target="tpu_custom_call" | custom-call | flops 268435456 | bytes 4194304 | tf_op jit(solution)/shard_map/cube_part/pallas_call | solution.py:329
  167.8 3.7 %collective-permute-start.17 = (bf16[1024,128]{1,0:T(8,128)(2,1)S(1)}, bf16[1024,128]{1,0:T(8,128)(2,1)S(1)}, u32[]{:S(2)}, u32[]{:S(2)}) collective-permute-start(bf16[1024,128]{1,0:T(8,128)(2,1)S(1)} %collective-permute-done.16), channel_id=1, source_target_pairs={{0,4},{4,0},{8,12},{12,8},{16,20},{20,16},{24,28},{28,24},{32,36},... | collective-permute-start | bytes 786440 | tf_op jit(solution)/shard_map/ppermute | solution.py:383
  174.1 3.9 %collective-permute-start.19 = (bf16[1024,128]{1,0:T(8,128)(2,1)S(1)}, bf16[1024,128]{1,0:T(8,128)(2,1)S(1)}, u32[]{:S(2)}, u32[]{:S(2)}) collective-permute-start(bf16[1024,128]{1,0:T(8,128)(2,1)S(1)} %collective-permute-done.16), channel_id=1, source_target_pairs={{0,64},{4,452},{8,72},{12,460},{16,80},{20,468},{24,88},{28,476},{... | collective-permute-start | bytes 786440 | tf_op jit(solution)/shard_map/ppermute | solution.py:380
  178.0 4.4 %cube_part.5.refs_0_ = f32[1024,128]{1,0:T(8,128)S(1)} custom-call(s32[44]{0:T(128)S(1)} %copy-done.9, f32[1024,128]{1,0:T(8,128)S(1)} %cube_part.4.refs_0_, bf16[8,2,1024,512]{3,2,1,0:T(8,128)(2,1)} %widen.1.refs_0_.refs_1_.refs_3_, bf16[1024,128]{1,0:T(8,128)(2,1)S(1)} %collective-permute-done.14.refs_2_, ...), custom_call_target="tpu_custom_call" | custom-call | flops 536870912 | bytes 7340032 | tf_op jit(solution)/shard_map/cube_part/pallas_call | solution.py:329
  195.1 4.4 %cube_part.6.refs_0_ = f32[1024,128]{1,0:T(8,128)S(1)} custom-call(s32[44]{0:T(128)S(1)} %copy-done.9, f32[1024,128]{1,0:T(8,128)S(1)} %cube_part.5.refs_0_, bf16[8,2,1024,512]{3,2,1,0:T(8,128)(2,1)} %widen.1.refs_0_.refs_1_.refs_3_, bf16[1024,128]{1,0:T(8,128)(2,1)S(1)} %collective-permute-done.18.refs_2_, ...), custom_call_target="tpu_custom_call" | custom-call | flops 536870912 | bytes 7340032 | tf_op jit(solution)/shard_map/cube_part/pallas_call | solution.py:329
  203.2 4.4 %cube_part.7.refs_0_ = f32[1024,128]{1,0:T(8,128)S(1)} custom-call(s32[44]{0:T(128)S(1)} %copy-done.9, f32[1024,128]{1,0:T(8,128)S(1)} %cube_part.6.refs_0_, bf16[8,2,1024,512]{3,2,1,0:T(8,128)(2,1)} %widen.1.refs_0_.refs_1_.refs_3_, bf16[1024,128]{1,0:T(8,128)(2,1)S(1)} %collective-permute-done.21.refs_2_, ...), custom_call_target="tpu_custom_call" | custom-call | flops 536870912 | bytes 7340032 | tf_op jit(solution)/shard_map/cube_part/pallas_call | solution.py:329
  (91 shorter events, 66.2 us)
Async XLA Ops:
  6.5 52.5 %all-gather.3.cloned.1.call-start = ((), (), s32[]{:S(2)}) async-start(), calls=%async_computation | async-start | bytes 1327104 | tf_op jit(solution)/shard_map/all_gather | solution.py:389
  9.6 11.6 %collective-permute-start = (bf16[10,32,128]{2,1,0:T(8,128)(2,1)S(1)}, bf16[10,32,128]{2,1,0:T(8,128)(2,1)S(1)}, u32[]{:S(2)}, u32[]{:S(2)}) collective-permute-start(bf16[10,32,128]{2,1,0:T(8,128)(2,1)S(1)} %get-tuple-element.28.refs_0_), channel_id=1, source_target_pairs={{0,1},{1,2},{2,3},{3,0},{4,5},{5,6},{6,7},{7,4},{8,9},{9,10},{10,1... | collective-permute-start | bytes 245768 | tf_op jit(solution)/shard_map/ppermute | solution.py:374
  13.0 8.2 %collective-permute-start.1 = (bf16[10,32,128]{2,1,0:T(8,128)(2,1)S(1)}, bf16[10,32,128]{2,1,0:T(8,128)(2,1)S(1)}, u32[]{:S(2)}, u32[]{:S(2)}) collective-permute-start(bf16[10,32,128]{2,1,0:T(8,128)(2,1)S(1)} %get-tuple-element.28.refs_0_), channel_id=1, source_target_pairs={{0,3},{1,0},{2,1},{3,2},{4,7},{5,4},{6,5},{7,6},{8,11},{9,8},{10,9... | collective-permute-start | bytes 245768 | tf_op jit(solution)/shard_map/ppermute | solution.py:374
  16.7 7.8 %collective-permute-start.2 = (bf16[10,32,128]{2,1,0:T(8,128)(2,1)S(1)}, bf16[10,32,128]{2,1,0:T(8,128)(2,1)S(1)}, u32[]{:S(2)}, u32[]{:S(2)}) collective-permute-start(bf16[10,32,128]{2,1,0:T(8,128)(2,1)S(1)} %get-tuple-element.28.refs_0_), channel_id=1, source_target_pairs={{0,2},{1,3},{2,0},{3,1},{4,6},{5,7},{6,4},{7,5},{8,10},{9,11},{10,... | collective-permute-start | bytes 245768 | tf_op jit(solution)/shard_map/ppermute | solution.py:374
  36.9 9.2 %collective-permute-start.4 = (bf16[4,10,32,128]{3,2,1,0:T(8,128)(2,1)}, bf16[4,10,32,128]{3,2,1,0:T(8,128)(2,1)S(1)}, u32[]{:S(2)}, u32[]{:S(2)}) collective-permute-start(bf16[4,10,32,128]{3,2,1,0:T(8,128)(2,1)} %order.1.refs_0_), channel_id=1, source_target_pairs={{0,8},{4,60},{8,16},{12,4},{16,24},{20,12},{24,32},{28,20},{32,40}... | collective-permute-start | bytes 983048 | tf_op jit(solution)/shard_map/ppermute | solution.py:377
  46.1 12.9 %collective-permute-start.6 = (bf16[4,10,32,128]{3,2,1,0:T(8,128)(2,1)S(1)}, bf16[4,10,32,128]{3,2,1,0:T(8,128)(2,1)S(1)}, u32[]{:S(2)}, u32[]{:S(2)}) collective-permute-start(bf16[4,10,32,128]{3,2,1,0:T(8,128)(2,1)S(1)} %collective-permute-done.4.refs_1_), channel_id=1, source_target_pairs={{0,8},{4,60},{8,16},{12,4},{16,24},{20,12},{24,32},{28,20},{32,40}... | collective-permute-start | bytes 983048 | tf_op jit(solution)/shard_map/ppermute | solution.py:377
  50.0 11.1 %collective-permute-start.3 = (bf16[4,10,32,128]{3,2,1,0:T(8,128)(2,1)}, bf16[4,10,32,128]{3,2,1,0:T(8,128)(2,1)S(1)}, u32[]{:S(2)}, u32[]{:S(2)}) collective-permute-start(bf16[4,10,32,128]{3,2,1,0:T(8,128)(2,1)} %order.1.refs_0_), channel_id=1, source_target_pairs={{0,4},{4,0},{8,12},{12,8},{16,20},{20,16},{24,28},{28,24},{32,36},... | collective-permute-start | bytes 983048 | tf_op jit(solution)/shard_map/ppermute | solution.py:383
  59.0 25.8 %collective-permute-start.10 = (bf16[8,576,128]{2,1,0:T(8,128)(2,1)}, bf16[8,576,128]{2,1,0:T(8,128)(2,1)S(1)}, u32[]{:S(2)}, u32[]{:S(2)}) collective-permute-start(bf16[8,576,128]{2,1,0:T(8,128)(2,1)} %bitcast.25), channel_id=1, source_target_pairs={{0,4},{4,0},{8,12},{12,8},{16,20},{20,16},{24,28},{28,24},{32,36},... | collective-permute-start | bytes 3538952 | tf_op jit(solution)/shard_map/ppermute | solution.py:383
  61.1 10.2 %collective-permute-start.5 = (bf16[4,10,32,128]{3,2,1,0:T(8,128)(2,1)S(1)}, bf16[4,10,32,128]{3,2,1,0:T(8,128)(2,1)S(1)}, u32[]{:S(2)}, u32[]{:S(2)}) collective-permute-start(bf16[4,10,32,128]{3,2,1,0:T(8,128)(2,1)S(1)} %collective-permute-done.3.refs_0_), channel_id=1, source_target_pairs={{0,8},{4,60},{8,16},{12,4},{16,24},{20,12},{24,32},{28,20},{32,40}... | collective-permute-start | bytes 983048 | tf_op jit(solution)/shard_map/ppermute | solution.py:377
  71.2 10.2 %collective-permute-start.7 = (bf16[4,10,32,128]{3,2,1,0:T(8,128)(2,1)S(1)}, bf16[4,10,32,128]{3,2,1,0:T(8,128)(2,1)S(1)}, u32[]{:S(2)}, u32[]{:S(2)}) collective-permute-start(bf16[4,10,32,128]{3,2,1,0:T(8,128)(2,1)S(1)} %collective-permute-done.5.refs_2_), channel_id=1, source_target_pairs={{0,8},{4,60},{8,16},{12,4},{16,24},{20,12},{24,32},{28,20},{32,40}... | collective-permute-start | bytes 983048 | tf_op jit(solution)/shard_map/ppermute | solution.py:377
  73.9 25.3 %collective-permute-start.8 = (bf16[4,10,32,128]{3,2,1,0:T(8,128)(2,1)S(1)}, bf16[4,10,32,128]{3,2,1,0:T(8,128)(2,1)S(1)}, u32[]{:S(2)}, u32[]{:S(2)}) collective-permute-start(bf16[4,10,32,128]{3,2,1,0:T(8,128)(2,1)S(1)} %collective-permute-done.6.refs_0_), channel_id=1, source_target_pairs={{0,8},{4,60},{8,16},{12,4},{16,24},{20,12},{24,32},{28,20},{32,40}... | collective-permute-start | bytes 983048 | tf_op jit(solution)/shard_map/ppermute | solution.py:377
  81.4 23.3 %collective-permute-start.9 = (bf16[4,10,32,128]{3,2,1,0:T(8,128)(2,1)S(1)}, bf16[4,10,32,128]{3,2,1,0:T(8,128)(2,1)S(1)}, u32[]{:S(2)}, u32[]{:S(2)}) collective-permute-start(bf16[4,10,32,128]{3,2,1,0:T(8,128)(2,1)S(1)} %collective-permute-done.7.refs_1_), channel_id=1, source_target_pairs={{0,8},{4,60},{8,16},{12,4},{16,24},{20,12},{24,32},{28,20},{32,40}... | collective-permute-start | bytes 983048 | tf_op jit(solution)/shard_map/ppermute | solution.py:377
  99.2 18.3 %collective-permute-start.11 = (bf16[4,10,32,128]{3,2,1,0:T(8,128)(2,1)S(1)}, bf16[4,10,32,128]{3,2,1,0:T(8,128)(2,1)S(1)}, u32[]{:S(2)}, u32[]{:S(2)}) collective-permute-start(bf16[4,10,32,128]{3,2,1,0:T(8,128)(2,1)S(1)} %collective-permute-done.8.refs_0_), channel_id=1, source_target_pairs={{0,8},{4,60},{8,16},{12,4},{16,24},{20,12},{24,32},{28,20},{32,40}... | collective-permute-start | bytes 983048 | tf_op jit(solution)/shard_map/ppermute | solution.py:377
  123.4 24.8 %collective-permute-start.12 = (bf16[28,10,32,128]{3,2,1,0:T(8,128)(2,1)}, bf16[28,10,32,128]{3,2,1,0:T(8,128)(2,1)S(1)}, u32[]{:S(2)}, u32[]{:S(2)}) collective-permute-start(bf16[28,10,32,128]{3,2,1,0:T(8,128)(2,1)} %constant_dynamic-update-slice_fusion), channel_id=1, source_target_pairs={{0,4},{4,0},{8,12},{12,8},{16,20},{20,16},{24,28},{28,24},{32,36},... | collective-permute-start | bytes 6881288 | tf_op jit(solution)/shard_map/ppermute | solution.py:383
  135.3 32.5 %collective-permute-start.14 = (bf16[1024,128]{1,0:T(8,128)(2,1)}, bf16[1024,128]{1,0:T(8,128)(2,1)S(1)}, u32[]{:S(2)}, u32[]{:S(2)}) collective-permute-start(bf16[1024,128]{1,0:T(8,128)(2,1)} %finish.1.refs_1_), channel_id=1, source_target_pairs={{0,64},{4,452},{8,72},{12,460},{16,80},{20,468},{24,88},{28,476},{... | collective-permute-start | bytes 786440 | tf_op jit(solution)/shard_map/ppermute | solution.py:380
  139.6 28.2 %collective-permute-start.16 = (bf16[1024,128]{1,0:T(8,128)(2,1)S(1)}, bf16[1024,128]{1,0:T(8,128)(2,1)S(1)}, u32[]{:S(2)}, u32[]{:S(2)}) collective-permute-start(bf16[1024,128]{1,0:T(8,128)(2,1)S(1)} %collective-permute-done.15), channel_id=1, source_target_pairs={{0,64},{4,452},{8,72},{12,460},{16,80},{20,468},{24,88},{28,476},{... | collective-permute-start | bytes 786440 | tf_op jit(solution)/shard_map/ppermute | solution.py:380
  167.8 10.3 %collective-permute-start.17 = (bf16[1024,128]{1,0:T(8,128)(2,1)S(1)}, bf16[1024,128]{1,0:T(8,128)(2,1)S(1)}, u32[]{:S(2)}, u32[]{:S(2)}) collective-permute-start(bf16[1024,128]{1,0:T(8,128)(2,1)S(1)} %collective-permute-done.16), channel_id=1, source_target_pairs={{0,4},{4,0},{8,12},{12,8},{16,20},{20,16},{24,28},{28,24},{32,36},... | collective-permute-start | bytes 786440 | tf_op jit(solution)/shard_map/ppermute | solution.py:383
  171.4 11.0 %collective-permute-start.18 = (bf16[1024,128]{1,0:T(8,128)(2,1)S(1)}, bf16[1024,128]{1,0:T(8,128)(2,1)S(1)}, u32[]{:S(2)}, u32[]{:S(2)}) collective-permute-start(bf16[1024,128]{1,0:T(8,128)(2,1)S(1)} %collective-permute-done.14.refs_2_), channel_id=1, source_target_pairs={{0,64},{4,452},{8,72},{12,460},{16,80},{20,468},{24,88},{28,476},{... | collective-permute-start | bytes 786440 | tf_op jit(solution)/shard_map/ppermute | solution.py:380
  174.1 9.6 %collective-permute-start.19 = (bf16[1024,128]{1,0:T(8,128)(2,1)S(1)}, bf16[1024,128]{1,0:T(8,128)(2,1)S(1)}, u32[]{:S(2)}, u32[]{:S(2)}) collective-permute-start(bf16[1024,128]{1,0:T(8,128)(2,1)S(1)} %collective-permute-done.16), channel_id=1, source_target_pairs={{0,64},{4,452},{8,72},{12,460},{16,80},{20,468},{24,88},{28,476},{... | collective-permute-start | bytes 786440 | tf_op jit(solution)/shard_map/ppermute | solution.py:380
  183.7 9.5 %collective-permute-start.22 = (bf16[1024,128]{1,0:T(8,128)(2,1)S(1)}, bf16[1024,128]{1,0:T(8,128)(2,1)S(1)}, u32[]{:S(2)}, u32[]{:S(2)}) collective-permute-start(bf16[1024,128]{1,0:T(8,128)(2,1)S(1)} %collective-permute-done.19), channel_id=1, source_target_pairs={{0,64},{4,452},{8,72},{12,460},{16,80},{20,468},{24,88},{28,476},{... | collective-permute-start | bytes 786440 | tf_op jit(solution)/shard_map/ppermute | solution.py:380
  186.3 8.8 %collective-permute-start.20 = (bf16[1024,128]{1,0:T(8,128)(2,1)S(1)}, bf16[1024,128]{1,0:T(8,128)(2,1)S(1)}, u32[]{:S(2)}, u32[]{:S(2)}) collective-permute-start(bf16[1024,128]{1,0:T(8,128)(2,1)S(1)} %collective-permute-done.19), channel_id=1, source_target_pairs={{0,4},{4,0},{8,12},{12,8},{16,20},{20,16},{24,28},{28,24},{32,36},... | collective-permute-start | bytes 786440 | tf_op jit(solution)/shard_map/ppermute | solution.py:383
  188.2 11.3 %collective-permute-start.21 = (bf16[1024,128]{1,0:T(8,128)(2,1)S(1)}, bf16[1024,128]{1,0:T(8,128)(2,1)S(1)}, u32[]{:S(2)}, u32[]{:S(2)}) collective-permute-start(bf16[1024,128]{1,0:T(8,128)(2,1)S(1)} %collective-permute-done.18.refs_2_), channel_id=1, source_target_pairs={{0,64},{4,452},{8,72},{12,460},{16,80},{20,468},{24,88},{28,476},{... | collective-permute-start | bytes 786440 | tf_op jit(solution)/shard_map/ppermute | solution.py:380
  193.2 10.0 %collective-permute-start.23 = (bf16[1024,128]{1,0:T(8,128)(2,1)S(1)}, bf16[1024,128]{1,0:T(8,128)(2,1)S(1)}, u32[]{:S(2)}, u32[]{:S(2)}) collective-permute-start(bf16[1024,128]{1,0:T(8,128)(2,1)S(1)} %collective-permute-done.22), channel_id=1, source_target_pairs={{0,4},{4,0},{8,12},{12,8},{16,20},{20,16},{24,28},{28,24},{32,36},... | collective-permute-start | bytes 786440 | tf_op jit(solution)/shard_map/ppermute | solution.py:383
  199.5 9.5 %collective-permute-start.24 = (bf16[1024,128]{1,0:T(8,128)(2,1)S(1)}, bf16[1024,128]{1,0:T(8,128)(2,1)S(1)}, u32[]{:S(2)}, u32[]{:S(2)}) collective-permute-start(bf16[1024,128]{1,0:T(8,128)(2,1)S(1)} %collective-permute-done.21.refs_2_), channel_id=1, source_target_pairs={{0,64},{4,452},{8,72},{12,460},{16,80},{20,468},{24,88},{28,476},{... | collective-permute-start | bytes 786440 | tf_op jit(solution)/shard_map/ppermute | solution.py:380
  (21 other events, 403.9 us)
Sparse Core Ops, SparseCore 0:
  9.7 46.8 all-gather.2

commit v3 on v2

v3 whole, which is shorter than its diff:
```python
import jax
import jax.numpy as jnp
from jax import lax
from jax.experimental import pallas as pl
from jax.experimental.pallas import tpu as pltpu
from jax.sharding import PartitionSpec as P

B = 32
NB = 256
KX = 40
KSQ = 60
CAP = 10
ROWS = 1024
W = 128
BR = ROWS // B
GROUPS = 8
TILES = 4
HALF = TILES * W
PAY = 576
F32 = jnp.float32
BF16 = jnp.bfloat16
MIB = 1 << 20
SMEM = pl.BlockSpec(memory_space=pltpu.SMEM)
VMEM = pl.BlockSpec(memory_space=pltpu.VMEM)
HBM = pl.BlockSpec(memory_space=pl.ANY)


def params(limit):
    return pltpu.CompilerParams(vmem_limit_bytes=limit * MIB)


def cost(flops, size):
    return pl.CostEstimate(flops=flops, bytes_accessed=size, transcendentals=0)


def copies_in(pairs, sems):
    copies = [pltpu.make_async_copy(a, b, sems.at[k]) for k, (a, b) in enumerate(pairs)]
    for copy in copies:
        copy.start()
    for copy in copies:
        copy.wait()


def lane_hits(lists, base):
    ids = base + lax.broadcasted_iota(jnp.int32, (BR, W), 1) // B
    hit = jnp.zeros((BR, W), F32)
    for t in range(lists.shape[1]):
        hit = jnp.where(lists[:, t : t + 1] == ids, 1.0, hit)
    return hit


def slots_of(hit):
    below = lax.broadcasted_iota(jnp.int32, (BR, BR), 1) < lax.broadcasted_iota(
        jnp.int32, (BR, BR), 0
    )
    rank = jnp.dot(
        jnp.where(below, 1.0, 0.0).astype(BF16), hit.astype(BF16), preferred_element_type=F32
    )
    return jnp.where(hit > 0.0, rank, float(CAP))


def pack_kernel(base_ref, list_hbm, tile_hbm, pay_ref, left_ref, places_ref, list_ref, tile_ref, sems):
    copies_in([(list_hbm, list_ref), (tile_hbm, tile_ref)], sems)
    lists = list_ref[...]
    hit = lane_hits(lists, base_ref[0])
    slot = slots_of(hit)
    slot_int = slot.astype(jnp.int32)
    packed = [jnp.zeros((B, W), F32) for _ in range(CAP)]
    for i in range(BR):
        block = tile_ref[pl.ds(i * B, B), :].astype(F32)
        row = jnp.broadcast_to(slot_int[i : i + 1, :], (B, W))
        for s in range(min(i + 1, CAP)):
            packed[s] = jnp.where(row == s, block, packed[s])
    for s in range(CAP):
        value = packed[s].astype(BF16)
        pay_ref[pl.ds(s * B, B), :] = value
        for x in range(TILES):
            left_ref[x, s] = value
    pay_ref[pl.ds(CAP * B, B), :] = slot.astype(BF16)
    pay_ref[pl.ds((CAP + 1) * B, PAY - (CAP + 1) * B), :] = jnp.zeros(
        (PAY - (CAP + 1) * B, W), BF16
    )

    ids = lax.broadcasted_iota(jnp.int32, (BR, NB), 1)
    every = jnp.zeros((BR, NB), F32)
    for t in range(KX):
        every = jnp.where(lists[:, t : t + 1] == ids, 1.0, every)
    slot = slots_of(every)
    rows = lax.broadcasted_iota(jnp.int32, (BR, NB), 0).astype(F32) - BR
    for s in range(CAP):
        at = jnp.sum(jnp.where(slot == s, rows, 0.0), axis=0, keepdims=True) + BR
        places_ref[pl.ds(s, 1), :] = at.astype(jnp.int32)


def pack(base, list_x, tile):
    return pl.pallas_call(
        pack_kernel,
        out_shape=(
            jax.ShapeDtypeStruct((PAY, W), BF16),
            jax.ShapeDtypeStruct((TILES, CAP, B, W), BF16),
            jax.ShapeDtypeStruct((CAP, NB), jnp.int32),
        ),
        in_specs=[SMEM, HBM, HBM],
        out_specs=(VMEM,) * 3,
        scratch_shapes=[
            pltpu.VMEM((BR, KX), jnp.int32),
            pltpu.VMEM((ROWS, W), BF16),
            pltpu.SemaphoreType.DMA((2,)),
        ],
        compiler_params=params(48),
        cost_estimate=cost(10_000_000, 500_000),
        name="pack",
    )(base, list_x, tile)


def right_kernel(table_ref, base_ref, *refs):
    lists_hbm, mine_hbm, other_hbm, right_ref, masks_ref = refs[:3], *refs[3:7]
    lists, pays_ref, sems = refs[7:10], refs[10], refs[11]
    rows = pl.ds(0, (CAP + 1) * B)
    pairs = list(zip(lists_hbm, lists))
    pairs += [(ref.at[:, rows], pays_ref.at[k]) for k, ref in enumerate((mine_hbm, other_hbm))]
    copies_in(pairs, sems)
    for k in range(3):
        masks_ref[k] = lane_hits(lists[k][...], base_ref[0])

    @pl.loop(0, 2 * TILES)
    def _(h):
        g, core = table_ref[2 * h], table_ref[2 * h + 1]
        first = pl.multiple_of(CAP * B + core * (BR // 2), BR // 2)
        for k in range(2):
            part = [pays_ref[k, g, pl.ds(s * B, B), :].astype(F32) for s in range(CAP)]
            slot = pays_ref[k, g, pl.ds(first, BR // 2), :].astype(F32).astype(jnp.int32)
            for t in range(BR // 2):
                row = jnp.broadcast_to(slot[t : t + 1, :], (B, W))
                value = jnp.zeros((B, W), F32)
                for s in range(CAP):
                    value = jnp.where(row == s, part[s], value)
                right_ref[h, pl.ds(t * B, B), pl.ds(k * W, W)] = value.astype(BF16)


def right(table, base, lists, mine, other):
    return pl.pallas_call(
        right_kernel,
        out_shape=(
            jax.ShapeDtypeStruct((2 * TILES, HALF, 2 * W), BF16),
            jax.ShapeDtypeStruct((3, BR, W), F32),
        ),
        in_specs=[SMEM, SMEM] + [HBM] * 5,
        out_specs=(VMEM, VMEM),
        scratch_shapes=[pltpu.VMEM(a.shape, jnp.int32) for a in lists]
        + [
            pltpu.VMEM((2, GROUPS, (CAP + 1) * B, W), BF16),
            pltpu.SemaphoreType.DMA((5,)),
        ],
        compiler_params=params(48),
        cost_estimate=cost(40_000_000, 4 * MIB),
        name="right",
    )(table, base, *lists, mine, other)


def widen(first, halves, table, places, dense=None):
    count = len(halves)

    def kernel(table_ref, places_ref, *refs):
        packed, refs = refs[:count], refs[count:]
        dense_ref, rows, wide, sems = refs if dense is None else refs[1:]
        lane = lax.broadcasted_iota(jnp.int32, (B, W), 1) // B
        masks = [lane == c for c in range(W // B)]
        puts = []
        for k in range(count):
            g, core = table_ref[2 * (first + k)], table_ref[2 * (first + k) + 1]
            start = (g * 2 + core) * HALF // B
            for q in range(TILES):
                rows[q, pl.ds(0, BR)] = jnp.zeros((BR, B, W), F32)
            for q in range(TILES):
                for s in range(CAP):
                    block = packed[k][q, s].astype(F32)
                    for c in range(W // B):
                        row = places_ref[s, start + q * (W // B) + c]
                        pltpu.store(rows.at[q, row], block, mask=masks[c])
            for q in range(TILES):
                for i in range(BR):
                    wide[k, pl.ds(i * B, B), pl.ds(q * W, W)] = rows[q, i].astype(BF16)
            put = pltpu.make_async_copy(wide.at[k], dense_ref.at[first + k], sems.at[k])
            put.start()
            puts.append(put)
        for put in puts:
            put.wait()

    operands, specs = [table, places, *halves], [SMEM, SMEM] + [VMEM] * count
    aliases = {}
    if dense is not None:
        aliases = {len(operands): 0}
        operands.append(dense)
        specs.append(HBM)
    return pl.pallas_call(
        kernel,
        out_shape=jax.ShapeDtypeStruct((2 * TILES, ROWS, HALF), BF16),
        in_specs=specs,
        out_specs=HBM,
        scratch_shapes=[
            pltpu.VMEM((TILES, BR + 1, B, W), F32),
            pltpu.VMEM((count, ROWS, HALF), BF16),
            pltpu.SemaphoreType.DMA((count,)),
        ],
        input_output_aliases=aliases,
        compiler_params=params(50),
        cost_estimate=cost(4 * ROWS * HALF * W * count, count * 3 * MIB),
        name="widen",
    )(*operands)


STEP = 256


def product_kernel(dense_ref, right_ref, mine_ref, other_ref):
    total = jnp.dot(dense_ref[0], right_ref[0], preferred_element_type=F32)
    for k in range(1, 2 * TILES):
        total += jnp.dot(dense_ref[k], right_ref[k], preferred_element_type=F32)
    mine_ref[...] = total[:, :W]
    other_ref[...] = total[:, W:]


def product(dense, right_side):
    part = pl.BlockSpec((STEP, W), lambda i: (i, 0))
    return pl.pallas_call(
        product_kernel,
        out_shape=(jax.ShapeDtypeStruct((ROWS, W), F32),) * 2,
        grid=(ROWS // STEP,),
        in_specs=[
            pl.BlockSpec((2 * TILES, STEP, HALF), lambda i: (0, i, 0)),
            pl.BlockSpec((2 * TILES, HALF, 2 * W), lambda i: (0, 0, 0)),
        ],
        out_specs=(part, part),
        compiler_params=params(50),
        cost_estimate=cost(8 * ROWS * ROWS * W * 2, 12 * MIB),
        name="product",
    )(dense, right_side)


def finish_kernel(mine_ref, other_ref, masks_ref, square_ref):
    scale = (NB / (KX * KX * B)) ** 0.5
    for i in range(BR):
        rows = pl.ds(i * B, B)
        keep = jnp.broadcast_to(masks_ref[1, i : i + 1, :], (B, W))
        value = (mine_ref[rows, :] + other_ref[rows, :]) * scale
        square_ref[rows, :] = jnp.where(keep > 0.0, value, 0.0).astype(BF16)


def finish(mine, other, masks):
    return pl.pallas_call(
        finish_kernel,
        out_shape=jax.ShapeDtypeStruct((ROWS, W), BF16),
        in_specs=[VMEM] * 3,
        out_specs=VMEM,
        cost_estimate=cost(400_000, MIB),
        name="finish",
    )(mine, other, masks)


def cube_part(steps, table, own, other, pieces, acc=None, last=None):
    scale = (NB / (KX * KSQ * B)) ** 0.5
    count = len(pieces)

    def kernel(table_ref, own_ref, other_ref, *refs):
        refs = list(refs)
        pieces_refs = [[refs.pop(0) for _ in piece] for piece in pieces]
        acc_ref = refs.pop(0) if acc is not None else None
        tile_ref, masks_ref = (refs.pop(0), refs.pop(0)) if last is not None else (None, None)
        out_ref, held, sems = refs
        y, row, core = (table_ref[4 * TILES + k] for k in range(3))
        for h in range(2 * count):
            d = jnp.bitwise_and((y - row - steps[h // 2]) * (1 - 2 * core), GROUPS - 1)
            same = core == h % 2
            ours = jnp.logical_or(jnp.logical_and(same, d <= 4), jnp.logical_and(d > 0, d < 4))
            d = jnp.where(d > 4, GROUPS - d, d)
            at = jnp.where(d == 0, 0, 2 * d - jnp.where(same == ours, 1, 0))
            at = jnp.where(d == 4, 2 * TILES - 1, at)
            at = jnp.where(ours, at, at + 2 * TILES)

            @pl.when(at < 2 * TILES)
            def _():
                pltpu.make_async_copy(own_ref.at[at], held.at[h], sems.at[h]).start()

            @pl.when(at >= 2 * TILES)
            def _():
                pltpu.make_async_copy(other_ref.at[at - 2 * TILES], held.at[h], sems.at[h]).start()

        total = None if acc_ref is None else acc_ref[...]
        for h in range(2 * count):
            pltpu.make_async_copy(own_ref.at[0], held.at[h], sems.at[h]).wait()
            refs_of = pieces_refs[h // 2]
            if len(refs_of) == 2:
                piece = refs_of[h % 2][...]
            else:
                piece = refs_of[0][pl.ds(h % 2 * HALF, HALF), :]
            term = jnp.dot(held[h], piece, preferred_element_type=F32)
            total = term if total is None else total + term
        if last is None:
            out_ref[...] = total
            return
        for k in range(BR):
            rows = pl.ds(k * B, B)
            keep_x = jnp.broadcast_to(masks_ref[0, k : k + 1, :], (B, W))
            keep_out = jnp.broadcast_to(masks_ref[2, k : k + 1, :], (B, W))
            sparse = jnp.where(keep_x > 0.0, tile_ref[rows, :].astype(F32), 0.0)
            cube = total[k * B : (k + 1) * B, :] * scale
            result = 1.5 * sparse - 0.5 * cube
            out_ref[rows, :] = jnp.where(keep_out > 0.0, result, 0.0).astype(BF16)

    operands = [table, own, other] + [array for piece in pieces for array in piece]
    if acc is not None:
        operands.append(acc)
    if last is not None:
        operands += last
    return pl.pallas_call(
        kernel,
        out_shape=jax.ShapeDtypeStruct((ROWS, W), F32 if last is None else BF16),
        in_specs=[SMEM, HBM, HBM] + [VMEM] * (len(operands) - 3),
        out_specs=VMEM,
        scratch_shapes=[
            pltpu.VMEM((2 * count, ROWS, HALF), BF16),
            pltpu.SemaphoreType.DMA((2 * count,)),
        ],
        compiler_params=params(50),
        cost_estimate=cost(2 * ROWS * ROWS * W * count, count * 3 * MIB + MIB),
        name="cube_last" if last is not None else "cube_part",
    )(*operands)


def local(matrix, list_x, list_sq, list_out):
    layers = lax.axis_size("layer")
    col = lax.axis_index("col").astype(jnp.int32)
    row = lax.axis_index("row").astype(jnp.int32)
    layer = lax.axis_index("layer").astype(jnp.int32)
    y, core = col // 2, col % 2
    sign = 1 - 2 * core
    base = jnp.reshape((col * layers + layer) * (W // B), (1,))

    brought = [(0, 1), (1, 1), (1, 0), (2, 1), (2, 0), (3, 1), (3, 0), (4, 1)]
    table = []
    for d, same in brought:
        table += [jnp.bitwise_and(y - sign * d, GROUPS - 1), core if same else 1 - core]
    table = jnp.stack(table + [y, row, core])
    cols = 2 * GROUPS
    swap = [(c, c ^ 1) for c in range(cols)]
    turn_y = [(c, (c + (2 if c % 2 == 0 else -2)) % cols) for c in range(cols)]

    def along_y(piece):
        return lax.ppermute(piece, "col", turn_y)

    def along_z(piece, step):
        return lax.ppermute(piece, "row", [(r, (r + step) % GROUPS) for r in range(GROUPS)])

    def across(piece):
        return lax.ppermute(piece, "col", swap)

    def after(piece, *done):
        return lax.optimization_barrier((piece, *done))[0]

    pay, left, places = pack(base, list_x, matrix)
    pays = lax.all_gather(pay, "row", axis=0, tiled=False)
    a0 = lax.all_to_all(left, "layer", 0, 0, tiled=True)
    b0 = across(a0)
    a1, b1 = along_y(a0), along_y(b0)
    dense = widen(0, [a0], table, places)
    a2, b2 = along_y(after(a1, dense)), along_y(b1)
    dense = widen(1, [a1, b1], table, places, dense)
    a3, b3 = along_y(after(a2, dense)), along_y(b2)
    dense = widen(3, [a2, b2], table, places, dense)
    a4 = along_y(after(a3, dense))
    dense = widen(5, [a3, b3], table, places, dense)
    pays = after(pays, dense)
    right_side, masks = right(table, base, (list_x, list_sq, list_out), pays, across(pays))
    dense = widen(7, [a4], table, places, dense)
    mine, other = product(dense, right_side)
    square = finish(mine, across(other), masks)

    def cubed(distance, pieces, *more):
        steps = [distance] if distance in (0, GROUPS // 2) else [-distance, distance]
        return cube_part(steps, table, dense, theirs, pieces, *more)

    down, up = along_z(square, 1), along_z(square, -1)
    theirs = across(after(dense, square))
    acc = cubed(0, [(square,)])
    down2, up2 = along_z(down, 1), along_z(up, -1)
    acc = cubed(1, [(down,), (up,)], acc)
    down3, up3 = along_z(after(down2, acc), 1), along_z(up2, -1)
    acc = cubed(2, [(down2,), (up2,)], acc)
    down4, up4 = along_z(after(down3[:HALF], acc), 1), along_z(up3[HALF:], -1)
    acc = cubed(3, [(down3,), (up3,)], acc)
    return cubed(4, [(down4, up4)], acc, (matrix, masks))


def solution(mesh):
    placed = (P("row", ("col", "layer")), P("row", None), P("row", None), P("row", None))
    return jax.shard_map(
        local, mesh=mesh, in_specs=placed, out_specs=P("row", ("col", "layer")), check_vma=False
    )
```

time: 220 us -> 170 us (0.77)
  the two profiles are of different devices: /device:TPU:16 before, /device:TPU:32 now
where the time goes in v3:
time: 170 us; the launch traced here: 169 us
  starting transfers between devices  57.8 us (34%)
  Pallas kernels  45.4 us (27%)
  waiting for transfers between devices  32.8 us (19%)
  between operations  13.9 us (8%)
  blocking collectives  11.5 us (7%)
  local copies, waits for them, and re-layouts  7.63 us (4%)
    ppermute x8, starting transfers between devices, along_z(): lax.ppermute(piece, 'row', [(r, (r + step) % GROUPS) for r in range(GROUP...  35.2 us
    ppermute x7, waiting for transfers between devices, along_y(): return lax.ppermute(piece, 'col', turn_y)  21.3 us
    pallas_call x5, Pallas kernels, cube_part(): pl.pallas_call(kernel, out_shape=jax.ShapeDtypeStruct((ROWS, W), F32 if l...  19.8 us
    ppermute x7, starting transfers between devices, along_y(): return lax.ppermute(piece, 'col', turn_y)  14.7 us
    pallas_call x5, Pallas kernels, widen(): pl.pallas_call(kernel, out_shape=jax.ShapeDtypeStruct((2 * TILES, ROWS, H...  13 us
    all_to_all x1, blocking collectives, local(): a0 = lax.all_to_all(left, 'layer', 0, 0, tiled=True)  11.5 us
    ppermute x8, waiting for transfers between devices, along_z(): lax.ppermute(piece, 'row', [(r, (r + step) % GROUPS) for r in range(GROUP...  9.57 us
    ppermute x4, starting transfers between devices, across(): return lax.ppermute(piece, 'col', swap)  7.9 us
  transfers between devices with their start and end apart: 20, of which 11 were waited for; matrix products, arithmetic and copies ran while one was open for 0% of the time, Pallas kernels for 17%

profile of v3, /device:TPU:32, one launch (start us, length us, event | category | flops | bytes accessed | tf_op | source)
XLA Modules:
  0.0 169.0 jit_solution(514570601168011081)
XLA Ops:
  9.6 11.5 %all_to_all.5.refs_0_ = bf16[4,10,32,128]{3,2,1,0:T(8,128)(2,1)S(1)} all-to-all(bf16[4,10,32,128]{3,2,1,0:T(8,128)(2,1)S(1)} %get-tuple-element.20), channel_id=1, replica_groups=mesh['row'=8,'col'=16,'layer'=4] {'layer'}, dimensions={0} | all-to-all | bytes 655360 | tf_op jit(solution)/shard_map/all_to_all | solution.py:363
  23.0 2.6 %collective-permute-start = (bf16[4,10,32,128]{3,2,1,0:T(8,128)(2,1)S(1)}, bf16[4,10,32,128]{3,2,1,0:T(8,128)(2,1)S(1)}, u32[]{:S(2)}, u32[]{:S(2)}) collective-permute-start(bf16[4,10,32,128]{3,2,1,0:T(8,128)(2,1)S(1)} %all_to_all.5.refs_0_), channel_id=1, source_target_pairs={{0,8},{4,60},{8,16},{12,4},{16,24},{20,12},{24,32},{28,20},{32,40}... | collective-permute-start | bytes 983048 | tf_op jit(solution)/shard_map/ppermute | solution.py:350
  25.6 2.6 %collective-permute-start.3 = (bf16[4,10,32,128]{3,2,1,0:T(8,128)(2,1)S(1)}, bf16[4,10,32,128]{3,2,1,0:T(8,128)(2,1)S(1)}, u32[]{:S(2)}, u32[]{:S(2)}) collective-permute-start(bf16[4,10,32,128]{3,2,1,0:T(8,128)(2,1)S(1)} %collective-permute-done.2), channel_id=1, source_target_pairs={{0,8},{4,60},{8,16},{12,4},{16,24},{20,12},{24,32},{28,20},{32,40}... | collective-permute-start | bytes 983048 | tf_op jit(solution)/shard_map/ppermute | solution.py:350
  28.3 2.3 %widen.5.refs_2_ = bf16[8,1024,512]{2,1,0:T(8,128)(2,1)} custom-call(s32[19]{0:T(128)S(1)} %stack.49.table_ref, s32[10,256]{1,0:T(8,128)S(1)} %get-tuple-element.19.places_ref, bf16[4,10,32,128]{3,2,1,0:T(8,128)(2,1)S(1)} %all_to_all.5.refs_0_), custom_call_target="tpu_custom_call" | custom-call | flops 268435456 | bytes 3145728 | tf_op jit(solution)/shard_map/widen/pallas_call | solution.py:196
  30.7 2.5 %collective-permute-done.refs_0_ = bf16[4,10,32,128]{3,2,1,0:T(8,128)(2,1)S(1)} collective-permute-done((bf16[4,10,32,128]{3,2,1,0:T(8,128)(2,1)S(1)}, bf16[4,10,32,128]{3,2,1,0:T(8,128)(2,1)S(1)}, u32[]{:S(2)}, u32[]{:S(2)}) %collective-permute-start) | collective-permute-done | bytes 327712 | tf_op jit(solution)/shard_map/ppermute | solution.py:350
  38.6 2.8 %widen.6.refs_2_ = bf16[8,1024,512]{2,1,0:T(8,128)(2,1)} custom-call(s32[19]{0:T(128)S(1)} %stack.49.table_ref, s32[10,256]{1,0:T(8,128)S(1)} %get-tuple-element.19.places_ref, bf16[4,10,32,128]{3,2,1,0:T(8,128)(2,1)S(1)} %collective-permute-done.refs_0_, ...), custom_call_target="tpu_custom_call", output_to_operand_aliasing={{}: (4, {})} | custom-call | flops 536870912 | bytes 6291456 | tf_op jit(solution)/shard_map/widen/pallas_call | solution.py:196
  48.8 2.8 %widen.7.refs_2_ = bf16[8,1024,512]{2,1,0:T(8,128)(2,1)} custom-call(s32[19]{0:T(128)S(1)} %stack.49.table_ref, s32[10,256]{1,0:T(8,128)S(1)} %get-tuple-element.19.places_ref, bf16[4,10,32,128]{3,2,1,0:T(8,128)(2,1)S(1)} %collective-permute-done.1.refs_0_, ...), custom_call_target="tpu_custom_call", output_to_operand_aliasing={{}: (4, {})} | custom-call | flops 536870912 | bytes 6291456 | tf_op jit(solution)/shard_map/widen/pallas_call | solution.py:196
  53.5 3.5 %collective-permute-done.7.refs_1_ = bf16[4,10,32,128]{3,2,1,0:T(8,128)(2,1)S(1)} collective-permute-done((bf16[4,10,32,128]{3,2,1,0:T(8,128)(2,1)S(1)}, bf16[4,10,32,128]{3,2,1,0:T(8,128)(2,1)S(1)}, u32[]{:S(2)}, u32[]{:S(2)}) %collective-permute-start.7) | collective-permute-done | bytes 327712 | tf_op jit(solution)/shard_map/ppermute | solution.py:350
  57.0 2.8 %widen.8.refs_1_ = bf16[8,1024,512]{2,1,0:T(8,128)(2,1)} custom-call(s32[19]{0:T(128)S(1)} %stack.49.table_ref, s32[10,256]{1,0:T(8,128)S(1)} %get-tuple-element.19.places_ref, bf16[4,10,32,128]{3,2,1,0:T(8,128)(2,1)S(1)} %collective-permute-done.4.refs_0_, ...), custom_call_target="tpu_custom_call", output_to_operand_aliasing={{}: (4, {})} | custom-call | flops 536870912 | bytes 6291456 | tf_op jit(solution)/shard_map/widen/pallas_call | solution.py:196
  63.9 8.3 %collective-permute-done.6.refs_0_ = bf16[4,10,32,128]{3,2,1,0:T(8,128)(2,1)S(1)} collective-permute-done((bf16[4,10,32,128]{3,2,1,0:T(8,128)(2,1)S(1)}, bf16[4,10,32,128]{3,2,1,0:T(8,128)(2,1)S(1)}, u32[]{:S(2)}, u32[]{:S(2)}) %collective-permute-start.6) | collective-permute-done | bytes 327712 | tf_op jit(solution)/shard_map/ppermute | solution.py:350
  74.5 3.7 %right.1 = (bf16[8,512,256]{2,1,0:T(8,128)(2,1)S(1)}, f32[3,32,128]{2,1,0:T(8,128)S(1)}) custom-call(s32[19]{0:T(128)S(1)} %stack.49.table_ref, s32[1]{0:T(128)} %bitcast.9.base_ref, s32[32,40]{1,0:T(8,128)S(1)} %copy-done.8, s32[32,60]{1,0:T(8,128)S(1)} %copy-done.9, s32[32,40]{1,0:T(8,128)S(1)} %copy-done.10, bf16[8,576,128]{2,1,0:T(8,128)(2,1)S(1)} %bitcast.12, ...), custom_call_target="tpu_custom_call" | custom-call | flops 40000000 | bytes 4194304 | tf_op jit(solution)/shard_map/right/pallas_call | solution.py:142
  78.2 5.5 %product.1 = (f32[1024,128]{1,0:T(8,128)S(1)}, f32[1024,128]{1,0:T(8,128)S(1)}) custom-call(bf16[8,1024,512]{2,1,0:T(8,128)(2,1)} %widen.9.dense_ref.own_ref, bf16[8,512,256]{2,1,0:T(8,128)(2,1)S(1)} %get-tuple-element.26.right_ref), custom_call_target="tpu_custom_call" | custom-call | flops 2147483648 | bytes 12582912 | tf_op jit(solution)/shard_map/product/pallas_call | solution.py:226
  93.2 11.0 %collective-permute-start.13 = (bf16[1024,128]{1,0:T(8,128)(2,1)}, bf16[1024,128]{1,0:T(8,128)(2,1)S(1)}, u32[]{:S(2)}, u32[]{:S(2)}) collective-permute-start(bf16[1024,128]{1,0:T(8,128)(2,1)} %finish.1.refs_0_), channel_id=1, source_target_pairs={{0,448},{64,0},{128,64},{192,128},{256,192},{320,256},{384,320},{4... | collective-permute-start | bytes 786440 | tf_op jit(solution)/shard_map/ppermute | solution.py:353
  106.1 4.5 %collective-permute-done.13.refs_1_ = bf16[1024,128]{1,0:T(8,128)(2,1)S(1)} collective-permute-done((bf16[1024,128]{1,0:T(8,128)(2,1)}, bf16[1024,128]{1,0:T(8,128)(2,1)S(1)}, u32[]{:S(2)}, u32[]{:S(2)}) %collective-permute-start.13) | collective-permute-done | bytes 262176 | tf_op jit(solution)/shard_map/ppermute | solution.py:353
  110.6 5.5 %collective-permute-start.15 = (bf16[1024,128]{1,0:T(8,128)(2,1)S(1)}, bf16[1024,128]{1,0:T(8,128)(2,1)S(1)}, u32[]{:S(2)}, u32[]{:S(2)}) collective-permute-start(bf16[1024,128]{1,0:T(8,128)(2,1)S(1)} %collective-permute-done.13.refs_1_), channel_id=1, source_target_pairs={{0,448},{64,0},{128,64},{192,128},{256,192},{320,256},{384,320},{4... | collective-permute-start | bytes 786440 | tf_op jit(solution)/shard_map/ppermute | solution.py:353
  118.0 3.3 %collective-permute-done.15.refs_1_ = bf16[1024,128]{1,0:T(8,128)(2,1)S(1)} collective-permute-done((bf16[1024,128]{1,0:T(8,128)(2,1)S(1)}, bf16[1024,128]{1,0:T(8,128)(2,1)S(1)}, u32[]{:S(2)}, u32[]{:S(2)}) %collective-permute-start.15) | collective-permute-done | bytes 262176 | tf_op jit(solution)/shard_map/ppermute | solution.py:353
  121.3 5.6 %collective-permute-start.17 = (bf16[1024,128]{1,0:T(8,128)(2,1)S(1)}, bf16[1024,128]{1,0:T(8,128)(2,1)S(1)}, u32[]{:S(2)}, u32[]{:S(2)}) collective-permute-start(bf16[1024,128]{1,0:T(8,128)(2,1)S(1)} %collective-permute-done.15.refs_1_), channel_id=1, source_target_pairs={{0,448},{64,0},{128,64},{192,128},{256,192},{320,256},{384,320},{4... | collective-permute-start | bytes 786440 | tf_op jit(solution)/shard_map/ppermute | solution.py:353
  126.9 3.3 %copy-done.11 = bf16[8,1024,512]{2,1,0:T(8,128)(2,1)} copy-done((bf16[8,1024,512]{2,1,0:T(8,128)(2,1)}, bf16[8,1024,512]{2,1,0:T(8,128)(2,1)S(1)}, u32[]{:S(2)}) %copy-start.11) | copy-done | bytes 8388632
  131.1 2.8 %cube_part.4.refs_2_ = f32[1024,128]{1,0:T(8,128)S(1)} custom-call(s32[19]{0:T(128)S(1)} %stack.49.table_ref, bf16[8,1024,512]{2,1,0:T(8,128)(2,1)} %widen.9.dense_ref.own_ref, bf16[8,1024,512]{2,1,0:T(8,128)(2,1)} %copy-done.11, bf16[1024,128]{1,0:T(8,128)(2,1)S(1)} %copy-done.3), custom_call_target="tpu_custom_call" | custom-call | flops 268435456 | bytes 4194304 | tf_op jit(solution)/shard_map/cube_part/pallas_call | solution.py:316
  134.0 4.3 %cube_part.5.refs_2_ = f32[1024,128]{1,0:T(8,128)S(1)} custom-call(s32[19]{0:T(128)S(1)} %stack.49.table_ref, bf16[8,1024,512]{2,1,0:T(8,128)(2,1)} %widen.9.dense_ref.own_ref, bf16[8,1024,512]{2,1,0:T(8,128)(2,1)} %copy-done.11, bf16[1024,128]{1,0:T(8,128)(2,1)S(1)} %collective-permute-done.11.refs_0_, ...), custom_call_target="tpu_custom_call" | custom-call | flops 536870912 | bytes 7340032 | tf_op jit(solution)/shard_map/cube_part/pallas_call | solution.py:316
  140.3 5.3 %collective-permute-start.18 = (bf16[512,128]{1,0:T(8,128)(2,1)S(1)}, bf16[512,128]{1,0:T(8,128)(2,1)S(1)}, u32[]{:S(2)}, u32[]{:S(2)}) collective-permute-start(bf16[512,128]{1,0:T(8,128)(2,1)S(1)} %slice.9), channel_id=1, source_target_pairs={{0,448},{64,0},{128,64},{192,128},{256,192},{320,256},{384,320},{4... | collective-permute-start | bytes 393224 | tf_op jit(solution)/shard_map/ppermute | solution.py:353
  145.6 4.3 %cube_part.6.refs_2_ = f32[1024,128]{1,0:T(8,128)S(1)} custom-call(s32[19]{0:T(128)S(1)} %stack.49.table_ref, bf16[8,1024,512]{2,1,0:T(8,128)(2,1)} %widen.9.dense_ref.own_ref, bf16[8,1024,512]{2,1,0:T(8,128)(2,1)} %copy-done.11, bf16[1024,128]{1,0:T(8,128)(2,1)S(1)} %collective-permute-done.12.refs_0_, ...), custom_call_target="tpu_custom_call" | custom-call | flops 536870912 | bytes 7340032 | tf_op jit(solution)/shard_map/cube_part/pallas_call | solution.py:316
  152.1 4.3 %cube_part.7.refs_2_ = f32[1024,128]{1,0:T(8,128)S(1)} custom-call(s32[19]{0:T(128)S(1)} %stack.49.table_ref, bf16[8,1024,512]{2,1,0:T(8,128)(2,1)} %widen.9.dense_ref.own_ref, bf16[8,1024,512]{2,1,0:T(8,128)(2,1)} %copy-done.11, bf16[1024,128]{1,0:T(8,128)(2,1)S(1)} %collective-permute-done.14.refs_0_, ...), custom_call_target="tpu_custom_call" | custom-call | flops 536870912 | bytes 7340032 | tf_op jit(solution)/shard_map/cube_part/pallas_call | solution.py:316
  158.2 3.9 %cube_last.1 = bf16[1024,128]{1,0:T(8,128)(2,1)} custom-call(s32[19]{0:T(128)S(1)} %stack.49.table_ref, bf16[8,1024,512]{2,1,0:T(8,128)(2,1)} %widen.9.dense_ref.own_ref, bf16[8,1024,512]{2,1,0:T(8,128)(2,1)} %copy-done.11, bf16[512,128]{1,0:T(8,128)(2,1)S(1)} %collective-permute-done.16.refs_0_, bf16[512,128]{1,0:T(8,128)(2,1)S(1)} %collective-permute-done.18.refs_1_, ...), custom_call_target="tpu_custom_call" | custom-call | flops 268435456 | bytes 4194304 | tf_op jit(solution)/shard_map/cube_last/pallas_call | solution.py:316
  (61 shorter events, 46.0 us)
Async XLA Ops:
  6.5 53.3 %all-gather.3.cloned.1.call-start = ((), (), s32[]{:S(2)}) async-start(), calls=%async_computation.1 | async-start | bytes 1327104 | tf_op jit(solution)/shard_map/all_gather | solution.py:362
  21.1 4.5 %collective-permute-start.2 = (bf16[4,10,32,128]{3,2,1,0:T(8,128)(2,1)S(1)}, bf16[4,10,32,128]{3,2,1,0:T(8,128)(2,1)S(1)}, u32[]{:S(2)}, u32[]{:S(2)}) collective-permute-start(bf16[4,10,32,128]{3,2,1,0:T(8,128)(2,1)S(1)} %all_to_all.5.refs_0_), channel_id=1, source_target_pairs={{0,4},{4,0},{8,12},{12,8},{16,20},{20,16},{24,28},{28,24},{32,36},... | collective-permute-start | bytes 983048 | tf_op jit(solution)/shard_map/ppermute | solution.py:356
  23.0 10.2 %collective-permute-start = (bf16[4,10,32,128]{3,2,1,0:T(8,128)(2,1)S(1)}, bf16[4,10,32,128]{3,2,1,0:T(8,128)(2,1)S(1)}, u32[]{:S(2)}, u32[]{:S(2)}) collective-permute-start(bf16[4,10,32,128]{3,2,1,0:T(8,128)(2,1)S(1)} %all_to_all.5.refs_0_), channel_id=1, source_target_pairs={{0,8},{4,60},{8,16},{12,4},{16,24},{20,12},{24,32},{28,20},{32,40}... | collective-permute-start | bytes 983048 | tf_op jit(solution)/shard_map/ppermute | solution.py:350
  25.6 11.1 %collective-permute-start.3 = (bf16[4,10,32,128]{3,2,1,0:T(8,128)(2,1)S(1)}, bf16[4,10,32,128]{3,2,1,0:T(8,128)(2,1)S(1)}, u32[]{:S(2)}, u32[]{:S(2)}) collective-permute-start(bf16[4,10,32,128]{3,2,1,0:T(8,128)(2,1)S(1)} %collective-permute-done.2), channel_id=1, source_target_pairs={{0,8},{4,60},{8,16},{12,4},{16,24},{20,12},{24,32},{28,20},{32,40}... | collective-permute-start | bytes 983048 | tf_op jit(solution)/shard_map/ppermute | solution.py:350
  33.2 10.2 %collective-permute-start.1 = (bf16[4,10,32,128]{3,2,1,0:T(8,128)(2,1)S(1)}, bf16[4,10,32,128]{3,2,1,0:T(8,128)(2,1)S(1)}, u32[]{:S(2)}, u32[]{:S(2)}) collective-permute-start(bf16[4,10,32,128]{3,2,1,0:T(8,128)(2,1)S(1)} %collective-permute-done.refs_0_), channel_id=1, source_target_pairs={{0,8},{4,60},{8,16},{12,4},{16,24},{20,12},{24,32},{28,20},{32,40}... | collective-permute-start | bytes 983048 | tf_op jit(solution)/shard_map/ppermute | solution.py:350
  36.7 10.2 %collective-permute-start.5 = (bf16[4,10,32,128]{3,2,1,0:T(8,128)(2,1)S(1)}, bf16[4,10,32,128]{3,2,1,0:T(8,128)(2,1)S(1)}, u32[]{:S(2)}, u32[]{:S(2)}) collective-permute-start(bf16[4,10,32,128]{3,2,1,0:T(8,128)(2,1)S(1)} %collective-permute-done.3.refs_1_), channel_id=1, source_target_pairs={{0,8},{4,60},{8,16},{12,4},{16,24},{20,12},{24,32},{28,20},{32,40}... | collective-permute-start | bytes 983048 | tf_op jit(solution)/shard_map/ppermute | solution.py:350
  43.3 10.2 %collective-permute-start.4 = (bf16[4,10,32,128]{3,2,1,0:T(8,128)(2,1)S(1)}, bf16[4,10,32,128]{3,2,1,0:T(8,128)(2,1)S(1)}, u32[]{:S(2)}, u32[]{:S(2)}) collective-permute-start(bf16[4,10,32,128]{3,2,1,0:T(8,128)(2,1)S(1)} %collective-permute-done.1.refs_0_), channel_id=1, source_target_pairs={{0,8},{4,60},{8,16},{12,4},{16,24},{20,12},{24,32},{28,20},{32,40}... | collective-permute-start | bytes 983048 | tf_op jit(solution)/shard_map/ppermute | solution.py:350
  46.9 10.2 %collective-permute-start.7 = (bf16[4,10,32,128]{3,2,1,0:T(8,128)(2,1)S(1)}, bf16[4,10,32,128]{3,2,1,0:T(8,128)(2,1)S(1)}, u32[]{:S(2)}, u32[]{:S(2)}) collective-permute-start(bf16[4,10,32,128]{3,2,1,0:T(8,128)(2,1)S(1)} %collective-permute-done.5.refs_1_), channel_id=1, source_target_pairs={{0,8},{4,60},{8,16},{12,4},{16,24},{20,12},{24,32},{28,20},{32,40}... | collective-permute-start | bytes 983048 | tf_op jit(solution)/shard_map/ppermute | solution.py:350
  59.8 14.6 %copy-start = (bf16[4608,128]{1,0:T(8,128)(2,1)S(1)}, bf16[4608,128]{1,0:T(8,128)(2,1)}, u32[]{:S(2)}) copy-start(bf16[4608,128]{1,0:T(8,128)(2,1)} %all-gather.3.cloned.1.call-done) | copy-start | bytes 3538948
  59.9 14.6 %copy-start.8 = (s32[32,40]{1,0:T(8,128)S(1)}, s32[32,40]{1,0:T(8,128)}, u32[]{:S(2)}) copy-start(s32[32,40]{1,0:T(8,128)} %refs_0_.1) | copy-start | bytes 15364
  59.9 14.6 %copy-start.9 = (s32[32,60]{1,0:T(8,128)S(1)}, s32[32,60]{1,0:T(8,128)}, u32[]{:S(2)}) copy-start(s32[32,60]{1,0:T(8,128)} %refs_1_.1) | copy-start | bytes 23044
  59.9 14.6 %copy-start.10 = (s32[32,40]{1,0:T(8,128)S(1)}, s32[32,40]{1,0:T(8,128)}, u32[]{:S(2)}) copy-start(s32[32,40]{1,0:T(8,128)} %refs_2_.1) | copy-start | bytes 15364
  59.9 14.5 %collective-permute-start.8 = (bf16[8,576,128]{2,1,0:T(8,128)(2,1)}, bf16[8,576,128]{2,1,0:T(8,128)(2,1)S(1)}, u32[]{:S(2)}, u32[]{:S(2)}) collective-permute-start(bf16[8,576,128]{2,1,0:T(8,128)(2,1)} %bitcast.11), channel_id=1, source_target_pairs={{0,4},{4,0},{8,12},{12,8},{16,20},{20,16},{24,28},{28,24},{32,36},... | collective-permute-start | bytes 3538952 | tf_op jit(solution)/shard_map/ppermute | solution.py:356
  61.9 10.2 %collective-permute-start.6 = (bf16[4,10,32,128]{3,2,1,0:T(8,128)(2,1)S(1)}, bf16[4,10,32,128]{3,2,1,0:T(8,128)(2,1)S(1)}, u32[]{:S(2)}, u32[]{:S(2)}) collective-permute-start(bf16[4,10,32,128]{3,2,1,0:T(8,128)(2,1)S(1)} %collective-permute-done.4.refs_0_), channel_id=1, source_target_pairs={{0,8},{4,60},{8,16},{12,4},{16,24},{20,12},{24,32},{28,20},{32,40}... | collective-permute-start | bytes 983048 | tf_op jit(solution)/shard_map/ppermute | solution.py:350
  84.6 3.8 %collective-permute-start.9 = (f32[1024,128]{1,0:T(8,128)S(1)}, f32[1024,128]{1,0:T(8,128)S(1)}, u32[]{:S(2)}, u32[]{:S(2)}) collective-permute-start(f32[1024,128]{1,0:T(8,128)S(1)} %get-tuple-element.28), channel_id=1, source_target_pairs={{0,4},{4,0},{8,12},{12,8},{16,20},{20,16},{24,28},{28,24},{32,36},... | collective-permute-start | bytes 1572872 | tf_op jit(solution)/shard_map/ppermute | solution.py:356
  91.2 35.7 %collective-permute-start.10 = (bf16[8,1024,512]{2,1,0:T(8,128)(2,1)}, bf16[8,1024,512]{2,1,0:T(8,128)(2,1)S(1)}, u32[]{:S(2)}, u32[]{:S(2)}) collective-permute-start(bf16[8,1024,512]{2,1,0:T(8,128)(2,1)} %widen.9.dense_ref.own_ref), channel_id=1, source_target_pairs={{0,4},{4,0},{8,12},{12,8},{16,20},{20,16},{24,28},{28,24},{32,36},... | collective-permute-start | bytes 25165832 | tf_op jit(solution)/shard_map/ppermute | solution.py:356
  93.2 17.4 %collective-permute-start.13 = (bf16[1024,128]{1,0:T(8,128)(2,1)}, bf16[1024,128]{1,0:T(8,128)(2,1)S(1)}, u32[]{:S(2)}, u32[]{:S(2)}) collective-permute-start(bf16[1024,128]{1,0:T(8,128)(2,1)} %finish.1.refs_0_), channel_id=1, source_target_pairs={{0,448},{64,0},{128,64},{192,128},{256,192},{320,256},{384,320},{4... | collective-permute-start | bytes 786440 | tf_op jit(solution)/shard_map/ppermute | solution.py:353
  104.2 11.9 %collective-permute-start.11 = (bf16[1024,128]{1,0:T(8,128)(2,1)}, bf16[1024,128]{1,0:T(8,128)(2,1)S(1)}, u32[]{:S(2)}, u32[]{:S(2)}) collective-permute-start(bf16[1024,128]{1,0:T(8,128)(2,1)} %finish.1.refs_0_), channel_id=1, source_target_pairs={{0,64},{64,128},{128,192},{192,256},{256,320},{320,384},{384,448},... | collective-permute-start | bytes 786440 | tf_op jit(solution)/shard_map/ppermute | solution.py:353
  110.6 10.8 %collective-permute-start.15 = (bf16[1024,128]{1,0:T(8,128)(2,1)S(1)}, bf16[1024,128]{1,0:T(8,128)(2,1)S(1)}, u32[]{:S(2)}, u32[]{:S(2)}) collective-permute-start(bf16[1024,128]{1,0:T(8,128)(2,1)S(1)} %collective-permute-done.13.refs_1_), channel_id=1, source_target_pairs={{0,448},{64,0},{128,64},{192,128},{256,192},{320,256},{384,320},{4... | collective-permute-start | bytes 786440 | tf_op jit(solution)/shard_map/ppermute | solution.py:353
  116.1 22.3 %collective-permute-start.12 = (bf16[1024,128]{1,0:T(8,128)(2,1)S(1)}, bf16[1024,128]{1,0:T(8,128)(2,1)S(1)}, u32[]{:S(2)}, u32[]{:S(2)}) collective-permute-start(bf16[1024,128]{1,0:T(8,128)(2,1)S(1)} %collective-permute-done.11.refs_0_), channel_id=1, source_target_pairs={{0,64},{64,128},{128,192},{192,256},{256,320},{320,384},{384,448},... | collective-permute-start | bytes 786440 | tf_op jit(solution)/shard_map/ppermute | solution.py:353
  121.3 19.0 %collective-permute-start.17 = (bf16[1024,128]{1,0:T(8,128)(2,1)S(1)}, bf16[1024,128]{1,0:T(8,128)(2,1)S(1)}, u32[]{:S(2)}, u32[]{:S(2)}) collective-permute-start(bf16[1024,128]{1,0:T(8,128)(2,1)S(1)} %collective-permute-done.15.refs_1_), channel_id=1, source_target_pairs={{0,448},{64,0},{128,64},{192,128},{256,192},{320,256},{384,320},{4... | collective-permute-start | bytes 786440 | tf_op jit(solution)/shard_map/ppermute | solution.py:353
  138.3 11.6 %collective-permute-start.14 = (bf16[1024,128]{1,0:T(8,128)(2,1)S(1)}, bf16[1024,128]{1,0:T(8,128)(2,1)S(1)}, u32[]{:S(2)}, u32[]{:S(2)}) collective-permute-start(bf16[1024,128]{1,0:T(8,128)(2,1)S(1)} %collective-permute-done.12.refs_0_), channel_id=1, source_target_pairs={{0,64},{64,128},{128,192},{192,256},{256,320},{320,384},{384,448},... | collective-permute-start | bytes 786440 | tf_op jit(solution)/shard_map/ppermute | solution.py:353
  140.3 16.1 %collective-permute-start.18 = (bf16[512,128]{1,0:T(8,128)(2,1)S(1)}, bf16[512,128]{1,0:T(8,128)(2,1)S(1)}, u32[]{:S(2)}, u32[]{:S(2)}) collective-permute-start(bf16[512,128]{1,0:T(8,128)(2,1)S(1)} %slice.9), channel_id=1, source_target_pairs={{0,448},{64,0},{128,64},{192,128},{256,192},{320,256},{384,320},{4... | collective-permute-start | bytes 393224 | tf_op jit(solution)/shard_map/ppermute | solution.py:353
  150.0 8.2 %collective-permute-start.16 = (bf16[512,128]{1,0:T(8,128)(2,1)S(1)}, bf16[512,128]{1,0:T(8,128)(2,1)S(1)}, u32[]{:S(2)}, u32[]{:S(2)}) collective-permute-start(bf16[512,128]{1,0:T(8,128)(2,1)S(1)} %slice.8), channel_id=1, source_target_pairs={{0,64},{64,128},{128,192},{192,256},{256,320},{320,384},{384,448},... | collective-permute-start | bytes 393224 | tf_op jit(solution)/shard_map/ppermute | solution.py:353
  (9 other events, 29.5 us)
Sparse Core Ops, SparseCore 0:
  9.7 46.6 all-gather.2

commit v4 on v3

v4 whole, which is shorter than its diff:
```python
import jax
import jax.numpy as jnp
from jax import lax
from jax.experimental import pallas as pl
from jax.experimental.pallas import tpu as pltpu
from jax.sharding import PartitionSpec as P

B = 32
NB = 256
KX = 40
KSQ = 60
CAP = 10
ROWS = 1024
W = 128
BR = ROWS // B
GROUPS = 8
TILES = 4
HALF = TILES * W
PAY = 576
FIRST, REST = 5, 3
F32 = jnp.float32
BF16 = jnp.bfloat16
MIB = 1 << 20
SMEM = pl.BlockSpec(memory_space=pltpu.SMEM)
VMEM = pl.BlockSpec(memory_space=pltpu.VMEM)
HBM = pl.BlockSpec(memory_space=pltpu.HBM)


def params(limit):
    return pltpu.CompilerParams(vmem_limit_bytes=limit * MIB)


COST = pl.CostEstimate(flops=1, bytes_accessed=1, transcendentals=0)


def copies_in(pairs, sems):
    copies = [pltpu.make_async_copy(a, b, sems.at[k]) for k, (a, b) in enumerate(pairs)]
    for copy in copies:
        copy.start()
    for copy in copies:
        copy.wait()


def lane_hits(lists, base):
    ids = base + lax.broadcasted_iota(jnp.int32, (BR, W), 1) // B
    hit = jnp.zeros((BR, W), F32)
    for t in range(lists.shape[1]):
        hit = jnp.where(lists[:, t : t + 1] == ids, 1.0, hit)
    return hit


def slots_of(hit):
    below = lax.broadcasted_iota(jnp.int32, (BR, BR), 1) < lax.broadcasted_iota(
        jnp.int32, (BR, BR), 0
    )
    rank = jnp.dot(
        jnp.where(below, 1.0, 0.0).astype(BF16), hit.astype(BF16), preferred_element_type=F32
    )
    return jnp.where(hit > 0.0, rank, float(CAP))


def pack_kernel(base_ref, list_hbm, tile_hbm, pay_ref, left_ref, places_ref, list_ref, tile_ref, sems):
    copies_in([(list_hbm, list_ref), (tile_hbm, tile_ref)], sems)
    lists = list_ref[...]
    hit = lane_hits(lists, base_ref[0])
    slot = slots_of(hit)
    slot_int = slot.astype(jnp.int32)
    packed = [jnp.zeros((B, W), F32) for _ in range(CAP)]
    for i in range(BR):
        block = tile_ref[pl.ds(i * B, B), :].astype(F32)
        row = jnp.broadcast_to(slot_int[i : i + 1, :], (B, W))
        for s in range(min(i + 1, CAP)):
            packed[s] = jnp.where(row == s, block, packed[s])
    for s in range(CAP):
        value = packed[s].astype(BF16)
        pay_ref[pl.ds(s * B, B), :] = value
        for x in range(TILES):
            left_ref[x, s] = value
    pay_ref[pl.ds(CAP * B, B), :] = slot.astype(BF16)
    pay_ref[pl.ds((CAP + 1) * B, PAY - (CAP + 1) * B), :] = jnp.zeros(
        (PAY - (CAP + 1) * B, W), BF16
    )

    ids = lax.broadcasted_iota(jnp.int32, (BR, NB), 1)
    every = jnp.zeros((BR, NB), F32)
    for t in range(KX):
        every = jnp.where(lists[:, t : t + 1] == ids, 1.0, every)
    slot = slots_of(every)
    rows = lax.broadcasted_iota(jnp.int32, (BR, NB), 0).astype(F32) - BR
    for s in range(CAP):
        at = jnp.sum(jnp.where(slot == s, rows, 0.0), axis=0, keepdims=True) + BR
        places_ref[pl.ds(s, 1), :] = at.astype(jnp.int32)


def pack(base, list_x, tile):
    return pl.pallas_call(
        pack_kernel,
        out_shape=(
            jax.ShapeDtypeStruct((PAY, W), BF16),
            jax.ShapeDtypeStruct((TILES, CAP, B, W), BF16),
            jax.ShapeDtypeStruct((CAP, NB), jnp.int32),
        ),
        in_specs=[SMEM, HBM, HBM],
        out_specs=(VMEM,) * 3,
        scratch_shapes=[
            pltpu.VMEM((BR, KX), jnp.int32),
            pltpu.VMEM((ROWS, W), BF16),
            pltpu.SemaphoreType.DMA((2,)),
        ],
        compiler_params=params(48),
        cost_estimate=COST,
        name="pack",
    )(base, list_x, tile)


def right_kernel(table_ref, base_ref, *refs):
    lists_hbm, mine_hbm, other_hbm, right_ref, masks_ref = refs[:3], *refs[3:7]
    lists, pays_ref, sems = refs[7:10], refs[10], refs[11]
    rows = pl.ds(0, (CAP + 1) * B)
    pairs = list(zip(lists_hbm, lists))
    pairs += [(ref.at[:, rows], pays_ref.at[k]) for k, ref in enumerate((mine_hbm, other_hbm))]
    copies_in(pairs, sems)
    for k, (which, owner) in enumerate(((0, 0), (2, 0), (1, 0), (1, 1))):
        masks_ref[k] = lane_hits(lists[which][...], base_ref[owner])

    @pl.loop(0, 2 * TILES)
    def _(h):
        g, core = table_ref[2 * h], table_ref[2 * h + 1]
        first = pl.multiple_of(CAP * B + core * (BR // 2), BR // 2)
        for k in range(2):
            part = [pays_ref[k, g, pl.ds(s * B, B), :].astype(F32) for s in range(CAP)]
            slot = pays_ref[k, g, pl.ds(first, BR // 2), :].astype(F32).astype(jnp.int32)
            for t in range(BR // 2):
                row = jnp.broadcast_to(slot[t : t + 1, :], (B, W))
                value = jnp.zeros((B, W), F32)
                for s in range(CAP):
                    value = jnp.where(row == s, part[s], value)
                right_ref[h, pl.ds(t * B, B), pl.ds(k * W, W)] = value.astype(BF16)


def right(table, base, lists, mine, other):
    return pl.pallas_call(
        right_kernel,
        out_shape=(
            jax.ShapeDtypeStruct((2 * TILES, HALF, 2 * W), BF16),
            jax.ShapeDtypeStruct((4, BR, W), F32),
        ),
        in_specs=[SMEM, SMEM] + [HBM] * 5,
        out_specs=(VMEM, VMEM),
        scratch_shapes=[pltpu.VMEM(a.shape, jnp.int32) for a in lists]
        + [
            pltpu.VMEM((2, GROUPS, (CAP + 1) * B, W), BF16),
            pltpu.SemaphoreType.DMA((5,)),
        ],
        compiler_params=params(48),
        cost_estimate=COST,
        name="right",
    )(table, base, *lists, mine, other)


def unpack(packed_ref, start, places_ref, rows, wide):
    lane = lax.broadcasted_iota(jnp.int32, (B, W), 1) // B
    masks = [lane == c for c in range(W // B)]
    for q in range(TILES):
        rows[q, pl.ds(0, BR)] = jnp.zeros((BR, B, W), F32)
    for q in range(TILES):
        for s in range(CAP):
            block = packed_ref[q, s].astype(F32)
            for c in range(W // B):
                row = places_ref[s, start + q * (W // B) + c]
                pltpu.store(rows.at[q, row], block, mask=masks[c])
    for q in range(TILES):
        for i in range(BR):
            wide[pl.ds(i * B, B), pl.ds(q * W, W)] = rows[q, i].astype(BF16)


def half_start(table_ref, k):
    return (table_ref[2 * k] * 2 + table_ref[2 * k + 1]) * (HALF // B)


def widen(first, halves, table, places, dense=None):
    count = len(halves)

    def kernel(table_ref, places_ref, *refs):
        packed, refs = refs[:count], refs[count:]
        dense_ref, rows, wide, sems = refs if dense is None else refs[1:]
        puts = []
        for k in range(count):
            unpack(packed[k], half_start(table_ref, first + k), places_ref, rows, wide.at[k])
            put = pltpu.make_async_copy(wide.at[k], dense_ref.at[first + k], sems.at[k])
            put.start()
            puts.append(put)
        for put in puts:
            put.wait()

    operands, specs = [table, places, *halves], [SMEM, SMEM] + [VMEM] * count
    aliases = {}
    if dense is not None:
        aliases = {len(operands): 0}
        operands.append(dense)
        specs.append(HBM)
    return pl.pallas_call(
        kernel,
        out_shape=jax.ShapeDtypeStruct((FIRST, ROWS, HALF), BF16),
        in_specs=specs,
        out_specs=HBM,
        scratch_shapes=[
            pltpu.VMEM((TILES, BR + 1, B, W), F32),
            pltpu.VMEM((count, ROWS, HALF), BF16),
            pltpu.SemaphoreType.DMA((count,)),
        ],
        input_output_aliases=aliases,
        compiler_params=params(50),
        cost_estimate=COST,
        name="widen",
    )(*operands)


def product(halves, table, places, dense, right_side):
    count = FIRST + len(halves)

    def kernel(table_ref, places_ref, *refs):
        packed, refs = refs[: len(halves)], refs[len(halves) :]
        right_ref, dense_in, dense_ref, sum_ref, rows, wide, in_sems, out_sems = refs
        fetches = [
            pltpu.make_async_copy(dense_in.at[k], wide.at[k], in_sems.at[k]) for k in range(FIRST)
        ]
        for fetch in fetches:
            fetch.start()
        puts = []
        for k in range(len(halves)):
            at = FIRST + k
            unpack(packed[k], half_start(table_ref, at), places_ref, rows, wide.at[at])
            put = pltpu.make_async_copy(wide.at[at], dense_ref.at[k], out_sems.at[k])
            put.start()
            puts.append(put)
        for fetch in fetches:
            fetch.wait()

        @pl.loop(0, ROWS // STEP)
        def _(i):
            part = pl.ds(pl.multiple_of(i * STEP, STEP), STEP)
            total = jnp.dot(wide[0, part, :], right_ref[0], preferred_element_type=F32)
            for k in range(1, count):
                total += jnp.dot(wide[k, part, :], right_ref[k], preferred_element_type=F32)
            sum_ref[part, :] = total

        for put in puts:
            put.wait()

    return pl.pallas_call(
        kernel,
        out_shape=(
            jax.ShapeDtypeStruct((REST, ROWS, HALF), BF16),
            jax.ShapeDtypeStruct((ROWS, 2 * W), F32),
        ),
        in_specs=[SMEM, SMEM] + [VMEM] * (len(halves) + 1) + [HBM],
        out_specs=(HBM, VMEM),
        scratch_shapes=[
            pltpu.VMEM((TILES, BR + 1, B, W), F32),
            pltpu.VMEM((count, ROWS, HALF), BF16),
            pltpu.SemaphoreType.DMA((FIRST,)),
            pltpu.SemaphoreType.DMA((len(halves),)),
        ],
        compiler_params=params(50),
        cost_estimate=COST,
        name="product",
    )(table, places, *halves, right_side, dense)


STEP = 256


def close_kernel(
    table_ref, places_ref, packed_ref, right_ref, sum_ref, dense_in, dense_ref, out_ref, rows, wide, sem
):
    last = FIRST + REST - 1
    unpack(packed_ref, half_start(table_ref, last), places_ref, rows, wide)
    put = pltpu.make_async_copy(wide, dense_ref.at[REST - 1], sem)
    put.start()
    out_ref[...] = jnp.dot(wide[...], right_ref[last], preferred_element_type=F32) + sum_ref[...]
    put.wait()


def close(packed, table, places, right_side, total, dense):
    return pl.pallas_call(
        close_kernel,
        out_shape=(
            jax.ShapeDtypeStruct((REST, ROWS, HALF), BF16),
            jax.ShapeDtypeStruct((ROWS, 2 * W), F32),
        ),
        in_specs=[SMEM, SMEM, VMEM, VMEM, VMEM, HBM],
        out_specs=(HBM, VMEM),
        scratch_shapes=[
            pltpu.VMEM((TILES, BR + 1, B, W), F32),
            pltpu.VMEM((ROWS, HALF), BF16),
            pltpu.SemaphoreType.DMA,
        ],
        input_output_aliases={5: 0},
        compiler_params=params(50),
        cost_estimate=COST,
        name="close",
    )(table, places, packed, right_side, total, dense)


def finish_kernel(sum_ref, passed_ref, masks_ref, mine_ref, other_ref):
    scale = (NB / (KX * KX * B)) ** 0.5
    for i in range(BR):
        rows = pl.ds(i * B, B)
        for k, square_ref in enumerate((mine_ref, other_ref)):
            keep = jnp.broadcast_to(masks_ref[2 + k, i : i + 1, :], (B, W))
            value = sum_ref[rows, pl.ds(k * W, W)] + passed_ref[rows, pl.ds((1 - k) * W, W)]
            square_ref[rows, :] = jnp.where(keep > 0.0, value * scale, 0.0).astype(BF16)


def finish(total, passed, masks):
    return pl.pallas_call(
        finish_kernel,
        out_shape=(jax.ShapeDtypeStruct((ROWS, W), BF16),) * 2,
        in_specs=[VMEM] * 3,
        out_specs=(VMEM,) * 2,
        compiler_params=params(48),
        cost_estimate=COST,
        name="finish",
    )(total, passed, masks)


def cube_part(steps, table, lists, pieces, acc=None, last=None):
    scale = (NB / (KX * KSQ * B)) ** 0.5
    count = len(pieces)

    def kernel(table_ref, own_first, own_rest, other_first, other_rest, *refs):
        refs = list(refs)
        pieces_refs = [refs.pop(0) for _ in pieces]
        acc_ref = refs.pop(0) if acc is not None else None
        tile_ref, masks_ref = (refs.pop(0), refs.pop(0)) if last is not None else (None, None)
        out_ref, held, sems = refs
        y, row, core = (table_ref[4 * TILES + k] for k in range(3))
        apart = (y - row) * (1 - 2 * core)
        for h in range(2 * count):
            p, half = h // 2, h % 2
            d = jnp.bitwise_and(apart - steps[p], GROUPS - 1)
            same = core == half
            ours = jnp.logical_or(
                jnp.logical_and(same, d <= 4), jnp.logical_and(d > 0, d < 4)
            )
            d = jnp.where(d > 4, GROUPS - d, d)
            at = jnp.where(d == 0, 0, 2 * d - jnp.where(same == ours, 1, 0))
            early = at < FIRST
            held_half = held.at[p, :, pl.ds(half * HALF, HALF)]
            for mine in (True, False):
                here = ours if mine else jnp.logical_not(ours)
                begin, rest = (own_first, own_rest) if mine else (other_first, other_rest)

                @pl.when(jnp.logical_and(here, early))
                def _():
                    pltpu.make_async_copy(begin.at[at], held_half, sems.at[h]).start()

                @pl.when(jnp.logical_and(here, jnp.logical_not(early)))
                def _():
                    pltpu.make_async_copy(rest.at[at - FIRST], held_half, sems.at[h]).start()

        total = None if acc_ref is None else acc_ref[...]
        for p in range(count):
            for half in range(2):
                held_half = held.at[p, :, pl.ds(half * HALF, HALF)]
                pltpu.make_async_copy(own_first.at[0], held_half, sems.at[2 * p + half]).wait()
            term = jnp.dot(held[p], pieces_refs[p][...], preferred_element_type=F32)
            total = term if total is None else total + term
        if last is None:
            out_ref[...] = total
            return
        for k in range(BR):
            rows = pl.ds(k * B, B)
            keep_x = jnp.broadcast_to(masks_ref[0, k : k + 1, :], (B, W))
            keep_out = jnp.broadcast_to(masks_ref[1, k : k + 1, :], (B, W))
            sparse = jnp.where(keep_x > 0.0, tile_ref[rows, :].astype(F32), 0.0)
            cube = total[k * B : (k + 1) * B, :] * scale
            result = 1.5 * sparse - 0.5 * cube
            out_ref[rows, :] = jnp.where(keep_out > 0.0, result, 0.0).astype(BF16)

    operands = [table, *lists, *pieces]
    if acc is not None:
        operands.append(acc)
    if last is not None:
        operands += last
    return pl.pallas_call(
        kernel,
        out_shape=jax.ShapeDtypeStruct((ROWS, W), F32 if last is None else BF16),
        in_specs=[SMEM] + [HBM] * 4 + [VMEM] * (len(operands) - 5),
        out_specs=VMEM,
        scratch_shapes=[
            pltpu.VMEM((count, ROWS, 2 * HALF), BF16),
            pltpu.SemaphoreType.DMA((2 * count,)),
        ],
        compiler_params=params(50),
        cost_estimate=COST,
        name="cube_last" if last is not None else "cube_part",
    )(*operands)


def local(matrix, list_x, list_sq, list_out):
    layers = lax.axis_size("layer")
    col = lax.axis_index("col").astype(jnp.int32)
    row = lax.axis_index("row").astype(jnp.int32)
    layer = lax.axis_index("layer").astype(jnp.int32)
    y, core = col // 2, col % 2
    sign = 1 - 2 * core
    base = jnp.stack([(c * layers + layer) * (W // B) for c in (col, jnp.bitwise_xor(col, 1))])

    brought = [(0, 1), (1, 1), (1, 0), (2, 1), (2, 0), (3, 1), (3, 0), (4, 1)]
    table = []
    for d, same in brought:
        table += [jnp.bitwise_and(y - sign * d, GROUPS - 1), core if same else 1 - core]
    table = jnp.stack(table + [y, row, core])
    cols = 2 * GROUPS
    swap = [(c, c ^ 1) for c in range(cols)]
    turn_y = [(c, (c + (2 if c % 2 == 0 else -2)) % cols) for c in range(cols)]
    turn_z = [
        (r * cols + c, (r + (1 if c % 2 == 0 else -1)) % GROUPS * cols + c)
        for r in range(GROUPS)
        for c in range(cols)
    ]

    def along_y(piece):
        return lax.ppermute(piece, "col", turn_y)

    def along_z(piece):
        return lax.ppermute(piece, ("row", "col"), turn_z)

    def across(piece):
        return lax.ppermute(piece, "col", swap)

    def after(piece, *done):
        return lax.optimization_barrier((piece, *done))[0]

    pay, left, places = pack(base, list_x, matrix)
    pays = lax.all_gather(pay, "row", axis=0, tiled=False)
    a0 = lax.all_to_all(left, "layer", 0, 0, tiled=True)
    b0 = across(a0)
    a1, b1 = along_y(a0), along_y(b0)
    dense = widen(0, [a0], table, places)
    a2, b2 = along_y(after(a1, dense)), along_y(b1)
    dense = widen(1, [a1, b1], table, places, dense)
    a3, b3 = along_y(after(a2, dense)), along_y(b2)
    a4 = along_y(a3)
    dense = widen(3, [after(a2, a3), b2], table, places, dense)
    pays = after(pays, dense)
    right_side, masks = right(table, base, (list_x, list_sq, list_out), pays, across(pays))
    rest, total = product([a3, b3], table, places, dense, right_side)
    rest, total = close(a4, table, places, right_side, total, rest)
    c0, d0 = finish(total, across(total), masks)

    lists = (dense, rest, across(dense), across(after(rest, c0)))

    def cubed(distance, pieces, *more):
        steps = [distance] if len(pieces) == 1 else [-distance, distance]
        return cube_part(steps, table, lists, pieces, *more)

    c1, d1 = along_z(c0), along_z(d0)
    c2, d2 = along_z(c1), along_z(d1)
    c3, d3 = along_z(c2), along_z(d2)
    acc = cubed(0, [c0])
    acc = cubed(1, [c1, across(d1)], acc)
    c4 = along_z(after(c3, acc))
    acc = cubed(2, [c2, across(d2)], acc)
    acc = cubed(3, [c3, across(d3)], acc)
    return cubed(4, [c4], acc, (matrix, masks))


def solution(mesh):
    placed = (P("row", ("col", "layer")), P("row", None), P("row", None), P("row", None))
    return jax.shard_map(
        local, mesh=mesh, in_specs=placed, out_specs=P("row", ("col", "layer")), check_vma=False
    )
```

time: 170 us -> 170 us (level)
  the two profiles are of different devices: /device:TPU:32 before, /device:TPU:17 now
where the time goes in v4:
time: 170 us; the launch traced here: 169 us
  starting transfers between devices  79.2 us (47%)
  Pallas kernels  44.4 us (26%)
  waiting for transfers between devices  14.4 us (8%)
  between operations  13.9 us (8%)
  blocking collectives  9.98 us (6%)
  local copies, waits for them, and re-layouts  7.07 us (4%)
    ppermute x7, starting transfers between devices, along_z(): return lax.ppermute(piece, ('row', 'col'), turn_z)  32.2 us
    ppermute x8, starting transfers between devices, across(): return lax.ppermute(piece, 'col', swap)  24.3 us
    ppermute x7, starting transfers between devices, along_y(): return lax.ppermute(piece, 'col', turn_y)  22.7 us
    pallas_call x5, Pallas kernels, cube_part(): pl.pallas_call(kernel, out_shape=jax.ShapeDtypeStruct((ROWS, W), F32 if l...  20.3 us
    ppermute x7, waiting for transfers between devices, along_y(): return lax.ppermute(piece, 'col', turn_y)  10.5 us
    all_to_all x1, blocking collectives, local(): a0 = lax.all_to_all(left, 'layer', 0, 0, tiled=True)  9.98 us
    pallas_call x3, Pallas kernels, widen(): pl.pallas_call(kernel, out_shape=jax.ShapeDtypeStruct((FIRST, ROWS, HALF)...  8.03 us
    unnamed x22, local copies, waits for them, and re-layouts  6.97 us
  transfers between devices with their start and end apart: 23, of which 7 were waited for; matrix products, arithmetic and copies ran while one was open for 0% of the time, Pallas kernels for 23%

profile of v4, /device:TPU:17, one launch (start us, length us, event | category | flops | bytes accessed | tf_op | source)
XLA Modules:
  0.0 169.0 jit_solution(5865496738661556676)
XLA Ops:
  10.2 10.0 %all_to_all.5.refs_0_ = bf16[4,10,32,128]{3,2,1,0:T(8,128)(2,1)S(1)} all-to-all(bf16[4,10,32,128]{3,2,1,0:T(8,128)(2,1)S(1)} %get-tuple-element.23), channel_id=1, replica_groups=mesh['row'=8,'col'=16,'layer'=4] {'layer'}, dimensions={0} | all-to-all | bytes 655360 | tf_op jit(solution)/shard_map/all_to_all | solution.py:439
  22.3 5.5 %collective-permute-start.2 = (bf16[4,10,32,128]{3,2,1,0:T(8,128)(2,1)S(1)}, bf16[4,10,32,128]{3,2,1,0:T(8,128)(2,1)S(1)}, u32[]{:S(2)}, u32[]{:S(2)}) collective-permute-start(bf16[4,10,32,128]{3,2,1,0:T(8,128)(2,1)S(1)} %all_to_all.5.refs_0_), channel_id=1, source_target_pairs={{0,4},{4,0},{8,12},{12,8},{16,20},{20,16},{24,28},{28,24},{32,36},... | collective-permute-start | bytes 983048 | tf_op jit(solution)/shard_map/ppermute | solution.py:432
  32.4 3.8 %collective-permute-start.1 = (bf16[4,10,32,128]{3,2,1,0:T(8,128)(2,1)S(1)}, bf16[4,10,32,128]{3,2,1,0:T(8,128)(2,1)S(1)}, u32[]{:S(2)}, u32[]{:S(2)}) collective-permute-start(bf16[4,10,32,128]{3,2,1,0:T(8,128)(2,1)S(1)} %collective-permute-done.refs_0_), channel_id=1, source_target_pairs={{0,8},{4,60},{8,16},{12,4},{16,24},{20,12},{24,32},{28,20},{32,40}... | collective-permute-start | bytes 983048 | tf_op jit(solution)/shard_map/ppermute | solution.py:426
  36.2 3.2 %collective-permute-done.3.refs_1_ = bf16[4,10,32,128]{3,2,1,0:T(8,128)(2,1)S(1)} collective-permute-done((bf16[4,10,32,128]{3,2,1,0:T(8,128)(2,1)S(1)}, bf16[4,10,32,128]{3,2,1,0:T(8,128)(2,1)S(1)}, u32[]{:S(2)}, u32[]{:S(2)}) %collective-permute-start.3) | collective-permute-done | bytes 327712 | tf_op jit(solution)/shard_map/ppermute | solution.py:426
  39.4 2.9 %widen.4.refs_2_ = bf16[5,1024,512]{2,1,0:T(8,128)(2,1)} custom-call(s32[19]{0:T(128)S(1)} %stack.58.table_ref, s32[10,256]{1,0:T(8,128)S(1)} %get-tuple-element.22.places_ref, bf16[4,10,32,128]{3,2,1,0:T(8,128)(2,1)S(1)} %collective-permute-done.refs_0_, ...), custom_call_target="tpu_custom_call", output_to_operand_aliasing={{}: (4, {})} | custom-call | flops 1 | bytes 1 | tf_op jit(solution)/shard_map/widen/pallas_call | solution.py:202
  45.0 4.2 %collective-permute-start.5 = (bf16[4,10,32,128]{3,2,1,0:T(8,128)(2,1)S(1)}, bf16[4,10,32,128]{3,2,1,0:T(8,128)(2,1)S(1)}, u32[]{:S(2)}, u32[]{:S(2)}) collective-permute-start(bf16[4,10,32,128]{3,2,1,0:T(8,128)(2,1)S(1)} %collective-permute-done.3.refs_1_), channel_id=1, source_target_pairs={{0,8},{4,60},{8,16},{12,4},{16,24},{20,12},{24,32},{28,20},{32,40}... | collective-permute-start | bytes 983048 | tf_op jit(solution)/shard_map/ppermute | solution.py:426
  49.3 3.1 %collective-permute-done.4.refs_0_ = bf16[4,10,32,128]{3,2,1,0:T(8,128)(2,1)S(1)} collective-permute-done((bf16[4,10,32,128]{3,2,1,0:T(8,128)(2,1)S(1)}, bf16[4,10,32,128]{3,2,1,0:T(8,128)(2,1)S(1)}, u32[]{:S(2)}, u32[]{:S(2)}) %collective-permute-start.4) | collective-permute-done | bytes 327712 | tf_op jit(solution)/shard_map/ppermute | solution.py:426
  52.4 3.5 %collective-permute-done.5.refs_1_ = bf16[4,10,32,128]{3,2,1,0:T(8,128)(2,1)S(1)} collective-permute-done((bf16[4,10,32,128]{3,2,1,0:T(8,128)(2,1)S(1)}, bf16[4,10,32,128]{3,2,1,0:T(8,128)(2,1)S(1)}, u32[]{:S(2)}, u32[]{:S(2)}) %collective-permute-start.5) | collective-permute-done | bytes 327712 | tf_op jit(solution)/shard_map/ppermute | solution.py:426
  58.7 5.0 %collective-permute-start.7 = (bf16[8,576,128]{2,1,0:T(8,128)(2,1)}, bf16[8,576,128]{2,1,0:T(8,128)(2,1)S(1)}, u32[]{:S(2)}, u32[]{:S(2)}) collective-permute-start(bf16[8,576,128]{2,1,0:T(8,128)(2,1)} %bitcast.12), channel_id=1, source_target_pairs={{0,4},{4,0},{8,12},{12,8},{16,20},{20,16},{24,28},{28,24},{32,36},... | collective-permute-start | bytes 3538952 | tf_op jit(solution)/shard_map/ppermute | solution.py:432
  65.7 3.5 %collective-permute-start.8 = (bf16[4,10,32,128]{3,2,1,0:T(8,128)(2,1)S(1)}, bf16[4,10,32,128]{3,2,1,0:T(8,128)(2,1)S(1)}, u32[]{:S(2)}, u32[]{:S(2)}) collective-permute-start(bf16[4,10,32,128]{3,2,1,0:T(8,128)(2,1)S(1)} %collective-permute-done.5.refs_1_), channel_id=1, source_target_pairs={{0,8},{4,60},{8,16},{12,4},{16,24},{20,12},{24,32},{28,20},{32,40}... | collective-permute-start | bytes 983048 | tf_op jit(solution)/shard_map/ppermute | solution.py:426
  69.2 4.9 %collective-permute-start.6 = (bf16[4,10,32,128]{3,2,1,0:T(8,128)(2,1)S(1)}, bf16[4,10,32,128]{3,2,1,0:T(8,128)(2,1)S(1)}, u32[]{:S(2)}, u32[]{:S(2)}) collective-permute-start(bf16[4,10,32,128]{3,2,1,0:T(8,128)(2,1)S(1)} %collective-permute-done.4.refs_0_), channel_id=1, source_target_pairs={{0,8},{4,60},{8,16},{12,4},{16,24},{20,12},{24,32},{28,20},{32,40}... | collective-permute-start | bytes 983048 | tf_op jit(solution)/shard_map/ppermute | solution.py:426
  75.4 4.1 %right.1 = (bf16[8,512,256]{2,1,0:T(8,128)(2,1)S(1)}, f32[4,32,128]{2,1,0:T(8,128)S(1)}) custom-call(s32[19]{0:T(128)S(1)} %stack.58.table_ref, s32[2]{0:T(128)S(1)} %pad_add_fusion.base_ref, s32[32,40]{1,0:T(8,128)S(1)} %copy-done.6, s32[32,60]{1,0:T(8,128)S(1)} %copy-done.7, s32[32,40]{1,0:T(8,128)S(1)} %copy-done.8, bf16[8,576,128]{2,1,0:T(8,128)(2,1)S(1)} %bitcast.13, ...), custom_call_target="tpu_custom_call" | custom-call | flops 1 | bytes 1 | tf_op jit(solution)/shard_map/right/pallas_call | solution.py:142
  79.5 6.7 %product.1 = (bf16[3,1024,512]{2,1,0:T(8,128)(2,1)}, f32[1024,256]{1,0:T(8,128)S(1)}) custom-call(s32[19]{0:T(128)S(1)} %stack.58.table_ref, s32[10,256]{1,0:T(8,128)S(1)} %get-tuple-element.22.places_ref, bf16[4,10,32,128]{3,2,1,0:T(8,128)(2,1)S(1)} %collective-permute-done.4.refs_0_, bf16[4,10,32,128]{3,2,1,0:T(8,128)(2,1)S(1)} %collective-permute-done.8.refs_1_, ...), custom_call_target="tpu_custom_call" | custom-call | flops 1 | bytes 1 | tf_op jit(solution)/shard_map/product/pallas_call | solution.py:251
  86.2 3.2 %close.1 = (bf16[3,1024,512]{2,1,0:T(8,128)(2,1)}, f32[1024,256]{1,0:T(8,128)S(1)}) custom-call(s32[19]{0:T(128)S(1)} %stack.58.table_ref, s32[10,256]{1,0:T(8,128)S(1)} %get-tuple-element.22.places_ref, bf16[4,10,32,128]{3,2,1,0:T(8,128)(2,1)S(1)} %collective-permute-done.6.packed_ref, ...), custom_call_target="tpu_custom_call", output_to_operand_aliasing={{0}: (5, {})} | custom-call | flops 1 | bytes 1 | tf_op jit(solution)/shard_map/close/pallas_call | solution.py:286
  89.4 3.1 %collective-permute-start.10 = (f32[1024,256]{1,0:T(8,128)S(1)}, f32[1024,256]{1,0:T(8,128)S(1)}, u32[]{:S(2)}, u32[]{:S(2)}) collective-permute-start(f32[1024,256]{1,0:T(8,128)S(1)} %get-tuple-element.33.sum_ref), channel_id=1, source_target_pairs={{0,4},{4,0},{8,12},{12,8},{16,20},{20,16},{24,28},{28,24},{32,36},... | collective-permute-start | bytes 3145736 | tf_op jit(solution)/shard_map/ppermute | solution.py:432
  97.3 10.7 %collective-permute-start.15 = (bf16[1024,128]{1,0:T(8,128)(2,1)S(1)}, bf16[1024,128]{1,0:T(8,128)(2,1)S(1)}, u32[]{:S(2)}, u32[]{:S(2)}) collective-permute-start(bf16[1024,128]{1,0:T(8,128)(2,1)S(1)} %get-tuple-element.37), channel_id=1, source_target_pairs={{0,64},{4,452},{8,72},{12,460},{16,80},{20,468},{24,88},{28,476},{... | collective-permute-start | bytes 786440 | tf_op jit(solution)/shard_map/ppermute | solution.py:429
  111.2 5.0 %collective-permute-start.18 = (bf16[1024,128]{1,0:T(8,128)(2,1)S(1)}, bf16[1024,128]{1,0:T(8,128)(2,1)S(1)}, u32[]{:S(2)}, u32[]{:S(2)}) collective-permute-start(bf16[1024,128]{1,0:T(8,128)(2,1)S(1)} %collective-permute-done.15), channel_id=1, source_target_pairs={{0,64},{4,452},{8,72},{12,460},{16,80},{20,468},{24,88},{28,476},{... | collective-permute-start | bytes 786440 | tf_op jit(solution)/shard_map/ppermute | solution.py:429
  119.6 5.0 %collective-permute-start.19 = (bf16[1024,128]{1,0:T(8,128)(2,1)S(1)}, bf16[1024,128]{1,0:T(8,128)(2,1)S(1)}, u32[]{:S(2)}, u32[]{:S(2)}) collective-permute-start(bf16[1024,128]{1,0:T(8,128)(2,1)S(1)} %collective-permute-done.18), channel_id=1, source_target_pairs={{0,64},{4,452},{8,72},{12,460},{16,80},{20,468},{24,88},{28,476},{... | collective-permute-start | bytes 786440 | tf_op jit(solution)/shard_map/ppermute | solution.py:429
  126.5 4.3 %collective-permute-start.14 = (bf16[1024,128]{1,0:T(8,128)(2,1)S(1)}, bf16[1024,128]{1,0:T(8,128)(2,1)S(1)}, u32[]{:S(2)}, u32[]{:S(2)}) collective-permute-start(bf16[1024,128]{1,0:T(8,128)(2,1)S(1)} %collective-permute-done.13.refs_0_), channel_id=1, source_target_pairs={{0,64},{4,452},{8,72},{12,460},{16,80},{20,468},{24,88},{28,476},{... | collective-permute-start | bytes 786440 | tf_op jit(solution)/shard_map/ppermute | solution.py:429
  139.5 2.9 %cube_part.4.refs_2_ = f32[1024,128]{1,0:T(8,128)S(1)} custom-call(s32[19]{0:T(128)S(1)} %stack.58.table_ref, bf16[5,1024,512]{2,1,0:T(8,128)(2,1)} %widen.5.refs_3_.own_first, bf16[3,1024,512]{2,1,0:T(8,128)(2,1)S(1)} %copy-done, bf16[5,1024,512]{2,1,0:T(8,128)(2,1)} %copy-done.9, bf16[3,1024,512]{2,1,0:T(8,128)(2,1)} %copy-done.10, ...), custom_call_target="tpu_custom_call" | custom-call | flops 1 | bytes 1 | tf_op jit(solution)/shard_map/cube_part/pallas_call | solution.py:387
  142.4 4.6 %cube_part.5.refs_2_ = f32[1024,128]{1,0:T(8,128)S(1)} custom-call(s32[19]{0:T(128)S(1)} %stack.58.table_ref, bf16[5,1024,512]{2,1,0:T(8,128)(2,1)} %widen.5.refs_3_.own_first, bf16[3,1024,512]{2,1,0:T(8,128)(2,1)} %get-tuple-element.36.own_rest, bf16[5,1024,512]{2,1,0:T(8,128)(2,1)} %copy-done.9, bf16[3,1024,512]{2,1,0:T(8,128)(2,1)} %copy-done.10, ...), custom_call_target="tpu_custom_call" | custom-call | flops 1 | bytes 1 | tf_op jit(solution)/shard_map/cube_part/pallas_call | solution.py:387
  149.2 4.6 %cube_part.6.refs_2_ = f32[1024,128]{1,0:T(8,128)S(1)} custom-call(s32[19]{0:T(128)S(1)} %stack.58.table_ref, bf16[5,1024,512]{2,1,0:T(8,128)(2,1)} %widen.5.refs_3_.own_first, bf16[3,1024,512]{2,1,0:T(8,128)(2,1)} %get-tuple-element.36.own_rest, bf16[5,1024,512]{2,1,0:T(8,128)(2,1)} %copy-done.9, bf16[3,1024,512]{2,1,0:T(8,128)(2,1)} %copy-done.10, ...), custom_call_target="tpu_custom_call" | custom-call | flops 1 | bytes 1 | tf_op jit(solution)/shard_map/cube_part/pallas_call | solution.py:387
  153.9 4.6 %cube_part.7.refs_1_ = f32[1024,128]{1,0:T(8,128)S(1)} custom-call(s32[19]{0:T(128)S(1)} %stack.58.table_ref, bf16[5,1024,512]{2,1,0:T(8,128)(2,1)} %widen.5.refs_3_.own_first, bf16[3,1024,512]{2,1,0:T(8,128)(2,1)} %get-tuple-element.36.own_rest, bf16[5,1024,512]{2,1,0:T(8,128)(2,1)} %copy-done.9, bf16[3,1024,512]{2,1,0:T(8,128)(2,1)} %copy-done.10, ...), custom_call_target="tpu_custom_call" | custom-call | flops 1 | bytes 1 | tf_op jit(solution)/shard_map/cube_part/pallas_call | solution.py:387
  158.5 3.6 %cube_last.1 = bf16[1024,128]{1,0:T(8,128)(2,1)} custom-call(s32[19]{0:T(128)S(1)} %stack.58.table_ref, bf16[5,1024,512]{2,1,0:T(8,128)(2,1)} %widen.5.refs_3_.own_first, bf16[3,1024,512]{2,1,0:T(8,128)(2,1)} %get-tuple-element.36.own_rest, bf16[5,1024,512]{2,1,0:T(8,128)(2,1)} %copy-done.9, bf16[3,1024,512]{2,1,0:T(8,128)(2,1)} %copy-done.10, ...), custom_call_target="tpu_custom_call" | custom-call | flops 1 | bytes 1 | tf_op jit(solution)/shard_map/cube_last/pallas_call | solution.py:387
  (61 shorter events, 43.0 us)
Async XLA Ops:
  6.5 52.2 %all-gather.3.cloned.1.call-start = ((), (), s32[]{:S(2)}) async-start(), calls=%async_computation.1 | async-start | bytes 1327104 | tf_op jit(solution)/shard_map/all_gather | solution.py:438
  20.2 10.0 %collective-permute-start = (bf16[4,10,32,128]{3,2,1,0:T(8,128)(2,1)S(1)}, bf16[4,10,32,128]{3,2,1,0:T(8,128)(2,1)S(1)}, u32[]{:S(2)}, u32[]{:S(2)}) collective-permute-start(bf16[4,10,32,128]{3,2,1,0:T(8,128)(2,1)S(1)} %all_to_all.5.refs_0_), channel_id=1, source_target_pairs={{0,8},{4,60},{8,16},{12,4},{16,24},{20,12},{24,32},{28,20},{32,40}... | collective-permute-start | bytes 983048 | tf_op jit(solution)/shard_map/ppermute | solution.py:426
  22.3 8.0 %collective-permute-start.2 = (bf16[4,10,32,128]{3,2,1,0:T(8,128)(2,1)S(1)}, bf16[4,10,32,128]{3,2,1,0:T(8,128)(2,1)S(1)}, u32[]{:S(2)}, u32[]{:S(2)}) collective-permute-start(bf16[4,10,32,128]{3,2,1,0:T(8,128)(2,1)S(1)} %all_to_all.5.refs_0_), channel_id=1, source_target_pairs={{0,4},{4,0},{8,12},{12,8},{16,20},{20,16},{24,28},{28,24},{32,36},... | collective-permute-start | bytes 983048 | tf_op jit(solution)/shard_map/ppermute | solution.py:432
  30.3 9.2 %collective-permute-start.3 = (bf16[4,10,32,128]{3,2,1,0:T(8,128)(2,1)S(1)}, bf16[4,10,32,128]{3,2,1,0:T(8,128)(2,1)S(1)}, u32[]{:S(2)}, u32[]{:S(2)}) collective-permute-start(bf16[4,10,32,128]{3,2,1,0:T(8,128)(2,1)S(1)} %collective-permute-done.2), channel_id=1, source_target_pairs={{0,8},{4,60},{8,16},{12,4},{16,24},{20,12},{24,32},{28,20},{32,40}... | collective-permute-start | bytes 983048 | tf_op jit(solution)/shard_map/ppermute | solution.py:426
  32.4 10.6 %collective-permute-start.1 = (bf16[4,10,32,128]{3,2,1,0:T(8,128)(2,1)S(1)}, bf16[4,10,32,128]{3,2,1,0:T(8,128)(2,1)S(1)}, u32[]{:S(2)}, u32[]{:S(2)}) collective-permute-start(bf16[4,10,32,128]{3,2,1,0:T(8,128)(2,1)S(1)} %collective-permute-done.refs_0_), channel_id=1, source_target_pairs={{0,8},{4,60},{8,16},{12,4},{16,24},{20,12},{24,32},{28,20},{32,40}... | collective-permute-start | bytes 983048 | tf_op jit(solution)/shard_map/ppermute | solution.py:426
  42.3 31.8 %copy-start.6 = (s32[32,40]{1,0:T(8,128)S(1)}, s32[32,40]{1,0:T(8,128)}, u32[]{:S(2)}) copy-start(s32[32,40]{1,0:T(8,128)} %refs_0_.1) | copy-start | bytes 15364
  43.0 9.4 %collective-permute-start.4 = (bf16[4,10,32,128]{3,2,1,0:T(8,128)(2,1)S(1)}, bf16[4,10,32,128]{3,2,1,0:T(8,128)(2,1)S(1)}, u32[]{:S(2)}, u32[]{:S(2)}) collective-permute-start(bf16[4,10,32,128]{3,2,1,0:T(8,128)(2,1)S(1)} %collective-permute-done.1.refs_0_), channel_id=1, source_target_pairs={{0,8},{4,60},{8,16},{12,4},{16,24},{20,12},{24,32},{28,20},{32,40}... | collective-permute-start | bytes 983048 | tf_op jit(solution)/shard_map/ppermute | solution.py:426
  45.0 10.8 %collective-permute-start.5 = (bf16[4,10,32,128]{3,2,1,0:T(8,128)(2,1)S(1)}, bf16[4,10,32,128]{3,2,1,0:T(8,128)(2,1)S(1)}, u32[]{:S(2)}, u32[]{:S(2)}) collective-permute-start(bf16[4,10,32,128]{3,2,1,0:T(8,128)(2,1)S(1)} %collective-permute-done.3.refs_1_), channel_id=1, source_target_pairs={{0,8},{4,60},{8,16},{12,4},{16,24},{20,12},{24,32},{28,20},{32,40}... | collective-permute-start | bytes 983048 | tf_op jit(solution)/shard_map/ppermute | solution.py:426
  58.7 15.4 %collective-permute-start.7 = (bf16[8,576,128]{2,1,0:T(8,128)(2,1)}, bf16[8,576,128]{2,1,0:T(8,128)(2,1)S(1)}, u32[]{:S(2)}, u32[]{:S(2)}) collective-permute-start(bf16[8,576,128]{2,1,0:T(8,128)(2,1)} %bitcast.12), channel_id=1, source_target_pairs={{0,4},{4,0},{8,12},{12,8},{16,20},{20,16},{24,28},{28,24},{32,36},... | collective-permute-start | bytes 3538952 | tf_op jit(solution)/shard_map/ppermute | solution.py:432
  63.8 69.8 %collective-permute-start.9 = (bf16[5,1024,512]{2,1,0:T(8,128)(2,1)}, bf16[5,1024,512]{2,1,0:T(8,128)(2,1)S(1)}, u32[]{:S(2)}, u32[]{:S(2)}) collective-permute-start(bf16[5,1024,512]{2,1,0:T(8,128)(2,1)} %widen.5.refs_3_.own_first), channel_id=1, source_target_pairs={{0,4},{4,0},{8,12},{12,8},{16,20},{20,16},{24,28},{28,24},{32,36},... | collective-permute-start | bytes 15728648 | tf_op jit(solution)/shard_map/ppermute | solution.py:432
  65.7 13.8 %collective-permute-start.8 = (bf16[4,10,32,128]{3,2,1,0:T(8,128)(2,1)S(1)}, bf16[4,10,32,128]{3,2,1,0:T(8,128)(2,1)S(1)}, u32[]{:S(2)}, u32[]{:S(2)}) collective-permute-start(bf16[4,10,32,128]{3,2,1,0:T(8,128)(2,1)S(1)} %collective-permute-done.5.refs_1_), channel_id=1, source_target_pairs={{0,8},{4,60},{8,16},{12,4},{16,24},{20,12},{24,32},{28,20},{32,40}... | collective-permute-start | bytes 983048 | tf_op jit(solution)/shard_map/ppermute | solution.py:426
  69.2 17.0 %collective-permute-start.6 = (bf16[4,10,32,128]{3,2,1,0:T(8,128)(2,1)S(1)}, bf16[4,10,32,128]{3,2,1,0:T(8,128)(2,1)S(1)}, u32[]{:S(2)}, u32[]{:S(2)}) collective-permute-start(bf16[4,10,32,128]{3,2,1,0:T(8,128)(2,1)S(1)} %collective-permute-done.4.refs_0_), channel_id=1, source_target_pairs={{0,8},{4,60},{8,16},{12,4},{16,24},{20,12},{24,32},{28,20},{32,40}... | collective-permute-start | bytes 983048 | tf_op jit(solution)/shard_map/ppermute | solution.py:426
  89.4 5.4 %collective-permute-start.10 = (f32[1024,256]{1,0:T(8,128)S(1)}, f32[1024,256]{1,0:T(8,128)S(1)}, u32[]{:S(2)}, u32[]{:S(2)}) collective-permute-start(f32[1024,256]{1,0:T(8,128)S(1)} %get-tuple-element.33.sum_ref), channel_id=1, source_target_pairs={{0,4},{4,0},{8,12},{12,8},{16,20},{20,16},{24,28},{28,24},{32,36},... | collective-permute-start | bytes 3145736 | tf_op jit(solution)/shard_map/ppermute | solution.py:432
  95.0 40.9 %collective-permute-start.11 = (bf16[3,1024,512]{2,1,0:T(8,128)(2,1)}, bf16[3,1024,512]{2,1,0:T(8,128)(2,1)S(1)}, u32[]{:S(2)}, u32[]{:S(2)}) collective-permute-start(bf16[3,1024,512]{2,1,0:T(8,128)(2,1)} %get-tuple-element.36.own_rest), channel_id=1, source_target_pairs={{0,4},{4,0},{8,12},{12,8},{16,20},{20,16},{24,28},{28,24},{32,36},... | collective-permute-start | bytes 9437192 | tf_op jit(solution)/shard_map/ppermute | solution.py:432
  97.3 14.0 %collective-permute-start.15 = (bf16[1024,128]{1,0:T(8,128)(2,1)S(1)}, bf16[1024,128]{1,0:T(8,128)(2,1)S(1)}, u32[]{:S(2)}, u32[]{:S(2)}) collective-permute-start(bf16[1024,128]{1,0:T(8,128)(2,1)S(1)} %get-tuple-element.37), channel_id=1, source_target_pairs={{0,64},{4,452},{8,72},{12,460},{16,80},{20,468},{24,88},{28,476},{... | collective-permute-start | bytes 786440 | tf_op jit(solution)/shard_map/ppermute | solution.py:429
  108.0 8.3 %collective-permute-start.12 = (bf16[1024,128]{1,0:T(8,128)(2,1)S(1)}, bf16[1024,128]{1,0:T(8,128)(2,1)S(1)}, u32[]{:S(2)}, u32[]{:S(2)}) collective-permute-start(bf16[1024,128]{1,0:T(8,128)(2,1)S(1)} %get-tuple-element.35.refs_0_), channel_id=1, source_target_pairs={{0,64},{4,452},{8,72},{12,460},{16,80},{20,468},{24,88},{28,476},{... | collective-permute-start | bytes 786440 | tf_op jit(solution)/shard_map/ppermute | solution.py:429
  111.2 8.3 %collective-permute-start.18 = (bf16[1024,128]{1,0:T(8,128)(2,1)S(1)}, bf16[1024,128]{1,0:T(8,128)(2,1)S(1)}, u32[]{:S(2)}, u32[]{:S(2)}) collective-permute-start(bf16[1024,128]{1,0:T(8,128)(2,1)S(1)} %collective-permute-done.15), channel_id=1, source_target_pairs={{0,64},{4,452},{8,72},{12,460},{16,80},{20,468},{24,88},{28,476},{... | collective-permute-start | bytes 786440 | tf_op jit(solution)/shard_map/ppermute | solution.py:429
  116.3 10.2 %collective-permute-start.13 = (bf16[1024,128]{1,0:T(8,128)(2,1)S(1)}, bf16[1024,128]{1,0:T(8,128)(2,1)S(1)}, u32[]{:S(2)}, u32[]{:S(2)}) collective-permute-start(bf16[1024,128]{1,0:T(8,128)(2,1)S(1)} %collective-permute-done.12.refs_0_), channel_id=1, source_target_pairs={{0,64},{4,452},{8,72},{12,460},{16,80},{20,468},{24,88},{28,476},{... | collective-permute-start | bytes 786440 | tf_op jit(solution)/shard_map/ppermute | solution.py:429
  119.6 11.3 %collective-permute-start.19 = (bf16[1024,128]{1,0:T(8,128)(2,1)S(1)}, bf16[1024,128]{1,0:T(8,128)(2,1)S(1)}, u32[]{:S(2)}, u32[]{:S(2)}) collective-permute-start(bf16[1024,128]{1,0:T(8,128)(2,1)S(1)} %collective-permute-done.18), channel_id=1, source_target_pairs={{0,64},{4,452},{8,72},{12,460},{16,80},{20,468},{24,88},{28,476},{... | collective-permute-start | bytes 786440 | tf_op jit(solution)/shard_map/ppermute | solution.py:429
  124.6 17.8 %collective-permute-start.16 = (bf16[1024,128]{1,0:T(8,128)(2,1)S(1)}, bf16[1024,128]{1,0:T(8,128)(2,1)S(1)}, u32[]{:S(2)}, u32[]{:S(2)}) collective-permute-start(bf16[1024,128]{1,0:T(8,128)(2,1)S(1)} %collective-permute-done.15), channel_id=1, source_target_pairs={{0,4},{4,0},{8,12},{12,8},{16,20},{20,16},{24,28},{28,24},{32,36},... | collective-permute-start | bytes 786440 | tf_op jit(solution)/shard_map/ppermute | solution.py:432
  126.5 20.5 %collective-permute-start.14 = (bf16[1024,128]{1,0:T(8,128)(2,1)S(1)}, bf16[1024,128]{1,0:T(8,128)(2,1)S(1)}, u32[]{:S(2)}, u32[]{:S(2)}) collective-permute-start(bf16[1024,128]{1,0:T(8,128)(2,1)S(1)} %collective-permute-done.13.refs_0_), channel_id=1, source_target_pairs={{0,64},{4,452},{8,72},{12,460},{16,80},{20,468},{24,88},{28,476},{... | collective-permute-start | bytes 786440 | tf_op jit(solution)/shard_map/ppermute | solution.py:429
  130.9 18.3 %collective-permute-start.21 = (bf16[1024,128]{1,0:T(8,128)(2,1)S(1)}, bf16[1024,128]{1,0:T(8,128)(2,1)S(1)}, u32[]{:S(2)}, u32[]{:S(2)}) collective-permute-start(bf16[1024,128]{1,0:T(8,128)(2,1)S(1)} %collective-permute-done.18), channel_id=1, source_target_pairs={{0,4},{4,0},{8,12},{12,8},{16,20},{20,16},{24,28},{28,24},{32,36},... | collective-permute-start | bytes 786440 | tf_op jit(solution)/shard_map/ppermute | solution.py:432
  133.6 20.3 %collective-permute-start.20 = (bf16[1024,128]{1,0:T(8,128)(2,1)S(1)}, bf16[1024,128]{1,0:T(8,128)(2,1)S(1)}, u32[]{:S(2)}, u32[]{:S(2)}) collective-permute-start(bf16[1024,128]{1,0:T(8,128)(2,1)S(1)} %collective-permute-done.19), channel_id=1, source_target_pairs={{0,4},{4,0},{8,12},{12,8},{16,20},{20,16},{24,28},{28,24},{32,36},... | collective-permute-start | bytes 786440 | tf_op jit(solution)/shard_map/ppermute | solution.py:432
  147.0 11.5 %collective-permute-start.17 = (bf16[1024,128]{1,0:T(8,128)(2,1)S(1)}, bf16[1024,128]{1,0:T(8,128)(2,1)S(1)}, u32[]{:S(2)}, u32[]{:S(2)}) collective-permute-start(bf16[1024,128]{1,0:T(8,128)(2,1)S(1)} %collective-permute-done.14.refs_0_), channel_id=1, source_target_pairs={{0,64},{4,452},{8,72},{12,460},{16,80},{20,468},{24,88},{28,476},{... | collective-permute-start | bytes 786440 | tf_op jit(solution)/shard_map/ppermute | solution.py:429
  (10 other events, 83.8 us)
Sparse Core Ops, SparseCore 0:
  10.4 42.8 all-gather.2

commit v5 on v3

v5 whole, which is shorter than its diff:
```python
import jax
import jax.numpy as jnp
from jax import lax
from jax.experimental import pallas as pl
from jax.experimental.pallas import tpu as pltpu
from jax.sharding import PartitionSpec as P

B = 32
NB = 256
KX = 40
KSQ = 60
CAP = 10
ROWS = 1024
W = 128
BR = ROWS // B
GROUPS = 8
TILES = 4
HALF = TILES * W
PAY = 576
FIRST = 2 * TILES - 1
F32 = jnp.float32
BF16 = jnp.bfloat16
MIB = 1 << 20
SMEM = pl.BlockSpec(memory_space=pltpu.SMEM)
VMEM = pl.BlockSpec(memory_space=pltpu.VMEM)
HBM = pl.BlockSpec(memory_space=pltpu.HBM)


def params(limit):
    return pltpu.CompilerParams(vmem_limit_bytes=limit * MIB)


def cost(flops, size):
    return pl.CostEstimate(flops=flops, bytes_accessed=size, transcendentals=0)


def copies_in(pairs, sems):
    copies = [pltpu.make_async_copy(a, b, sems.at[k]) for k, (a, b) in enumerate(pairs)]
    for copy in copies:
        copy.start()
    for copy in copies:
        copy.wait()


def lane_hits(lists, base):
    ids = base + lax.broadcasted_iota(jnp.int32, (BR, W), 1) // B
    hit = jnp.zeros((BR, W), F32)
    for t in range(lists.shape[1]):
        hit = jnp.where(lists[:, t : t + 1] == ids, 1.0, hit)
    return hit


def slots_of(hit):
    below = lax.broadcasted_iota(jnp.int32, (BR, BR), 1) < lax.broadcasted_iota(
        jnp.int32, (BR, BR), 0
    )
    rank = jnp.dot(
        jnp.where(below, 1.0, 0.0).astype(BF16), hit.astype(BF16), preferred_element_type=F32
    )
    return jnp.where(hit > 0.0, rank, float(CAP))


def pack_kernel(base_ref, list_hbm, tile_hbm, pay_ref, left_ref, places_ref, list_ref, tile_ref, sems):
    copies_in([(list_hbm, list_ref), (tile_hbm, tile_ref)], sems)
    lists = list_ref[...]
    hit = lane_hits(lists, base_ref[0])
    slot = slots_of(hit)
    slot_int = slot.astype(jnp.int32)
    packed = [jnp.zeros((B, W), F32) for _ in range(CAP)]
    for i in range(BR):
        block = tile_ref[pl.ds(i * B, B), :].astype(F32)
        row = jnp.broadcast_to(slot_int[i : i + 1, :], (B, W))
        for s in range(min(i + 1, CAP)):
            packed[s] = jnp.where(row == s, block, packed[s])
    for s in range(CAP):
        value = packed[s].astype(BF16)
        pay_ref[pl.ds(s * B, B), :] = value
        for x in range(TILES):
            left_ref[x, s] = value
    pay_ref[pl.ds(CAP * B, B), :] = slot.astype(BF16)
    pay_ref[pl.ds((CAP + 1) * B, PAY - (CAP + 1) * B), :] = jnp.zeros(
        (PAY - (CAP + 1) * B, W), BF16
    )

    ids = lax.broadcasted_iota(jnp.int32, (BR, NB), 1)
    every = jnp.zeros((BR, NB), F32)
    for t in range(KX):
        every = jnp.where(lists[:, t : t + 1] == ids, 1.0, every)
    slot = slots_of(every)
    rows = lax.broadcasted_iota(jnp.int32, (BR, NB), 0).astype(F32) - BR
    for s in range(CAP):
        at = jnp.sum(jnp.where(slot == s, rows, 0.0), axis=0, keepdims=True) + BR
        places_ref[pl.ds(s, 1), :] = at.astype(jnp.int32)


def pack(base, list_x, tile):
    return pl.pallas_call(
        pack_kernel,
        out_shape=(
            jax.ShapeDtypeStruct((PAY, W), BF16),
            jax.ShapeDtypeStruct((TILES, CAP, B, W), BF16),
            jax.ShapeDtypeStruct((CAP, NB), jnp.int32),
        ),
        in_specs=[SMEM, HBM, HBM],
        out_specs=(VMEM,) * 3,
        scratch_shapes=[
            pltpu.VMEM((BR, KX), jnp.int32),
            pltpu.VMEM((ROWS, W), BF16),
            pltpu.SemaphoreType.DMA((2,)),
        ],
        compiler_params=params(48),
        cost_estimate=cost(10_000_000, 500_000),
        name="pack",
    )(base, list_x, tile)


def right_kernel(table_ref, base_ref, *refs):
    lists_hbm, mine_hbm, other_hbm, right_ref, masks_ref = refs[:3], *refs[3:7]
    lists, pays_ref, sems = refs[7:10], refs[10], refs[11]
    rows = pl.ds(0, (CAP + 1) * B)
    pairs = list(zip(lists_hbm, lists))
    pairs += [(ref.at[:, rows], pays_ref.at[k]) for k, ref in enumerate((mine_hbm, other_hbm))]
    copies_in(pairs, sems)
    for k in range(3):
        masks_ref[k] = lane_hits(lists[k][...], base_ref[0])

    @pl.loop(0, 2 * TILES)
    def _(h):
        g, core = table_ref[2 * h], table_ref[2 * h + 1]
        first = pl.multiple_of(CAP * B + core * (BR // 2), BR // 2)
        for k in range(2):
            part = [pays_ref[k, g, pl.ds(s * B, B), :].astype(F32) for s in range(CAP)]
            slot = pays_ref[k, g, pl.ds(first, BR // 2), :].astype(F32).astype(jnp.int32)
            for t in range(BR // 2):
                row = jnp.broadcast_to(slot[t : t + 1, :], (B, W))
                value = jnp.zeros((B, W), F32)
                for s in range(CAP):
                    value = jnp.where(row == s, part[s], value)
                right_ref[h, pl.ds(t * B, B), pl.ds(k * W, W)] = value.astype(BF16)


def right(table, base, lists, mine, other):
    return pl.pallas_call(
        right_kernel,
        out_shape=(
            jax.ShapeDtypeStruct((2 * TILES, HALF, 2 * W), BF16),
            jax.ShapeDtypeStruct((3, BR, W), F32),
        ),
        in_specs=[SMEM, SMEM] + [HBM] * 5,
        out_specs=(VMEM, VMEM),
        scratch_shapes=[pltpu.VMEM(a.shape, jnp.int32) for a in lists]
        + [
            pltpu.VMEM((2, GROUPS, (CAP + 1) * B, W), BF16),
            pltpu.SemaphoreType.DMA((5,)),
        ],
        compiler_params=params(48),
        cost_estimate=cost(40_000_000, 4 * MIB),
        name="right",
    )(table, base, *lists, mine, other)


def unpack(packed_ref, start, places_ref, rows, wide):
    lane = lax.broadcasted_iota(jnp.int32, (B, W), 1) // B
    masks = [lane == c for c in range(W // B)]
    for q in range(TILES):
        rows[q, pl.ds(0, BR)] = jnp.zeros((BR, B, W), F32)
    for q in range(TILES):
        for s in range(CAP):
            block = packed_ref[q, s].astype(F32)
            for c in range(W // B):
                row = places_ref[s, start + q * (W // B) + c]
                pltpu.store(rows.at[q, row], block, mask=masks[c])
    for q in range(TILES):
        for i in range(BR):
            wide[pl.ds(i * B, B), pl.ds(q * W, W)] = rows[q, i].astype(BF16)


def half_start(table_ref, k):
    return (table_ref[2 * k] * 2 + table_ref[2 * k + 1]) * (HALF // B)


def widen(first, halves, table, places):
    count = len(halves)

    def kernel(table_ref, places_ref, *refs):
        dense_ref, rows = refs[count:]
        for k in range(count):
            unpack(refs[k], half_start(table_ref, first + k), places_ref, rows, dense_ref.at[k])

    return pl.pallas_call(
        kernel,
        out_shape=jax.ShapeDtypeStruct((count, ROWS, HALF), BF16),
        in_specs=[SMEM, SMEM] + [VMEM] * count,
        out_specs=VMEM,
        scratch_shapes=[pltpu.VMEM((TILES, BR + 1, B, W), F32)],
        compiler_params=params(24),
        cost_estimate=cost(4 * ROWS * HALF * W * count, count * 3 * MIB),
        name="widen",
    )(table, places, *halves)


def product(halves, table, places, lists, right_side):
    count = len(halves)
    sizes = [array.shape[0] for array in lists] + [count]
    first = sum(sizes) - count

    def kernel(table_ref, places_ref, *refs):
        packed, refs = refs[:count], refs[count:]
        right_ref, parts, sum_ref, rows = refs[0], refs[1:-2], refs[-2], refs[-1]
        for k in range(count):
            unpack(packed[k], half_start(table_ref, first + k), places_ref, rows, parts[-1].at[k])

        @pl.loop(0, ROWS // STEP)
        def _(i):
            part = pl.ds(pl.multiple_of(i * STEP, STEP), STEP)
            at, total = 0, None
            for ref, size in zip(parts, sizes):
                for k in range(size):
                    term = jnp.dot(ref[k, part, :], right_ref[at], preferred_element_type=F32)
                    at, total = at + 1, term if total is None else total + term
            sum_ref[part, :] = total

    return pl.pallas_call(
        kernel,
        out_shape=(
            jax.ShapeDtypeStruct((count, ROWS, HALF), BF16),
            jax.ShapeDtypeStruct((ROWS, 2 * W), F32),
        ),
        in_specs=[SMEM, SMEM] + [VMEM] * (count + 1 + len(lists)),
        out_specs=(VMEM, VMEM),
        scratch_shapes=[pltpu.VMEM((TILES, BR + 1, B, W), F32)],
        compiler_params=params(24),
        cost_estimate=cost(16 * ROWS * HALF * W, 12 * MIB),
        name="product",
    )(table, places, *halves, right_side, *lists)


STEP = 256


def close_kernel(
    table_ref, places_ref, packed_ref, right_ref, sum_ref, dense_ref, mine_ref, other_ref, rows
):
    unpack(packed_ref, half_start(table_ref, FIRST), places_ref, rows, dense_ref.at[0])
    total = jnp.dot(dense_ref[0], right_ref[FIRST], preferred_element_type=F32) + sum_ref[...]
    mine_ref[...] = total[:, :W]
    other_ref[...] = total[:, W:]


def close(packed, table, places, right_side, total):
    return pl.pallas_call(
        close_kernel,
        out_shape=(jax.ShapeDtypeStruct((1, ROWS, HALF), BF16),)
        + (jax.ShapeDtypeStruct((ROWS, W), F32),) * 2,
        in_specs=[SMEM, SMEM, VMEM, VMEM, VMEM],
        out_specs=(VMEM,) * 3,
        scratch_shapes=[pltpu.VMEM((TILES, BR + 1, B, W), F32)],
        compiler_params=params(32),
        cost_estimate=cost(4 * ROWS * HALF * W, 3 * MIB),
        name="close",
    )(table, places, packed, right_side, total)


def finish_kernel(mine_ref, other_ref, masks_ref, square_ref):
    scale = (NB / (KX * KX * B)) ** 0.5
    for i in range(BR):
        rows = pl.ds(i * B, B)
        keep = jnp.broadcast_to(masks_ref[1, i : i + 1, :], (B, W))
        value = (mine_ref[rows, :] + other_ref[rows, :]) * scale
        square_ref[rows, :] = jnp.where(keep > 0.0, value, 0.0).astype(BF16)


def finish(mine, other, masks):
    return pl.pallas_call(
        finish_kernel,
        out_shape=jax.ShapeDtypeStruct((ROWS, W), BF16),
        in_specs=[VMEM] * 3,
        out_specs=VMEM,
        compiler_params=params(32),
        cost_estimate=cost(400_000, MIB),
        name="finish",
    )(mine, other, masks)


def cube_kernel(table_ref, *refs):
    *lists, square_ref, tile_ref, masks_ref, out_ref, acc = refs
    scale = (NB / (KX * KSQ * B)) ** 0.5
    at = 0
    for ref in lists:
        for k in range(ref.shape[0]):
            g, core = table_ref[at], table_ref[at + 1]
            half = square_ref[g, pl.ds(pl.multiple_of(core * HALF, HALF), HALF), :]
            term = jnp.dot(ref[k], half, preferred_element_type=F32)
            acc[...] = term if at == 0 else acc[...] + term
            at += 2
    for k in range(BR):
        rows = pl.ds(k * B, B)
        keep_x = jnp.broadcast_to(masks_ref[0, k : k + 1, :], (B, W))
        keep_out = jnp.broadcast_to(masks_ref[2, k : k + 1, :], (B, W))
        sparse = jnp.where(keep_x > 0.0, tile_ref[rows, :].astype(F32), 0.0)
        result = 1.5 * sparse - 0.5 * (acc[rows, :] * scale)
        out_ref[rows, :] = jnp.where(keep_out > 0.0, result, 0.0).astype(BF16)


def cube(table, lists, squares, tile, masks):
    return pl.pallas_call(
        cube_kernel,
        out_shape=jax.ShapeDtypeStruct((ROWS, W), BF16),
        in_specs=[SMEM] + [VMEM] * (len(lists) + 3),
        out_specs=VMEM,
        scratch_shapes=[pltpu.VMEM((ROWS, W), F32)],
        compiler_params=params(24),
        cost_estimate=cost(2 * GROUPS * ROWS * ROWS * W, 20 * MIB),
        name="cube",
    )(table, *lists, squares, tile, masks)


def local(matrix, list_x, list_sq, list_out):
    layers = lax.axis_size("layer")
    col = lax.axis_index("col").astype(jnp.int32)
    layer = lax.axis_index("layer").astype(jnp.int32)
    y, core = col // 2, col % 2
    sign = 1 - 2 * core
    base = jnp.reshape((col * layers + layer) * (W // B), (1,))

    brought = [(0, 1), (1, 1), (1, 0), (2, 1), (2, 0), (3, 1), (3, 0), (4, 1)]
    table = []
    for turn, own in ((-sign, core), (sign, 1 - core)):
        for d, same in brought:
            table += [jnp.bitwise_and(y + turn * d, GROUPS - 1), own if same else 1 - own]
    table = jnp.stack(table)

    cols = 2 * GROUPS
    swap = [(c, c ^ 1) for c in range(cols)]
    turn_y = [(c, (c + (2 if c % 2 == 0 else -2)) % cols) for c in range(cols)]

    def along_y(piece):
        return lax.ppermute(piece, "col", turn_y)

    def across(piece):
        return lax.ppermute(piece, "col", swap)

    def after(piece, *done):
        return lax.optimization_barrier((piece, *done))[0]

    pay, left, places = pack(base, list_x, matrix)
    pays = lax.all_gather(pay, "row", axis=0, tiled=False)
    a0 = lax.all_to_all(left, "layer", 0, 0, tiled=True)
    b0 = across(a0)
    a1, b1 = along_y(a0), along_y(b0)
    lists = [widen(0, [a0], table, places)]
    a2, b2 = along_y(after(a1, lists[-1])), along_y(b1)
    lists.append(widen(1, [a1, b1], table, places))
    a3, b3 = along_y(after(a2, lists[-1])), along_y(b2)
    lists.append(widen(3, [a2, b2], table, places))
    a4 = along_y(after(a3, lists[-1]))
    pays = after(pays, lists[-1], a3, b3)
    right_side, masks = right(table, base, (list_x, list_sq, list_out), pays, across(pays))
    dense, total = product([a3, b3], table, places, lists, right_side)
    end, mine, other = close(a4, table, places, right_side, total)
    square = finish(mine, across(other), masks)

    squares = lax.all_gather(square, "row", axis=0, tiled=False)
    lists += [dense, end]
    lists += [across(part) for part in lists]
    return cube(table, lists, squares, matrix, masks)


def solution(mesh):
    placed = (P("row", ("col", "layer")), P("row", None), P("row", None), P("row", None))
    return jax.shard_map(
        local, mesh=mesh, in_specs=placed, out_specs=P("row", ("col", "layer")), check_vma=False
    )
```

time: 170 us -> 159 us (0.935)
  the two profiles are of different devices: /device:TPU:32 before, /device:TPU:2 now
where the time goes in v5:
time: 159 us; the launch traced here: 158 us
  waiting for transfers between devices  47.2 us (30%)
  local copies, waits for them, and re-layouts  30.5 us (19%)
  starting transfers between devices  30.3 us (19%)
  Pallas kernels  22 us (14%)
  blocking collectives  13.9 us (9%)
  between operations  13.7 us (9%)
    unnamed x64, local copies, waits for them, and re-layouts  30.4 us
    all_gather x1, waiting for transfers between devices, local(): squares = lax.all_gather(square, 'row', axis=0, tiled=False)  24 us
    ppermute x8, starting transfers between devices, across(): return lax.ppermute(piece, 'col', swap)  16.9 us
    ppermute x7, waiting for transfers between devices, along_y(): return lax.ppermute(piece, 'col', turn_y)  16.1 us
    all_to_all x1, blocking collectives, local(): a0 = lax.all_to_all(left, 'layer', 0, 0, tiled=True)  13.9 us
    ppermute x7, starting transfers between devices, along_y(): return lax.ppermute(piece, 'col', turn_y)  13.4 us
    ppermute x8, waiting for transfers between devices, across(): return lax.ppermute(piece, 'col', swap)  7 us
    pallas_call x1, Pallas kernels, cube(): pl.pallas_call(cube_kernel, out_shape=jax.ShapeDtypeStruct((ROWS, W), BF1...  5.74 us
  transfers between devices with their start and end apart: 17, of which 10 were waited for; matrix products, arithmetic and copies ran while one was open for 0% of the time, Pallas kernels for 8%

profile of v5, /device:TPU:2, one launch (start us, length us, event | category | flops | bytes accessed | tf_op | source)
XLA Modules:
  0.0 157.6 jit_solution(13663184324824378275)
XLA Ops:
  9.7 13.9 %all_to_all.5.refs_0_ = bf16[4,10,32,128]{3,2,1,0:T(8,128)(2,1)S(1)} all-to-all(bf16[4,10,32,128]{3,2,1,0:T(8,128)(2,1)S(1)} %get-tuple-element.20), channel_id=1, replica_groups=mesh['row'=8,'col'=16,'layer'=4] {'layer'}, dimensions={0} | all-to-all | bytes 655360 | tf_op jit(solution)/shard_map/all_to_all | solution.py:348
  23.5 1.9 %collective-permute-start.1 = (bf16[4,10,32,128]{3,2,1,0:T(8,128)(2,1)S(1)}, bf16[4,10,32,128]{3,2,1,0:T(8,128)(2,1)S(1)}, u32[]{:S(2)}, u32[]{:S(2)}) collective-permute-start(bf16[4,10,32,128]{3,2,1,0:T(8,128)(2,1)S(1)} %all_to_all.5.refs_0_), channel_id=1, source_target_pairs={{0,4},{4,0},{8,12},{12,8},{16,20},{20,16},{24,28},{28,24},{32,36},... | collective-permute-start | bytes 983048 | tf_op jit(solution)/shard_map/ppermute | solution.py:341
  25.4 1.9 %collective-permute-start = (bf16[4,10,32,128]{3,2,1,0:T(8,128)(2,1)S(1)}, bf16[4,10,32,128]{3,2,1,0:T(8,128)(2,1)}, u32[]{:S(2)}, u32[]{:S(2)}) collective-permute-start(bf16[4,10,32,128]{3,2,1,0:T(8,128)(2,1)S(1)} %all_to_all.5.refs_0_), channel_id=1, source_target_pairs={{0,8},{4,60},{8,16},{12,4},{16,24},{20,12},{24,32},{28,20},{32,40}... | collective-permute-start | bytes 983048 | tf_op jit(solution)/shard_map/ppermute | solution.py:338
  27.4 1.9 %collective-permute-start.2 = (bf16[4,10,32,128]{3,2,1,0:T(8,128)(2,1)S(1)}, bf16[4,10,32,128]{3,2,1,0:T(8,128)(2,1)}, u32[]{:S(2)}, u32[]{:S(2)}) collective-permute-start(bf16[4,10,32,128]{3,2,1,0:T(8,128)(2,1)S(1)} %collective-permute-done.1), channel_id=1, source_target_pairs={{0,8},{4,60},{8,16},{12,4},{16,24},{20,12},{24,32},{28,20},{32,40}... | collective-permute-start | bytes 983048 | tf_op jit(solution)/shard_map/ppermute | solution.py:338
  30.8 4.9 %collective-permute-done.refs_0_ = bf16[4,10,32,128]{3,2,1,0:T(8,128)(2,1)} collective-permute-done((bf16[4,10,32,128]{3,2,1,0:T(8,128)(2,1)S(1)}, bf16[4,10,32,128]{3,2,1,0:T(8,128)(2,1)}, u32[]{:S(2)}, u32[]{:S(2)}) %collective-permute-start) | collective-permute-done | bytes 327712 | tf_op jit(solution)/shard_map/ppermute | solution.py:338
  35.7 1.9 %collective-permute-start.3 = (bf16[4,10,32,128]{3,2,1,0:T(8,128)(2,1)}, bf16[4,10,32,128]{3,2,1,0:T(8,128)(2,1)S(1)}, u32[]{:S(2)}, u32[]{:S(2)}) collective-permute-start(bf16[4,10,32,128]{3,2,1,0:T(8,128)(2,1)} %collective-permute-done.refs_0_), channel_id=1, source_target_pairs={{0,8},{4,60},{8,16},{12,4},{16,24},{20,12},{24,32},{28,20},{32,40}... | collective-permute-start | bytes 983048 | tf_op jit(solution)/shard_map/ppermute | solution.py:338
  41.1 2.1 %widen.4.refs_4_.refs_1_ = bf16[2,1024,512]{2,1,0:T(8,128)(2,1)S(1)} custom-call(s32[32]{0:T(128)S(1)} %stack.68.table_ref, s32[10,256]{1,0:T(8,128)S(1)} %get-tuple-element.19.places_ref, bf16[4,10,32,128]{3,2,1,0:T(8,128)(2,1)} %collective-permute-done.refs_0_, bf16[4,10,32,128]{3,2,1,0:T(8,128)(2,1)} %collective-permute-done.2.refs_1_), custom_call_target="tpu_custom_call" | custom-call | flops 536870912 | bytes 6291456 | tf_op jit(solution)/shard_map/widen/pallas_call | solution.py:190
  43.2 2.9 %collective-permute-done.3.refs_0_ = bf16[4,10,32,128]{3,2,1,0:T(8,128)(2,1)S(1)} collective-permute-done((bf16[4,10,32,128]{3,2,1,0:T(8,128)(2,1)}, bf16[4,10,32,128]{3,2,1,0:T(8,128)(2,1)S(1)}, u32[]{:S(2)}, u32[]{:S(2)}) %collective-permute-start.3) | collective-permute-done | bytes 327712 | tf_op jit(solution)/shard_map/ppermute | solution.py:338
  46.1 1.9 %collective-permute-start.5 = (bf16[4,10,32,128]{3,2,1,0:T(8,128)(2,1)S(1)}, bf16[4,10,32,128]{3,2,1,0:T(8,128)(2,1)S(1)}, u32[]{:S(2)}, u32[]{:S(2)}) collective-permute-start(bf16[4,10,32,128]{3,2,1,0:T(8,128)(2,1)S(1)} %collective-permute-done.3.refs_0_), channel_id=1, source_target_pairs={{0,8},{4,60},{8,16},{12,4},{16,24},{20,12},{24,32},{28,20},{32,40}... | collective-permute-start | bytes 983048 | tf_op jit(solution)/shard_map/ppermute | solution.py:338
  49.6 1.9 %collective-permute-start.6 = (bf16[4,10,32,128]{3,2,1,0:T(8,128)(2,1)S(1)}, bf16[4,10,32,128]{3,2,1,0:T(8,128)(2,1)S(1)}, u32[]{:S(2)}, u32[]{:S(2)}) collective-permute-start(bf16[4,10,32,128]{3,2,1,0:T(8,128)(2,1)S(1)} %collective-permute-done.4.refs_1_), channel_id=1, source_target_pairs={{0,8},{4,60},{8,16},{12,4},{16,24},{20,12},{24,32},{28,20},{32,40}... | collective-permute-start | bytes 983048 | tf_op jit(solution)/shard_map/ppermute | solution.py:338
  56.3 3.5 %collective-permute-done.6.refs_1_ = bf16[4,10,32,128]{3,2,1,0:T(8,128)(2,1)S(1)} collective-permute-done((bf16[4,10,32,128]{3,2,1,0:T(8,128)(2,1)S(1)}, bf16[4,10,32,128]{3,2,1,0:T(8,128)(2,1)S(1)}, u32[]{:S(2)}, u32[]{:S(2)}) %collective-permute-start.6) | collective-permute-done | bytes 327712 | tf_op jit(solution)/shard_map/ppermute | solution.py:338
  60.5 2.0 %collective-permute-start.7 = (bf16[8,576,128]{2,1,0:T(8,128)(2,1)}, bf16[8,576,128]{2,1,0:T(8,128)(2,1)S(1)}, u32[]{:S(2)}, u32[]{:S(2)}) collective-permute-start(bf16[8,576,128]{2,1,0:T(8,128)(2,1)} %bitcast.15), channel_id=1, source_target_pairs={{0,4},{4,0},{8,12},{12,8},{16,20},{20,16},{24,28},{28,24},{32,36},... | collective-permute-start | bytes 3538952 | tf_op jit(solution)/shard_map/ppermute | solution.py:341
  62.6 1.9 %collective-permute-start.8 = (bf16[4,10,32,128]{3,2,1,0:T(8,128)(2,1)S(1)}, bf16[4,10,32,128]{3,2,1,0:T(8,128)(2,1)S(1)}, u32[]{:S(2)}, u32[]{:S(2)}) collective-permute-start(bf16[4,10,32,128]{3,2,1,0:T(8,128)(2,1)S(1)} %collective-permute-done.5.refs_0_), channel_id=1, source_target_pairs={{0,8},{4,60},{8,16},{12,4},{16,24},{20,12},{24,32},{28,20},{32,40}... | collective-permute-start | bytes 983048 | tf_op jit(solution)/shard_map/ppermute | solution.py:338
  69.0 3.7 %right.1 = (bf16[8,512,256]{2,1,0:T(8,128)(2,1)S(1)}, f32[3,32,128]{2,1,0:T(8,128)S(1)}) custom-call(s32[32]{0:T(128)S(1)} %copy-done.27, s32[1]{0:T(128)} %bitcast.11.base_ref, s32[32,40]{1,0:T(8,128)S(1)} %copy-done.25, s32[32,60]{1,0:T(8,128)S(1)} %copy-done.30, s32[32,40]{1,0:T(8,128)S(1)} %copy-done.31, bf16[8,576,128]{2,1,0:T(8,128)(2,1)S(1)} %bitcast.16, ...), custom_call_target="tpu_custom_call" | custom-call | flops 40000000 | bytes 4194304 | tf_op jit(solution)/shard_map/right/pallas_call | solution.py:143
  73.7 4.4 %product.1 = (bf16[2,1024,512]{2,1,0:T(8,128)(2,1)S(1)}, f32[1024,256]{1,0:T(8,128)S(1)}) custom-call(s32[32]{0:T(128)S(1)} %copy-done.28, s32[10,256]{1,0:T(8,128)S(1)} %get-tuple-element.19.places_ref, bf16[4,10,32,128]{3,2,1,0:T(8,128)(2,1)S(1)} %collective-permute-done.5.refs_0_, bf16[4,10,32,128]{3,2,1,0:T(8,128)(2,1)S(1)} %copy-done.23, ...), custom_call_target="tpu_custom_call" | custom-call | flops 1073741824 | bytes 12582912 | tf_op jit(solution)/shard_map/product/pallas_call | solution.py:223
  82.0 2.0 %collective-permute-start.14 = (f32[1024,128]{1,0:T(8,128)S(1)}, f32[1024,128]{1,0:T(8,128)S(1)}, u32[]{:S(2)}, u32[]{:S(2)}) collective-permute-start(f32[1024,128]{1,0:T(8,128)S(1)} %get-tuple-element.31), channel_id=1, source_target_pairs={{0,4},{4,0},{8,12},{12,8},{16,20},{20,16},{24,28},{28,24},{32,36},... | collective-permute-start | bytes 1572872 | tf_op jit(solution)/shard_map/ppermute | solution.py:341
  86.6 2.0 %collective-permute-start.10 = (bf16[2,1024,512]{2,1,0:T(8,128)(2,1)S(1)}, bf16[2,1024,512]{2,1,0:T(8,128)(2,1)S(1)}, u32[]{:S(2)}, u32[]{:S(2)}) collective-permute-start(bf16[2,1024,512]{2,1,0:T(8,128)(2,1)S(1)} %widen.4.refs_4_.refs_1_), channel_id=1, source_target_pairs={{0,4},{4,0},{8,12},{12,8},{16,20},{20,16},{24,28},{28,24},{32,36},... | collective-permute-start | bytes 6291464 | tf_op jit(solution)/shard_map/ppermute | solution.py:341
  88.6 2.3 %collective-permute-start.11 = (bf16[2,1024,512]{2,1,0:T(8,128)(2,1)}, bf16[2,1024,512]{2,1,0:T(8,128)(2,1)S(1)}, u32[]{:S(2)}, u32[]{:S(2)}) collective-permute-start(bf16[2,1024,512]{2,1,0:T(8,128)(2,1)} %copy-done), channel_id=1, source_target_pairs={{0,4},{4,0},{8,12},{12,8},{16,20},{20,16},{24,28},{28,24},{32,36},... | collective-permute-start | bytes 6291464 | tf_op jit(solution)/shard_map/ppermute | solution.py:341
  90.9 2.0 %collective-permute-start.12 = (bf16[2,1024,512]{2,1,0:T(8,128)(2,1)}, bf16[2,1024,512]{2,1,0:T(8,128)(2,1)S(1)}, u32[]{:S(2)}, u32[]{:S(2)}) collective-permute-start(bf16[2,1024,512]{2,1,0:T(8,128)(2,1)} %copy-done.3), channel_id=1, source_target_pairs={{0,4},{4,0},{8,12},{12,8},{16,20},{20,16},{24,28},{28,24},{32,36},... | collective-permute-start | bytes 6291464 | tf_op jit(solution)/shard_map/ppermute | solution.py:341
  93.0 2.3 %collective-permute-start.9 = (bf16[1,1024,512]{2,1,0:T(8,128)(2,1)S(1)}, bf16[1,1024,512]{2,1,0:T(8,128)(2,1)S(1)}, u32[]{:S(2)}, u32[]{:S(2)}) collective-permute-start(bf16[1,1024,512]{2,1,0:T(8,128)(2,1)S(1)} %widen.3.refs_3_.refs_0_), channel_id=1, source_target_pairs={{0,4},{4,0},{8,12},{12,8},{16,20},{20,16},{24,28},{28,24},{32,36},... | collective-permute-start | bytes 3145736 | tf_op jit(solution)/shard_map/ppermute | solution.py:341
  95.3 2.2 %collective-permute-start.13 = (bf16[1,1024,512]{2,1,0:T(8,128)(2,1)}, bf16[1,1024,512]{2,1,0:T(8,128)(2,1)S(1)}, u32[]{:S(2)}, u32[]{:S(2)}) collective-permute-start(bf16[1,1024,512]{2,1,0:T(8,128)(2,1)} %copy-done.15), channel_id=1, source_target_pairs={{0,4},{4,0},{8,12},{12,8},{16,20},{20,16},{24,28},{28,24},{32,36},... | collective-permute-start | bytes 3145736 | tf_op jit(solution)/shard_map/ppermute | solution.py:341
  97.5 4.1 %collective-permute-done.9.refs_5_ = bf16[1,1024,512]{2,1,0:T(8,128)(2,1)S(1)} collective-permute-done((bf16[1,1024,512]{2,1,0:T(8,128)(2,1)S(1)}, bf16[1,1024,512]{2,1,0:T(8,128)(2,1)S(1)}, u32[]{:S(2)}, u32[]{:S(2)}) %collective-permute-start.9) | collective-permute-done | bytes 1048608 | tf_op jit(solution)/shard_map/ppermute | solution.py:341
  107.7 24.0 %all-gather.7.cloned.1.call-done = bf16[8192,128]{1,0:T(8,128)(2,1)} async-done(((bf16[1024,128]{1,0:T(8,128)(2,1)}), bf16[8192,128]{1,0:T(8,128)(2,1)}) %all-gather.7.cloned.1.call-update) | async-done | bytes 2097168 | tf_op jit(solution)/shard_map/all_gather | solution.py:363
  145.0 5.7 %cube.1 = bf16[1024,128]{1,0:T(8,128)(2,1)} custom-call(s32[32]{0:T(128)S(1)} %copy-done.29, bf16[1,1024,512]{2,1,0:T(8,128)(2,1)S(1)} %widen.3.refs_3_.refs_0_, bf16[2,1024,512]{2,1,0:T(8,128)(2,1)S(1)} %widen.4.refs_4_.refs_1_, bf16[2,1024,512]{2,1,0:T(8,128)(2,1)S(1)} %copy-done.2, bf16[2,1024,512]{2,1,0:T(8,128)(2,1)S(1)} %copy-done.4, ...), custom_call_target="tpu_custom_call" | custom-call | flops 2147483648 | bytes 20971520 | tf_op jit(solution)/shard_map/cube/pallas_call | solution.py:306
  (87 shorter events, 46.3 us)
Async XLA Ops:
  6.5 54.0 %all-gather.5.cloned.1.call-start = ((), (), s32[]{:S(2)}) async-start(), calls=%async_computation.1 | async-start | bytes 1327104 | tf_op jit(solution)/shard_map/all_gather | solution.py:347
  9.6 122.2 %all-gather.7.cloned.1.call-start = ((), (), s32[]{:S(2)}) async-start(), calls=%async_computation.2 | async-start | bytes 2359296 | tf_op jit(solution)/shard_map/all_gather | solution.py:363
  23.5 3.8 %collective-permute-start.1 = (bf16[4,10,32,128]{3,2,1,0:T(8,128)(2,1)S(1)}, bf16[4,10,32,128]{3,2,1,0:T(8,128)(2,1)S(1)}, u32[]{:S(2)}, u32[]{:S(2)}) collective-permute-start(bf16[4,10,32,128]{3,2,1,0:T(8,128)(2,1)S(1)} %all_to_all.5.refs_0_), channel_id=1, source_target_pairs={{0,4},{4,0},{8,12},{12,8},{16,20},{20,16},{24,28},{28,24},{32,36},... | collective-permute-start | bytes 983048 | tf_op jit(solution)/shard_map/ppermute | solution.py:341
  25.4 10.3 %collective-permute-start = (bf16[4,10,32,128]{3,2,1,0:T(8,128)(2,1)S(1)}, bf16[4,10,32,128]{3,2,1,0:T(8,128)(2,1)}, u32[]{:S(2)}, u32[]{:S(2)}) collective-permute-start(bf16[4,10,32,128]{3,2,1,0:T(8,128)(2,1)S(1)} %all_to_all.5.refs_0_), channel_id=1, source_target_pairs={{0,8},{4,60},{8,16},{12,4},{16,24},{20,12},{24,32},{28,20},{32,40}... | collective-permute-start | bytes 983048 | tf_op jit(solution)/shard_map/ppermute | solution.py:338
  27.4 11.9 %collective-permute-start.2 = (bf16[4,10,32,128]{3,2,1,0:T(8,128)(2,1)S(1)}, bf16[4,10,32,128]{3,2,1,0:T(8,128)(2,1)}, u32[]{:S(2)}, u32[]{:S(2)}) collective-permute-start(bf16[4,10,32,128]{3,2,1,0:T(8,128)(2,1)S(1)} %collective-permute-done.1), channel_id=1, source_target_pairs={{0,8},{4,60},{8,16},{12,4},{16,24},{20,12},{24,32},{28,20},{32,40}... | collective-permute-start | bytes 983048 | tf_op jit(solution)/shard_map/ppermute | solution.py:338
  29.4 23.9 %copy-start.26 = (s32[32]{0:T(128)}, s32[32]{0:T(128)S(1)}, u32[]{:S(2)}) copy-start(s32[32]{0:T(128)S(1)} %stack.68.table_ref) | copy-start | bytes 388
  30.8 34.8 %copy-start.25 = (s32[32,40]{1,0:T(8,128)S(1)}, s32[32,40]{1,0:T(8,128)}, u32[]{:S(2)}) copy-start(s32[32,40]{1,0:T(8,128)} %refs_0_.1) | copy-start | bytes 15364
  35.7 10.4 %collective-permute-start.3 = (bf16[4,10,32,128]{3,2,1,0:T(8,128)(2,1)}, bf16[4,10,32,128]{3,2,1,0:T(8,128)(2,1)S(1)}, u32[]{:S(2)}, u32[]{:S(2)}) collective-permute-start(bf16[4,10,32,128]{3,2,1,0:T(8,128)(2,1)} %collective-permute-done.refs_0_), channel_id=1, source_target_pairs={{0,8},{4,60},{8,16},{12,4},{16,24},{20,12},{24,32},{28,20},{32,40}... | collective-permute-start | bytes 983048 | tf_op jit(solution)/shard_map/ppermute | solution.py:338
  39.2 10.4 %collective-permute-start.4 = (bf16[4,10,32,128]{3,2,1,0:T(8,128)(2,1)}, bf16[4,10,32,128]{3,2,1,0:T(8,128)(2,1)S(1)}, u32[]{:S(2)}, u32[]{:S(2)}) collective-permute-start(bf16[4,10,32,128]{3,2,1,0:T(8,128)(2,1)} %collective-permute-done.2.refs_1_), channel_id=1, source_target_pairs={{0,8},{4,60},{8,16},{12,4},{16,24},{20,12},{24,32},{28,20},{32,40}... | collective-permute-start | bytes 983048 | tf_op jit(solution)/shard_map/ppermute | solution.py:338
  46.1 10.2 %collective-permute-start.5 = (bf16[4,10,32,128]{3,2,1,0:T(8,128)(2,1)S(1)}, bf16[4,10,32,128]{3,2,1,0:T(8,128)(2,1)S(1)}, u32[]{:S(2)}, u32[]{:S(2)}) collective-permute-start(bf16[4,10,32,128]{3,2,1,0:T(8,128)(2,1)S(1)} %collective-permute-done.3.refs_0_), channel_id=1, source_target_pairs={{0,8},{4,60},{8,16},{12,4},{16,24},{20,12},{24,32},{28,20},{32,40}... | collective-permute-start | bytes 983048 | tf_op jit(solution)/shard_map/ppermute | solution.py:338
  49.6 10.2 %collective-permute-start.6 = (bf16[4,10,32,128]{3,2,1,0:T(8,128)(2,1)S(1)}, bf16[4,10,32,128]{3,2,1,0:T(8,128)(2,1)S(1)}, u32[]{:S(2)}, u32[]{:S(2)}) collective-permute-start(bf16[4,10,32,128]{3,2,1,0:T(8,128)(2,1)S(1)} %collective-permute-done.4.refs_1_), channel_id=1, source_target_pairs={{0,8},{4,60},{8,16},{12,4},{16,24},{20,12},{24,32},{28,20},{32,40}... | collective-permute-start | bytes 983048 | tf_op jit(solution)/shard_map/ppermute | solution.py:338
  60.5 12.2 %copy-start.1 = (bf16[2,1024,512]{2,1,0:T(8,128)(2,1)S(1)}, bf16[2,1024,512]{2,1,0:T(8,128)(2,1)}, u32[]{:S(2)}) copy-start(bf16[2,1024,512]{2,1,0:T(8,128)(2,1)} %copy-done) | copy-start | bytes 6291460
  60.5 5.1 %collective-permute-start.7 = (bf16[8,576,128]{2,1,0:T(8,128)(2,1)}, bf16[8,576,128]{2,1,0:T(8,128)(2,1)S(1)}, u32[]{:S(2)}, u32[]{:S(2)}) collective-permute-start(bf16[8,576,128]{2,1,0:T(8,128)(2,1)} %bitcast.15), channel_id=1, source_target_pairs={{0,4},{4,0},{8,12},{12,8},{16,20},{20,16},{24,28},{28,24},{32,36},... | collective-permute-start | bytes 3538952 | tf_op jit(solution)/shard_map/ppermute | solution.py:341
  62.6 16.9 %collective-permute-start.8 = (bf16[4,10,32,128]{3,2,1,0:T(8,128)(2,1)S(1)}, bf16[4,10,32,128]{3,2,1,0:T(8,128)(2,1)S(1)}, u32[]{:S(2)}, u32[]{:S(2)}) collective-permute-start(bf16[4,10,32,128]{3,2,1,0:T(8,128)(2,1)S(1)} %collective-permute-done.5.refs_0_), channel_id=1, source_target_pairs={{0,8},{4,60},{8,16},{12,4},{16,24},{20,12},{24,32},{28,20},{32,40}... | collective-permute-start | bytes 983048 | tf_op jit(solution)/shard_map/ppermute | solution.py:338
  69.0 3.8 %copy-start.28 = (s32[32]{0:T(128)S(1)}, s32[32]{0:T(128)}, u32[]{:S(2)}) copy-start(s32[32]{0:T(128)} %copy-done.26) | copy-start | bytes 388
  79.4 52.4 %copy-start.14 = (bf16[1024,128]{1,0:T(8,128)(2,1)S(1)}, bf16[1024,128]{1,0:T(8,128)(2,1)}, u32[]{:S(2)}) copy-start(bf16[1024,128]{1,0:T(8,128)(2,1)} %refs_11_.1) | copy-start | bytes 786436
  79.4 52.4 %copy-start.29 = (s32[32]{0:T(128)S(1)}, s32[32]{0:T(128)}, u32[]{:S(2)}) copy-start(s32[32]{0:T(128)} %copy-done.26) | copy-start | bytes 388
  82.0 3.8 %collective-permute-start.14 = (f32[1024,128]{1,0:T(8,128)S(1)}, f32[1024,128]{1,0:T(8,128)S(1)}, u32[]{:S(2)}, u32[]{:S(2)}) collective-permute-start(f32[1024,128]{1,0:T(8,128)S(1)} %get-tuple-element.31), channel_id=1, source_target_pairs={{0,4},{4,0},{8,12},{12,8},{16,20},{20,16},{24,28},{28,24},{32,36},... | collective-permute-start | bytes 1572872 | tf_op jit(solution)/shard_map/ppermute | solution.py:341
  86.6 16.0 %collective-permute-start.10 = (bf16[2,1024,512]{2,1,0:T(8,128)(2,1)S(1)}, bf16[2,1024,512]{2,1,0:T(8,128)(2,1)S(1)}, u32[]{:S(2)}, u32[]{:S(2)}) collective-permute-start(bf16[2,1024,512]{2,1,0:T(8,128)(2,1)S(1)} %widen.4.refs_4_.refs_1_), channel_id=1, source_target_pairs={{0,4},{4,0},{8,12},{12,8},{16,20},{20,16},{24,28},{28,24},{32,36},... | collective-permute-start | bytes 6291464 | tf_op jit(solution)/shard_map/ppermute | solution.py:341
  88.6 15.3 %collective-permute-start.11 = (bf16[2,1024,512]{2,1,0:T(8,128)(2,1)}, bf16[2,1024,512]{2,1,0:T(8,128)(2,1)S(1)}, u32[]{:S(2)}, u32[]{:S(2)}) collective-permute-start(bf16[2,1024,512]{2,1,0:T(8,128)(2,1)} %copy-done), channel_id=1, source_target_pairs={{0,4},{4,0},{8,12},{12,8},{16,20},{20,16},{24,28},{28,24},{32,36},... | collective-permute-start | bytes 6291464 | tf_op jit(solution)/shard_map/ppermute | solution.py:341
  90.9 15.4 %collective-permute-start.12 = (bf16[2,1024,512]{2,1,0:T(8,128)(2,1)}, bf16[2,1024,512]{2,1,0:T(8,128)(2,1)S(1)}, u32[]{:S(2)}, u32[]{:S(2)}) collective-permute-start(bf16[2,1024,512]{2,1,0:T(8,128)(2,1)} %copy-done.3), channel_id=1, source_target_pairs={{0,4},{4,0},{8,12},{12,8},{16,20},{20,16},{24,28},{28,24},{32,36},... | collective-permute-start | bytes 6291464 | tf_op jit(solution)/shard_map/ppermute | solution.py:341
  93.0 8.7 %collective-permute-start.9 = (bf16[1,1024,512]{2,1,0:T(8,128)(2,1)S(1)}, bf16[1,1024,512]{2,1,0:T(8,128)(2,1)S(1)}, u32[]{:S(2)}, u32[]{:S(2)}) collective-permute-start(bf16[1,1024,512]{2,1,0:T(8,128)(2,1)S(1)} %widen.3.refs_3_.refs_0_), channel_id=1, source_target_pairs={{0,4},{4,0},{8,12},{12,8},{16,20},{20,16},{24,28},{28,24},{32,36},... | collective-permute-start | bytes 3145736 | tf_op jit(solution)/shard_map/ppermute | solution.py:341
  95.3 10.0 %collective-permute-start.13 = (bf16[1,1024,512]{2,1,0:T(8,128)(2,1)}, bf16[1,1024,512]{2,1,0:T(8,128)(2,1)S(1)}, u32[]{:S(2)}, u32[]{:S(2)}) collective-permute-start(bf16[1,1024,512]{2,1,0:T(8,128)(2,1)} %copy-done.15), channel_id=1, source_target_pairs={{0,4},{4,0},{8,12},{12,8},{16,20},{20,16},{24,28},{28,24},{32,36},... | collective-permute-start | bytes 3145736 | tf_op jit(solution)/shard_map/ppermute | solution.py:341
  131.8 1.6 %copy-start.2 = (bf16[2,1024,512]{2,1,0:T(8,128)(2,1)S(1)}, bf16[2,1024,512]{2,1,0:T(8,128)(2,1)}, u32[]{:S(2)}) copy-start(bf16[2,1024,512]{2,1,0:T(8,128)(2,1)} %copy-done) | copy-start | bytes 6291460
  (25 other events, 28.8 us)
Sparse Core Ops, SparseCore 0:
  9.7 46.9 all-gather.4
  86.7 45.0 all-gather.6

commit v6 on v5

--- a/solution.py
+++ b/solution.py
@@ -108,21 +108,33 @@
             pltpu.VMEM((ROWS, W), BF16),
             pltpu.SemaphoreType.DMA((2,)),
         ],
-        compiler_params=params(48),
+        compiler_params=params(6),
         cost_estimate=cost(10_000_000, 500_000),
         name="pack",
     )(base, list_x, tile)
 
 
-def right_kernel(table_ref, base_ref, *refs):
-    lists_hbm, mine_hbm, other_hbm, right_ref, masks_ref = refs[:3], *refs[3:7]
-    lists, pays_ref, sems = refs[7:10], refs[10], refs[11]
+def masks_kernel(base_ref, x_ref, sq_ref, out_ref, masks_ref):
+    for k, lists in enumerate((x_ref, sq_ref, out_ref)):
+        masks_ref[k] = lane_hits(lists[...], base_ref[0])
+
+
+def masks_of(base, lists):
+    return pl.pallas_call(
+        masks_kernel,
+        out_shape=jax.ShapeDtypeStruct((3, BR, W), F32),
+        in_specs=[SMEM] + [VMEM] * 3,
+        out_specs=VMEM,
+        compiler_params=params(4),
+        cost_estimate=cost(1_000_000, 100_000),
+        name="masks",
+    )(base, *lists)
+
+
+def right_kernel(table_ref, mine_hbm, other_hbm, right_ref, pays_ref, sems):
     rows = pl.ds(0, (CAP + 1) * B)
-    pairs = list(zip(lists_hbm, lists))
-    pairs += [(ref.at[:, rows], pays_ref.at[k]) for k, ref in enumerate((mine_hbm, other_hbm))]
+    pairs = [(ref.at[:, rows], pays_ref.at[k]) for k, ref in enumerate((mine_hbm, other_hbm))]
     copies_in(pairs, sems)
-    for k in range(3):
-        masks_ref[k] = lane_hits(lists[k][...], base_ref[0])
 
     @pl.loop(0, 2 * TILES)
     def _(h):
@@ -139,24 +151,20 @@
                 right_ref[h, pl.ds(t * B, B), pl.ds(k * W, W)] = value.astype(BF16)
 
 
-def right(table, base, lists, mine, other):
+def right(table, mine, other):
     return pl.pallas_call(
         right_kernel,
-        out_shape=(
-            jax.ShapeDtypeStruct((2 * TILES, HALF, 2 * W), BF16),
-            jax.ShapeDtypeStruct((3, BR, W), F32),
-        ),
-        in_specs=[SMEM, SMEM] + [HBM] * 5,
-        out_specs=(VMEM, VMEM),
-        scratch_shapes=[pltpu.VMEM(a.shape, jnp.int32) for a in lists]
-        + [
+        out_shape=jax.ShapeDtypeStruct((2 * TILES, HALF, 2 * W), BF16),
+        in_specs=[SMEM] + [HBM] * 2,
+        out_specs=VMEM,
+        scratch_shapes=[
             pltpu.VMEM((2, GROUPS, (CAP + 1) * B, W), BF16),
-            pltpu.SemaphoreType.DMA((5,)),
+            pltpu.SemaphoreType.DMA((2,)),
         ],
-        compiler_params=params(48),
+        compiler_params=params(12),
         cost_estimate=cost(40_000_000, 4 * MIB),
         name="right",
-    )(table, base, *lists, mine, other)
+    )(table, mine, other)
 
 
 def unpack(packed_ref, start, places_ref, rows, wide):
@@ -193,7 +201,7 @@
         in_specs=[SMEM, SMEM] + [VMEM] * count,
         out_specs=VMEM,
         scratch_shapes=[pltpu.VMEM((TILES, BR + 1, B, W), F32)],
-        compiler_params=params(24),
+        compiler_params=params(6),
         cost_estimate=cost(4 * ROWS * HALF * W * count, count * 3 * MIB),
         name="widen",
     )(table, places, *halves)
@@ -229,7 +237,7 @@
         in_specs=[SMEM, SMEM] + [VMEM] * (count + 1 + len(lists)),
         out_specs=(VMEM, VMEM),
         scratch_shapes=[pltpu.VMEM((TILES, BR + 1, B, W), F32)],
-        compiler_params=params(24),
+        compiler_params=params(8),
         cost_estimate=cost(16 * ROWS * HALF * W, 12 * MIB),
         name="product",
     )(table, places, *halves, right_side, *lists)
@@ -255,7 +263,7 @@
         in_specs=[SMEM, SMEM, VMEM, VMEM, VMEM],
         out_specs=(VMEM,) * 3,
         scratch_shapes=[pltpu.VMEM((TILES, BR + 1, B, W), F32)],
-        compiler_params=params(32),
+        compiler_params=params(8),
         cost_estimate=cost(4 * ROWS * HALF * W, 3 * MIB),
         name="close",
     )(table, places, packed, right_side, total)
@@ -276,7 +284,7 @@
         out_shape=jax.ShapeDtypeStruct((ROWS, W), BF16),
         in_specs=[VMEM] * 3,
         out_specs=VMEM,
-        compiler_params=params(32),
+        compiler_params=params(4),
         cost_estimate=cost(400_000, MIB),
         name="finish",
     )(mine, other, masks)
@@ -309,7 +317,7 @@
         in_specs=[SMEM] + [VMEM] * (len(lists) + 3),
         out_specs=VMEM,
         scratch_shapes=[pltpu.VMEM((ROWS, W), F32)],
-        compiler_params=params(24),
+        compiler_params=params(8),
         cost_estimate=cost(2 * GROUPS * ROWS * ROWS * W, 20 * MIB),
         name="cube",
     )(table, *lists, squares, tile, masks)
@@ -348,14 +356,15 @@
     a0 = lax.all_to_all(left, "layer", 0, 0, tiled=True)
     b0 = across(a0)
     a1, b1 = along_y(a0), along_y(b0)
-    lists = [widen(0, [a0], table, places)]
+    masks = masks_of(base, (list_x, list_sq, list_out))
+    lists = [widen(0, [after(a0, masks)], table, places)]
     a2, b2 = along_y(after(a1, lists[-1])), along_y(b1)
     lists.append(widen(1, [a1, b1], table, places))
     a3, b3 = along_y(after(a2, lists[-1])), along_y(b2)
     lists.append(widen(3, [a2, b2], table, places))
     a4 = along_y(after(a3, lists[-1]))
     pays = after(pays, lists[-1], a3, b3)
-    right_side, masks = right(table, base, (list_x, list_sq, list_out), pays, across(pays))
+    right_side = right(table, pays, across(pays))
     dense, total = product([a3, b3], table, places, lists, right_side)
     end, mine, other = close(a4, table, places, right_side, total)
     square = finish(mine, across(other), masks)

time: 159 us -> 155 us (0.975)
  waiting for transfers between devices: 47.2 us -> 43.5 us
    ppermute x7, waiting for transfers between devices: 16.1 us -> 12.4 us  [along_y(): return lax.ppermute(piece, 'col', turn_y)]
    unnamed x64 -> x56, local copies, waits for them, and re-layouts: 30.4 us -> 29.4 us
    pallas_call x1 -> x2, Pallas kernels: 3.73 us -> 3.64 us  [the longest x1 2.76 us: right(): pl.pallas_call(right_kernel, out_shape=jax.ShapeDtypeStruct((2 * TILES, H...]
  transfers between devices with their start and end apart: 17 -> 17, of which waited for: 10 -> 10; matrix products, arithmetic and copies ran while one was open for 0% -> 0% of each run, Pallas kernels for 8% -> 9%
where the time goes in v6:
time: 155 us; the launch traced here: 153 us
  waiting for transfers between devices  43.5 us (28%)
  starting transfers between devices  31 us (20%)
  local copies, waits for them, and re-layouts  29.5 us (19%)
  Pallas kernels  21.9 us (14%)
  blocking collectives  13.9 us (9%)
  between operations  13.7 us (9%)
    unnamed x56, local copies, waits for them, and re-layouts  29.4 us
    all_gather x1, waiting for transfers between devices, local(): squares = lax.all_gather(square, 'row', axis=0, tiled=False)  24.1 us
    ppermute x8, starting transfers between devices, across(): return lax.ppermute(piece, 'col', swap)  16.9 us
    ppermute x7, starting transfers between devices, along_y(): return lax.ppermute(piece, 'col', turn_y)  14.1 us
    all_to_all x1, blocking collectives, local(): a0 = lax.all_to_all(left, 'layer', 0, 0, tiled=True)  13.9 us
    ppermute x7, waiting for transfers between devices, along_y(): return lax.ppermute(piece, 'col', turn_y)  12.4 us
    ppermute x8, waiting for transfers between devices, across(): return lax.ppermute(piece, 'col', swap)  7 us
    pallas_call x1, Pallas kernels, cube(): pl.pallas_call(cube_kernel, out_shape=jax.ShapeDtypeStruct((ROWS, W), BF1...  5.73 us
  transfers between devices with their start and end apart: 17, of which 10 were waited for; matrix products, arithmetic and copies ran while one was open for 0% of the time, Pallas kernels for 9%

profile of v6, /device:TPU:2, one launch (start us, length us, event | category | flops | bytes accessed | tf_op | source)
XLA Modules:
  0.0 153.5 jit_solution(7820452022004609043)
XLA Ops:
  9.7 13.9 %all_to_all.5.refs_0_ = bf16[4,10,32,128]{3,2,1,0:T(8,128)(2,1)S(1)} all-to-all(bf16[4,10,32,128]{3,2,1,0:T(8,128)(2,1)S(1)} %get-tuple-element.19), channel_id=1, replica_groups=mesh['row'=8,'col'=16,'layer'=4] {'layer'}, dimensions={0} | all-to-all | bytes 655360 | tf_op jit(solution)/shard_map/all_to_all | solution.py:356
  23.5 1.9 %collective-permute-start.1 = (bf16[4,10,32,128]{3,2,1,0:T(8,128)(2,1)S(1)}, bf16[4,10,32,128]{3,2,1,0:T(8,128)(2,1)S(1)}, u32[]{:S(2)}, u32[]{:S(2)}) collective-permute-start(bf16[4,10,32,128]{3,2,1,0:T(8,128)(2,1)S(1)} %all_to_all.5.refs_0_), channel_id=1, source_target_pairs={{0,4},{4,0},{8,12},{12,8},{16,20},{20,16},{24,28},{28,24},{32,36},... | collective-permute-start | bytes 983048 | tf_op jit(solution)/shard_map/ppermute | solution.py:349
  25.4 1.9 %collective-permute-start = (bf16[4,10,32,128]{3,2,1,0:T(8,128)(2,1)S(1)}, bf16[4,10,32,128]{3,2,1,0:T(8,128)(2,1)}, u32[]{:S(2)}, u32[]{:S(2)}) collective-permute-start(bf16[4,10,32,128]{3,2,1,0:T(8,128)(2,1)S(1)} %all_to_all.5.refs_0_), channel_id=1, source_target_pairs={{0,8},{4,60},{8,16},{12,4},{16,24},{20,12},{24,32},{28,20},{32,40}... | collective-permute-start | bytes 983048 | tf_op jit(solution)/shard_map/ppermute | solution.py:346
  27.4 1.9 %collective-permute-start.2 = (bf16[4,10,32,128]{3,2,1,0:T(8,128)(2,1)S(1)}, bf16[4,10,32,128]{3,2,1,0:T(8,128)(2,1)}, u32[]{:S(2)}, u32[]{:S(2)}) collective-permute-start(bf16[4,10,32,128]{3,2,1,0:T(8,128)(2,1)S(1)} %collective-permute-done.1), channel_id=1, source_target_pairs={{0,8},{4,60},{8,16},{12,4},{16,24},{20,12},{24,32},{28,20},{32,40}... | collective-permute-start | bytes 983048 | tf_op jit(solution)/shard_map/ppermute | solution.py:346
  33.8 1.9 %collective-permute-done.refs_0_ = bf16[4,10,32,128]{3,2,1,0:T(8,128)(2,1)} collective-permute-done((bf16[4,10,32,128]{3,2,1,0:T(8,128)(2,1)S(1)}, bf16[4,10,32,128]{3,2,1,0:T(8,128)(2,1)}, u32[]{:S(2)}, u32[]{:S(2)}) %collective-permute-start) | collective-permute-done | bytes 327712 | tf_op jit(solution)/shard_map/ppermute | solution.py:346
  39.2 2.6 %collective-permute-start.4 = (bf16[4,10,32,128]{3,2,1,0:T(8,128)(2,1)}, bf16[4,10,32,128]{3,2,1,0:T(8,128)(2,1)S(1)}, u32[]{:S(2)}, u32[]{:S(2)}) collective-permute-start(bf16[4,10,32,128]{3,2,1,0:T(8,128)(2,1)} %collective-permute-done.2.refs_1_), channel_id=1, source_target_pairs={{0,8},{4,60},{8,16},{12,4},{16,24},{20,12},{24,32},{28,20},{32,40}... | collective-permute-start | bytes 983048 | tf_op jit(solution)/shard_map/ppermute | solution.py:346
  41.8 2.1 %widen.4.refs_4_.refs_1_ = bf16[2,1024,512]{2,1,0:T(8,128)(2,1)S(1)} custom-call(s32[32]{0:T(128)S(1)} %stack.68.table_ref, s32[10,256]{1,0:T(8,128)S(1)} %get-tuple-element.18.places_ref, bf16[4,10,32,128]{3,2,1,0:T(8,128)(2,1)} %collective-permute-done.refs_0_, bf16[4,10,32,128]{3,2,1,0:T(8,128)(2,1)} %collective-permute-done.2.refs_1_), custom_call_target="tpu_custom_call" | custom-call | flops 536870912 | bytes 6291456 | tf_op jit(solution)/shard_map/widen/pallas_call | solution.py:198
  43.9 2.2 %collective-permute-done.3.refs_0_ = bf16[4,10,32,128]{3,2,1,0:T(8,128)(2,1)S(1)} collective-permute-done((bf16[4,10,32,128]{3,2,1,0:T(8,128)(2,1)}, bf16[4,10,32,128]{3,2,1,0:T(8,128)(2,1)S(1)}, u32[]{:S(2)}, u32[]{:S(2)}) %collective-permute-start.3) | collective-permute-done | bytes 327712 | tf_op jit(solution)/shard_map/ppermute | solution.py:346
  46.1 1.9 %collective-permute-start.5 = (bf16[4,10,32,128]{3,2,1,0:T(8,128)(2,1)S(1)}, bf16[4,10,32,128]{3,2,1,0:T(8,128)(2,1)S(1)}, u32[]{:S(2)}, u32[]{:S(2)}) collective-permute-start(bf16[4,10,32,128]{3,2,1,0:T(8,128)(2,1)S(1)} %collective-permute-done.3.refs_0_), channel_id=1, source_target_pairs={{0,8},{4,60},{8,16},{12,4},{16,24},{20,12},{24,32},{28,20},{32,40}... | collective-permute-start | bytes 983048 | tf_op jit(solution)/shard_map/ppermute | solution.py:346
  49.6 1.9 %collective-permute-start.6 = (bf16[4,10,32,128]{3,2,1,0:T(8,128)(2,1)S(1)}, bf16[4,10,32,128]{3,2,1,0:T(8,128)(2,1)S(1)}, u32[]{:S(2)}, u32[]{:S(2)}) collective-permute-start(bf16[4,10,32,128]{3,2,1,0:T(8,128)(2,1)S(1)} %collective-permute-done.4.refs_1_), channel_id=1, source_target_pairs={{0,8},{4,60},{8,16},{12,4},{16,24},{20,12},{24,32},{28,20},{32,40}... | collective-permute-start | bytes 983048 | tf_op jit(solution)/shard_map/ppermute | solution.py:346
  56.3 3.5 %collective-permute-done.6.refs_1_ = bf16[4,10,32,128]{3,2,1,0:T(8,128)(2,1)S(1)} collective-permute-done((bf16[4,10,32,128]{3,2,1,0:T(8,128)(2,1)S(1)}, bf16[4,10,32,128]{3,2,1,0:T(8,128)(2,1)S(1)}, u32[]{:S(2)}, u32[]{:S(2)}) %collective-permute-start.6) | collective-permute-done | bytes 327712 | tf_op jit(solution)/shard_map/ppermute | solution.py:346
  60.5 2.0 %collective-permute-start.7 = (bf16[8,576,128]{2,1,0:T(8,128)(2,1)}, bf16[8,576,128]{2,1,0:T(8,128)(2,1)S(1)}, u32[]{:S(2)}, u32[]{:S(2)}) collective-permute-start(bf16[8,576,128]{2,1,0:T(8,128)(2,1)} %bitcast.15), channel_id=1, source_target_pairs={{0,4},{4,0},{8,12},{12,8},{16,20},{20,16},{24,28},{28,24},{32,36},... | collective-permute-start | bytes 3538952 | tf_op jit(solution)/shard_map/ppermute | solution.py:349
  62.5 1.9 %collective-permute-start.8 = (bf16[4,10,32,128]{3,2,1,0:T(8,128)(2,1)S(1)}, bf16[4,10,32,128]{3,2,1,0:T(8,128)(2,1)S(1)}, u32[]{:S(2)}, u32[]{:S(2)}) collective-permute-start(bf16[4,10,32,128]{3,2,1,0:T(8,128)(2,1)S(1)} %collective-permute-done.5.refs_0_), channel_id=1, source_target_pairs={{0,8},{4,60},{8,16},{12,4},{16,24},{20,12},{24,32},{28,20},{32,40}... | collective-permute-start | bytes 983048 | tf_op jit(solution)/shard_map/ppermute | solution.py:346
  66.8 2.8 %right.1.refs_2_.right_ref = bf16[8,512,256]{2,1,0:T(8,128)(2,1)S(1)} custom-call(s32[32]{0:T(128)S(1)} %stack.68.table_ref, bf16[8,576,128]{2,1,0:T(8,128)(2,1)S(1)} %bitcast.16, bf16[8,576,128]{2,1,0:T(8,128)(2,1)S(1)} %collective-permute-done.7.other_hbm), custom_call_target="tpu_custom_call" | custom-call | flops 40000000 | bytes 4194304 | tf_op jit(solution)/shard_map/right/pallas_call | solution.py:155
  69.6 4.4 %product.1 = (bf16[2,1024,512]{2,1,0:T(8,128)(2,1)S(1)}, f32[1024,256]{1,0:T(8,128)S(1)}) custom-call(s32[32]{0:T(128)S(1)} %stack.68.table_ref, s32[10,256]{1,0:T(8,128)S(1)} %get-tuple-element.18.places_ref, bf16[4,10,32,128]{3,2,1,0:T(8,128)(2,1)S(1)} %collective-permute-done.5.refs_0_, bf16[4,10,32,128]{3,2,1,0:T(8,128)(2,1)S(1)} %copy-done.23, ...), custom_call_target="tpu_custom_call" | custom-call | flops 1073741824 | bytes 12582912 | tf_op jit(solution)/shard_map/product/pallas_call | solution.py:231
  77.9 2.0 %collective-permute-start.14 = (f32[1024,128]{1,0:T(8,128)S(1)}, f32[1024,128]{1,0:T(8,128)S(1)}, u32[]{:S(2)}, u32[]{:S(2)}) collective-permute-start(f32[1024,128]{1,0:T(8,128)S(1)} %get-tuple-element.30), channel_id=1, source_target_pairs={{0,4},{4,0},{8,12},{12,8},{16,20},{20,16},{24,28},{28,24},{32,36},... | collective-permute-start | bytes 1572872 | tf_op jit(solution)/shard_map/ppermute | solution.py:349
  82.5 2.0 %collective-permute-start.10 = (bf16[2,1024,512]{2,1,0:T(8,128)(2,1)S(1)}, bf16[2,1024,512]{2,1,0:T(8,128)(2,1)S(1)}, u32[]{:S(2)}, u32[]{:S(2)}) collective-permute-start(bf16[2,1024,512]{2,1,0:T(8,128)(2,1)S(1)} %widen.4.refs_4_.refs_1_), channel_id=1, source_target_pairs={{0,4},{4,0},{8,12},{12,8},{16,20},{20,16},{24,28},{28,24},{32,36},... | collective-permute-start | bytes 6291464 | tf_op jit(solution)/shard_map/ppermute | solution.py:349
  84.6 2.3 %collective-permute-start.11 = (bf16[2,1024,512]{2,1,0:T(8,128)(2,1)}, bf16[2,1024,512]{2,1,0:T(8,128)(2,1)S(1)}, u32[]{:S(2)}, u32[]{:S(2)}) collective-permute-start(bf16[2,1024,512]{2,1,0:T(8,128)(2,1)} %copy-done), channel_id=1, source_target_pairs={{0,4},{4,0},{8,12},{12,8},{16,20},{20,16},{24,28},{28,24},{32,36},... | collective-permute-start | bytes 6291464 | tf_op jit(solution)/shard_map/ppermute | solution.py:349
  86.8 2.0 %collective-permute-start.12 = (bf16[2,1024,512]{2,1,0:T(8,128)(2,1)}, bf16[2,1024,512]{2,1,0:T(8,128)(2,1)S(1)}, u32[]{:S(2)}, u32[]{:S(2)}) collective-permute-start(bf16[2,1024,512]{2,1,0:T(8,128)(2,1)} %copy-done.3), channel_id=1, source_target_pairs={{0,4},{4,0},{8,12},{12,8},{16,20},{20,16},{24,28},{28,24},{32,36},... | collective-permute-start | bytes 6291464 | tf_op jit(solution)/shard_map/ppermute | solution.py:349
  88.9 2.3 %collective-permute-start.9 = (bf16[1,1024,512]{2,1,0:T(8,128)(2,1)S(1)}, bf16[1,1024,512]{2,1,0:T(8,128)(2,1)S(1)}, u32[]{:S(2)}, u32[]{:S(2)}) collective-permute-start(bf16[1,1024,512]{2,1,0:T(8,128)(2,1)S(1)} %widen.3.refs_3_.refs_0_), channel_id=1, source_target_pairs={{0,4},{4,0},{8,12},{12,8},{16,20},{20,16},{24,28},{28,24},{32,36},... | collective-permute-start | bytes 3145736 | tf_op jit(solution)/shard_map/ppermute | solution.py:349
  91.2 2.2 %collective-permute-start.13 = (bf16[1,1024,512]{2,1,0:T(8,128)(2,1)}, bf16[1,1024,512]{2,1,0:T(8,128)(2,1)S(1)}, u32[]{:S(2)}, u32[]{:S(2)}) collective-permute-start(bf16[1,1024,512]{2,1,0:T(8,128)(2,1)} %copy-done.15), channel_id=1, source_target_pairs={{0,4},{4,0},{8,12},{12,8},{16,20},{20,16},{24,28},{28,24},{32,36},... | collective-permute-start | bytes 3145736 | tf_op jit(solution)/shard_map/ppermute | solution.py:349
  93.4 4.1 %collective-permute-done.9.refs_5_ = bf16[1,1024,512]{2,1,0:T(8,128)(2,1)S(1)} collective-permute-done((bf16[1,1024,512]{2,1,0:T(8,128)(2,1)S(1)}, bf16[1,1024,512]{2,1,0:T(8,128)(2,1)S(1)}, u32[]{:S(2)}, u32[]{:S(2)}) %collective-permute-start.9) | collective-permute-done | bytes 1048608 | tf_op jit(solution)/shard_map/ppermute | solution.py:349
  103.6 24.1 %all-gather.7.cloned.1.call-done = bf16[8192,128]{1,0:T(8,128)(2,1)} async-done(((bf16[1024,128]{1,0:T(8,128)(2,1)}), bf16[8192,128]{1,0:T(8,128)(2,1)}) %all-gather.7.cloned.1.call-update) | async-done | bytes 2097168 | tf_op jit(solution)/shard_map/all_gather | solution.py:372
  140.9 5.7 %cube.1 = bf16[1024,128]{1,0:T(8,128)(2,1)} custom-call(s32[32]{0:T(128)S(1)} %stack.68.table_ref, bf16[1,1024,512]{2,1,0:T(8,128)(2,1)S(1)} %widen.3.refs_3_.refs_0_, bf16[2,1024,512]{2,1,0:T(8,128)(2,1)S(1)} %widen.4.refs_4_.refs_1_, bf16[2,1024,512]{2,1,0:T(8,128)(2,1)S(1)} %copy-done.2, bf16[2,1024,512]{2,1,0:T(8,128)(2,1)S(1)} %copy-done.4, ...), custom_call_target="tpu_custom_call" | custom-call | flops 2147483648 | bytes 20971520 | tf_op jit(solution)/shard_map/cube/pallas_call | solution.py:314
  (80 shorter events, 46.2 us)
Async XLA Ops:
  6.5 54.0 %all-gather.5.cloned.1.call-start = ((), (), s32[]{:S(2)}) async-start(), calls=%async_computation.1 | async-start | bytes 1327104 | tf_op jit(solution)/shard_map/all_gather | solution.py:355
  9.6 118.1 %all-gather.7.cloned.1.call-start = ((), (), s32[]{:S(2)}) async-start(), calls=%async_computation.2 | async-start | bytes 2359296 | tf_op jit(solution)/shard_map/all_gather | solution.py:372
  23.5 3.8 %collective-permute-start.1 = (bf16[4,10,32,128]{3,2,1,0:T(8,128)(2,1)S(1)}, bf16[4,10,32,128]{3,2,1,0:T(8,128)(2,1)S(1)}, u32[]{:S(2)}, u32[]{:S(2)}) collective-permute-start(bf16[4,10,32,128]{3,2,1,0:T(8,128)(2,1)S(1)} %all_to_all.5.refs_0_), channel_id=1, source_target_pairs={{0,4},{4,0},{8,12},{12,8},{16,20},{20,16},{24,28},{28,24},{32,36},... | collective-permute-start | bytes 983048 | tf_op jit(solution)/shard_map/ppermute | solution.py:349
  25.4 10.3 %collective-permute-start = (bf16[4,10,32,128]{3,2,1,0:T(8,128)(2,1)S(1)}, bf16[4,10,32,128]{3,2,1,0:T(8,128)(2,1)}, u32[]{:S(2)}, u32[]{:S(2)}) collective-permute-start(bf16[4,10,32,128]{3,2,1,0:T(8,128)(2,1)S(1)} %all_to_all.5.refs_0_), channel_id=1, source_target_pairs={{0,8},{4,60},{8,16},{12,4},{16,24},{20,12},{24,32},{28,20},{32,40}... | collective-permute-start | bytes 983048 | tf_op jit(solution)/shard_map/ppermute | solution.py:346
  27.4 11.9 %collective-permute-start.2 = (bf16[4,10,32,128]{3,2,1,0:T(8,128)(2,1)S(1)}, bf16[4,10,32,128]{3,2,1,0:T(8,128)(2,1)}, u32[]{:S(2)}, u32[]{:S(2)}) collective-permute-start(bf16[4,10,32,128]{3,2,1,0:T(8,128)(2,1)S(1)} %collective-permute-done.1), channel_id=1, source_target_pairs={{0,8},{4,60},{8,16},{12,4},{16,24},{20,12},{24,32},{28,20},{32,40}... | collective-permute-start | bytes 983048 | tf_op jit(solution)/shard_map/ppermute | solution.py:346
  35.7 10.4 %collective-permute-start.3 = (bf16[4,10,32,128]{3,2,1,0:T(8,128)(2,1)}, bf16[4,10,32,128]{3,2,1,0:T(8,128)(2,1)S(1)}, u32[]{:S(2)}, u32[]{:S(2)}) collective-permute-start(bf16[4,10,32,128]{3,2,1,0:T(8,128)(2,1)} %collective-permute-done.refs_0_), channel_id=1, source_target_pairs={{0,8},{4,60},{8,16},{12,4},{16,24},{20,12},{24,32},{28,20},{32,40}... | collective-permute-start | bytes 983048 | tf_op jit(solution)/shard_map/ppermute | solution.py:346
  39.2 10.4 %collective-permute-start.4 = (bf16[4,10,32,128]{3,2,1,0:T(8,128)(2,1)}, bf16[4,10,32,128]{3,2,1,0:T(8,128)(2,1)S(1)}, u32[]{:S(2)}, u32[]{:S(2)}) collective-permute-start(bf16[4,10,32,128]{3,2,1,0:T(8,128)(2,1)} %collective-permute-done.2.refs_1_), channel_id=1, source_target_pairs={{0,8},{4,60},{8,16},{12,4},{16,24},{20,12},{24,32},{28,20},{32,40}... | collective-permute-start | bytes 983048 | tf_op jit(solution)/shard_map/ppermute | solution.py:346
  46.1 10.2 %collective-permute-start.5 = (bf16[4,10,32,128]{3,2,1,0:T(8,128)(2,1)S(1)}, bf16[4,10,32,128]{3,2,1,0:T(8,128)(2,1)S(1)}, u32[]{:S(2)}, u32[]{:S(2)}) collective-permute-start(bf16[4,10,32,128]{3,2,1,0:T(8,128)(2,1)S(1)} %collective-permute-done.3.refs_0_), channel_id=1, source_target_pairs={{0,8},{4,60},{8,16},{12,4},{16,24},{20,12},{24,32},{28,20},{32,40}... | collective-permute-start | bytes 983048 | tf_op jit(solution)/shard_map/ppermute | solution.py:346
  49.6 10.2 %collective-permute-start.6 = (bf16[4,10,32,128]{3,2,1,0:T(8,128)(2,1)S(1)}, bf16[4,10,32,128]{3,2,1,0:T(8,128)(2,1)S(1)}, u32[]{:S(2)}, u32[]{:S(2)}) collective-permute-start(bf16[4,10,32,128]{3,2,1,0:T(8,128)(2,1)S(1)} %collective-permute-done.4.refs_1_), channel_id=1, source_target_pairs={{0,8},{4,60},{8,16},{12,4},{16,24},{20,12},{24,32},{28,20},{32,40}... | collective-permute-start | bytes 983048 | tf_op jit(solution)/shard_map/ppermute | solution.py:346
  60.5 9.1 %copy-start.1 = (bf16[2,1024,512]{2,1,0:T(8,128)(2,1)S(1)}, bf16[2,1024,512]{2,1,0:T(8,128)(2,1)}, u32[]{:S(2)}) copy-start(bf16[2,1024,512]{2,1,0:T(8,128)(2,1)} %copy-done) | copy-start | bytes 6291460
  60.5 5.1 %collective-permute-start.7 = (bf16[8,576,128]{2,1,0:T(8,128)(2,1)}, bf16[8,576,128]{2,1,0:T(8,128)(2,1)S(1)}, u32[]{:S(2)}, u32[]{:S(2)}) collective-permute-start(bf16[8,576,128]{2,1,0:T(8,128)(2,1)} %bitcast.15), channel_id=1, source_target_pairs={{0,4},{4,0},{8,12},{12,8},{16,20},{20,16},{24,28},{28,24},{32,36},... | collective-permute-start | bytes 3538952 | tf_op jit(solution)/shard_map/ppermute | solution.py:349
  62.5 12.8 %collective-permute-start.8 = (bf16[4,10,32,128]{3,2,1,0:T(8,128)(2,1)S(1)}, bf16[4,10,32,128]{3,2,1,0:T(8,128)(2,1)S(1)}, u32[]{:S(2)}, u32[]{:S(2)}) collective-permute-start(bf16[4,10,32,128]{3,2,1,0:T(8,128)(2,1)S(1)} %collective-permute-done.5.refs_0_), channel_id=1, source_target_pairs={{0,8},{4,60},{8,16},{12,4},{16,24},{20,12},{24,32},{28,20},{32,40}... | collective-permute-start | bytes 983048 | tf_op jit(solution)/shard_map/ppermute | solution.py:346
  66.8 2.8 %copy-start.23 = (bf16[4,10,32,128]{3,2,1,0:T(8,128)(2,1)S(1)}, bf16[4,10,32,128]{3,2,1,0:T(8,128)(2,1)}, u32[]{:S(2)}) copy-start(bf16[4,10,32,128]{3,2,1,0:T(8,128)(2,1)} %copy-done.22) | copy-start | bytes 983044
  75.3 52.4 %copy-start.14 = (bf16[1024,128]{1,0:T(8,128)(2,1)S(1)}, bf16[1024,128]{1,0:T(8,128)(2,1)}, u32[]{:S(2)}) copy-start(bf16[1024,128]{1,0:T(8,128)(2,1)} %refs_11_.1) | copy-start | bytes 786436
  77.9 3.8 %collective-permute-start.14 = (f32[1024,128]{1,0:T(8,128)S(1)}, f32[1024,128]{1,0:T(8,128)S(1)}, u32[]{:S(2)}, u32[]{:S(2)}) collective-permute-start(f32[1024,128]{1,0:T(8,128)S(1)} %get-tuple-element.30), channel_id=1, source_target_pairs={{0,4},{4,0},{8,12},{12,8},{16,20},{20,16},{24,28},{28,24},{32,36},... | collective-permute-start | bytes 1572872 | tf_op jit(solution)/shard_map/ppermute | solution.py:349
  82.5 16.0 %collective-permute-start.10 = (bf16[2,1024,512]{2,1,0:T(8,128)(2,1)S(1)}, bf16[2,1024,512]{2,1,0:T(8,128)(2,1)S(1)}, u32[]{:S(2)}, u32[]{:S(2)}) collective-permute-start(bf16[2,1024,512]{2,1,0:T(8,128)(2,1)S(1)} %widen.4.refs_4_.refs_1_), channel_id=1, source_target_pairs={{0,4},{4,0},{8,12},{12,8},{16,20},{20,16},{24,28},{28,24},{32,36},... | collective-permute-start | bytes 6291464 | tf_op jit(solution)/shard_map/ppermute | solution.py:349
  84.6 15.4 %collective-permute-start.11 = (bf16[2,1024,512]{2,1,0:T(8,128)(2,1)}, bf16[2,1024,512]{2,1,0:T(8,128)(2,1)S(1)}, u32[]{:S(2)}, u32[]{:S(2)}) collective-permute-start(bf16[2,1024,512]{2,1,0:T(8,128)(2,1)} %copy-done), channel_id=1, source_target_pairs={{0,4},{4,0},{8,12},{12,8},{16,20},{20,16},{24,28},{28,24},{32,36},... | collective-permute-start | bytes 6291464 | tf_op jit(solution)/shard_map/ppermute | solution.py:349
  86.8 15.4 %collective-permute-start.12 = (bf16[2,1024,512]{2,1,0:T(8,128)(2,1)}, bf16[2,1024,512]{2,1,0:T(8,128)(2,1)S(1)}, u32[]{:S(2)}, u32[]{:S(2)}) collective-permute-start(bf16[2,1024,512]{2,1,0:T(8,128)(2,1)} %copy-done.3), channel_id=1, source_target_pairs={{0,4},{4,0},{8,12},{12,8},{16,20},{20,16},{24,28},{28,24},{32,36},... | collective-permute-start | bytes 6291464 | tf_op jit(solution)/shard_map/ppermute | solution.py:349
  88.9 8.7 %collective-permute-start.9 = (bf16[1,1024,512]{2,1,0:T(8,128)(2,1)S(1)}, bf16[1,1024,512]{2,1,0:T(8,128)(2,1)S(1)}, u32[]{:S(2)}, u32[]{:S(2)}) collective-permute-start(bf16[1,1024,512]{2,1,0:T(8,128)(2,1)S(1)} %widen.3.refs_3_.refs_0_), channel_id=1, source_target_pairs={{0,4},{4,0},{8,12},{12,8},{16,20},{20,16},{24,28},{28,24},{32,36},... | collective-permute-start | bytes 3145736 | tf_op jit(solution)/shard_map/ppermute | solution.py:349
  91.2 10.0 %collective-permute-start.13 = (bf16[1,1024,512]{2,1,0:T(8,128)(2,1)}, bf16[1,1024,512]{2,1,0:T(8,128)(2,1)S(1)}, u32[]{:S(2)}, u32[]{:S(2)}) collective-permute-start(bf16[1,1024,512]{2,1,0:T(8,128)(2,1)} %copy-done.15), channel_id=1, source_target_pairs={{0,4},{4,0},{8,12},{12,8},{16,20},{20,16},{24,28},{28,24},{32,36},... | collective-permute-start | bytes 3145736 | tf_op jit(solution)/shard_map/ppermute | solution.py:349
  127.7 1.6 %copy-start.2 = (bf16[2,1024,512]{2,1,0:T(8,128)(2,1)S(1)}, bf16[2,1024,512]{2,1,0:T(8,128)(2,1)}, u32[]{:S(2)}) copy-start(bf16[2,1024,512]{2,1,0:T(8,128)(2,1)} %copy-done) | copy-start | bytes 6291460
  129.3 1.6 %copy-start.4 = (bf16[2,1024,512]{2,1,0:T(8,128)(2,1)S(1)}, bf16[2,1024,512]{2,1,0:T(8,128)(2,1)}, u32[]{:S(2)}) copy-start(bf16[2,1024,512]{2,1,0:T(8,128)(2,1)} %copy-done.3) | copy-start | bytes 6291460
  130.9 1.6 %copy-start.5 = (bf16[8192,128]{1,0:T(8,128)(2,1)S(1)}, bf16[8192,128]{1,0:T(8,128)(2,1)}, u32[]{:S(2)}) copy-start(bf16[8192,128]{1,0:T(8,128)(2,1)} %all-gather.7.cloned.1.call-done) | copy-start | bytes 6291460
  132.5 1.6 %copy-start.7 = (bf16[2,1024,512]{2,1,0:T(8,128)(2,1)S(1)}, bf16[2,1024,512]{2,1,0:T(8,128)(2,1)}, u32[]{:S(2)}) copy-start(bf16[2,1024,512]{2,1,0:T(8,128)(2,1)} %copy-done.6) | copy-start | bytes 6291460
  (21 other events, 23.1 us)
Sparse Core Ops, SparseCore 0:
  9.7 46.9 all-gather.4
  82.6 45.0 all-gather.6

commit v7 on v6

--- a/solution.py
+++ b/solution.py
@@ -214,9 +214,12 @@
 
     def kernel(table_ref, places_ref, *refs):
         packed, refs = refs[:count], refs[count:]
-        right_ref, parts, sum_ref, rows = refs[0], refs[1:-2], refs[-2], refs[-1]
+        right_ref, *parts, dense_ref, sum_ref, rows, wide, sem = refs
+        parts.append(wide)
         for k in range(count):
-            unpack(packed[k], half_start(table_ref, first + k), places_ref, rows, parts[-1].at[k])
+            unpack(packed[k], half_start(table_ref, first + k), places_ref, rows, wide.at[k])
+        put = pltpu.make_async_copy(wide, dense_ref, sem)
+        put.start()
 
         @pl.loop(0, ROWS // STEP)
         def _(i):
@@ -228,6 +231,8 @@
                     at, total = at + 1, term if total is None else total + term
             sum_ref[part, :] = total
 
+        put.wait()
+
     return pl.pallas_call(
         kernel,
         out_shape=(
@@ -235,9 +240,13 @@
             jax.ShapeDtypeStruct((ROWS, 2 * W), F32),
         ),
         in_specs=[SMEM, SMEM] + [VMEM] * (count + 1 + len(lists)),
-        out_specs=(VMEM, VMEM),
-        scratch_shapes=[pltpu.VMEM((TILES, BR + 1, B, W), F32)],
-        compiler_params=params(8),
+        out_specs=(HBM, VMEM),
+        scratch_shapes=[
+            pltpu.VMEM((TILES, BR + 1, B, W), F32),
+            pltpu.VMEM((count, ROWS, HALF), BF16),
+            pltpu.SemaphoreType.DMA,
+        ],
+        compiler_params=params(12),
         cost_estimate=cost(16 * ROWS * HALF * W, 12 * MIB),
         name="product",
     )(table, places, *halves, right_side, *lists)
@@ -247,12 +256,15 @@
 
 
 def close_kernel(
-    table_ref, places_ref, packed_ref, right_ref, sum_ref, dense_ref, mine_ref, other_ref, rows
+    table_ref, places_ref, packed_ref, right_ref, sum_ref, dense_ref, mine_ref, other_ref, rows, wide, sem
 ):
-    unpack(packed_ref, half_start(table_ref, FIRST), places_ref, rows, dense_ref.at[0])
-    total = jnp.dot(dense_ref[0], right_ref[FIRST], preferred_element_type=F32) + sum_ref[...]
+    unpack(packed_ref, half_start(table_ref, FIRST), places_ref, rows, wide.at[0])
+    put = pltpu.make_async_copy(wide, dense_ref, sem)
+    put.start()
+    total = jnp.dot(wide[0], right_ref[FIRST], preferred_element_type=F32) + sum_ref[...]
     mine_ref[...] = total[:, :W]
     other_ref[...] = total[:, W:]
+    put.wait()
 
 
 def close(packed, table, places, right_side, total):
@@ -261,9 +273,13 @@
         out_shape=(jax.ShapeDtypeStruct((1, ROWS, HALF), BF16),)
         + (jax.ShapeDtypeStruct((ROWS, W), F32),) * 2,
         in_specs=[SMEM, SMEM, VMEM, VMEM, VMEM],
-        out_specs=(VMEM,) * 3,
-        scratch_shapes=[pltpu.VMEM((TILES, BR + 1, B, W), F32)],
-        compiler_params=params(8),
+        out_specs=(HBM, VMEM, VMEM),
+        scratch_shapes=[
+            pltpu.VMEM((TILES, BR + 1, B, W), F32),
+            pltpu.VMEM((1, ROWS, HALF), BF16),
+            pltpu.SemaphoreType.DMA,
+        ],
+        compiler_params=params(12),
         cost_estimate=cost(4 * ROWS * HALF * W, 3 * MIB),
         name="close",
     )(table, places, packed, right_side, total)
@@ -291,16 +307,25 @@
 
 
 def cube_kernel(table_ref, *refs):
-    *lists, square_ref, tile_ref, masks_ref, out_ref, acc = refs
+    *lists, square_hbm, tile_ref, masks_ref, out_ref, acc, square_ref, held, sems = refs
     scale = (NB / (KX * KSQ * B)) ** 0.5
-    at = 0
-    for ref in lists:
-        for k in range(ref.shape[0]):
-            g, core = table_ref[at], table_ref[at + 1]
+    first = pltpu.make_async_copy(square_hbm, square_ref, sems.at[len(lists)])
+    first.start()
+    fetches, begins, start = [], [], 0
+    for at, ref in enumerate(lists):
+        count = ref.shape[0]
+        fetches.append(pltpu.make_async_copy(ref, held.at[pl.ds(start, count)], sems.at[at]))
+        fetches[-1].start()
+        begins.append(start)
+        start += count
+    first.wait()
+    for ref, fetch, begin in zip(lists, fetches, begins):
+        fetch.wait()
+        for k in range(begin, begin + ref.shape[0]):
+            g, core = table_ref[2 * k], table_ref[2 * k + 1]
             half = square_ref[g, pl.ds(pl.multiple_of(core * HALF, HALF), HALF), :]
-            term = jnp.dot(ref[k], half, preferred_element_type=F32)
-            acc[...] = term if at == 0 else acc[...] + term
-            at += 2
+            term = jnp.dot(held[k], half, preferred_element_type=F32)
+            acc[...] = term if k == 0 else acc[...] + term
     for k in range(BR):
         rows = pl.ds(k * B, B)
         keep_x = jnp.broadcast_to(masks_ref[0, k : k + 1, :], (B, W))
@@ -314,10 +339,15 @@
     return pl.pallas_call(
         cube_kernel,
         out_shape=jax.ShapeDtypeStruct((ROWS, W), BF16),
-        in_specs=[SMEM] + [VMEM] * (len(lists) + 3),
+        in_specs=[SMEM] + [HBM] * (len(lists) + 1) + [VMEM] * 2,
         out_specs=VMEM,
-        scratch_shapes=[pltpu.VMEM((ROWS, W), F32)],
-        compiler_params=params(8),
+        scratch_shapes=[
+            pltpu.VMEM((ROWS, W), F32),
+            pltpu.VMEM((GROUPS, ROWS, W), BF16),
+            pltpu.VMEM((2 * (FIRST + 1), ROWS, HALF), BF16),
+            pltpu.SemaphoreType.DMA((len(lists) + 1,)),
+        ],
+        compiler_params=params(60),
         cost_estimate=cost(2 * GROUPS * ROWS * ROWS * W, 20 * MIB),
         name="cube",
     )(table, *lists, squares, tile, masks)

time: 155 us -> 149 us (0.961)
  local copies, waits for them, and re-layouts: 29.5 us -> 13.4 us
  Pallas kernels: 21.9 us -> 30.3 us
  waiting for transfers between devices: 43.5 us -> 45.8 us
    unnamed x56 -> x40, local copies, waits for them, and re-layouts: 29.4 us -> 13.3 us
    pallas_call x1, Pallas kernels: 5.73 us -> 13 us  [cube(): pl.pallas_call(cube_kernel, out_shape=jax.ShapeDtypeStruct((ROWS, W), BF1...]
    all_gather x1, waiting for transfers between devices: 24.1 us -> 26.4 us  [local(): squares = lax.all_gather(square, 'row', axis=0, tiled=False)]
where the time goes in v7:
time: 149 us; the launch traced here: 148 us
  waiting for transfers between devices  45.8 us (31%)
  starting transfers between devices  31 us (21%)
  Pallas kernels  30.3 us (20%)
  blocking collectives  13.9 us (9%)
  between operations  13.8 us (9%)
  local copies, waits for them, and re-layouts  13.4 us (9%)
    all_gather x1, waiting for transfers between devices, local(): squares = lax.all_gather(square, 'row', axis=0, tiled=False)  26.4 us
    ppermute x8, starting transfers between devices, across(): return lax.ppermute(piece, 'col', swap)  16.9 us
    ppermute x7, starting transfers between devices, along_y(): return lax.ppermute(piece, 'col', turn_y)  14.1 us
    all_to_all x1, blocking collectives, local(): a0 = lax.all_to_all(left, 'layer', 0, 0, tiled=True)  13.9 us
    unnamed x40, local copies, waits for them, and re-layouts  13.3 us
    pallas_call x1, Pallas kernels, cube(): pl.pallas_call(cube_kernel, out_shape=jax.ShapeDtypeStruct((ROWS, W), BF1...  13 us
    ppermute x7, waiting for transfers between devices, along_y(): return lax.ppermute(piece, 'col', turn_y)  12.4 us
    ppermute x8, waiting for transfers between devices, across(): return lax.ppermute(piece, 'col', swap)  6.99 us
  transfers between devices with their start and end apart: 17, of which 10 were waited for; matrix products, arithmetic and copies ran while one was open for 0% of the time, Pallas kernels for 9%

profile of v7, /device:TPU:2, one launch (start us, length us, event | category | flops | bytes accessed | tf_op | source)
XLA Modules:
  0.0 148.0 jit_solution(10073066218313820559)
XLA Ops:
  9.7 13.9 %all_to_all.5.refs_0_ = bf16[4,10,32,128]{3,2,1,0:T(8,128)(2,1)S(1)} all-to-all(bf16[4,10,32,128]{3,2,1,0:T(8,128)(2,1)S(1)} %get-tuple-element.19), channel_id=1, replica_groups=mesh['row'=8,'col'=16,'layer'=4] {'layer'}, dimensions={0} | all-to-all | bytes 655360 | tf_op jit(solution)/shard_map/all_to_all | solution.py:386
  23.5 1.9 %collective-permute-start.1 = (bf16[4,10,32,128]{3,2,1,0:T(8,128)(2,1)S(1)}, bf16[4,10,32,128]{3,2,1,0:T(8,128)(2,1)S(1)}, u32[]{:S(2)}, u32[]{:S(2)}) collective-permute-start(bf16[4,10,32,128]{3,2,1,0:T(8,128)(2,1)S(1)} %all_to_all.5.refs_0_), channel_id=1, source_target_pairs={{0,4},{4,0},{8,12},{12,8},{16,20},{20,16},{24,28},{28,24},{32,36},... | collective-permute-start | bytes 983048 | tf_op jit(solution)/shard_map/ppermute | solution.py:379
  25.4 1.9 %collective-permute-start = (bf16[4,10,32,128]{3,2,1,0:T(8,128)(2,1)S(1)}, bf16[4,10,32,128]{3,2,1,0:T(8,128)(2,1)}, u32[]{:S(2)}, u32[]{:S(2)}) collective-permute-start(bf16[4,10,32,128]{3,2,1,0:T(8,128)(2,1)S(1)} %all_to_all.5.refs_0_), channel_id=1, source_target_pairs={{0,8},{4,60},{8,16},{12,4},{16,24},{20,12},{24,32},{28,20},{32,40}... | collective-permute-start | bytes 983048 | tf_op jit(solution)/shard_map/ppermute | solution.py:376
  27.4 1.9 %collective-permute-start.2 = (bf16[4,10,32,128]{3,2,1,0:T(8,128)(2,1)S(1)}, bf16[4,10,32,128]{3,2,1,0:T(8,128)(2,1)}, u32[]{:S(2)}, u32[]{:S(2)}) collective-permute-start(bf16[4,10,32,128]{3,2,1,0:T(8,128)(2,1)S(1)} %collective-permute-done.1), channel_id=1, source_target_pairs={{0,8},{4,60},{8,16},{12,4},{16,24},{20,12},{24,32},{28,20},{32,40}... | collective-permute-start | bytes 983048 | tf_op jit(solution)/shard_map/ppermute | solution.py:376
  35.7 1.9 %collective-permute-start.3 = (bf16[4,10,32,128]{3,2,1,0:T(8,128)(2,1)}, bf16[4,10,32,128]{3,2,1,0:T(8,128)(2,1)S(1)}, u32[]{:S(2)}, u32[]{:S(2)}) collective-permute-start(bf16[4,10,32,128]{3,2,1,0:T(8,128)(2,1)} %collective-permute-done.refs_0_), channel_id=1, source_target_pairs={{0,8},{4,60},{8,16},{12,4},{16,24},{20,12},{24,32},{28,20},{32,40}... | collective-permute-start | bytes 983048 | tf_op jit(solution)/shard_map/ppermute | solution.py:376
  39.2 2.6 %collective-permute-start.4 = (bf16[4,10,32,128]{3,2,1,0:T(8,128)(2,1)}, bf16[4,10,32,128]{3,2,1,0:T(8,128)(2,1)S(1)}, u32[]{:S(2)}, u32[]{:S(2)}) collective-permute-start(bf16[4,10,32,128]{3,2,1,0:T(8,128)(2,1)} %collective-permute-done.2.refs_1_), channel_id=1, source_target_pairs={{0,8},{4,60},{8,16},{12,4},{16,24},{20,12},{24,32},{28,20},{32,40}... | collective-permute-start | bytes 983048 | tf_op jit(solution)/shard_map/ppermute | solution.py:376
  41.9 2.1 %widen.4.refs_4_.refs_1_ = bf16[2,1024,512]{2,1,0:T(8,128)(2,1)S(1)} custom-call(s32[32]{0:T(128)S(1)} %stack.68.table_ref, s32[10,256]{1,0:T(8,128)S(1)} %get-tuple-element.18.places_ref, bf16[4,10,32,128]{3,2,1,0:T(8,128)(2,1)} %collective-permute-done.refs_0_, bf16[4,10,32,128]{3,2,1,0:T(8,128)(2,1)} %collective-permute-done.2.refs_1_), custom_call_target="tpu_custom_call" | custom-call | flops 536870912 | bytes 6291456 | tf_op jit(solution)/shard_map/widen/pallas_call | solution.py:198
  43.9 2.2 %collective-permute-done.3.refs_0_ = bf16[4,10,32,128]{3,2,1,0:T(8,128)(2,1)S(1)} collective-permute-done((bf16[4,10,32,128]{3,2,1,0:T(8,128)(2,1)}, bf16[4,10,32,128]{3,2,1,0:T(8,128)(2,1)S(1)}, u32[]{:S(2)}, u32[]{:S(2)}) %collective-permute-start.3) | collective-permute-done | bytes 327712 | tf_op jit(solution)/shard_map/ppermute | solution.py:376
  46.1 1.9 %collective-permute-start.5 = (bf16[4,10,32,128]{3,2,1,0:T(8,128)(2,1)S(1)}, bf16[4,10,32,128]{3,2,1,0:T(8,128)(2,1)S(1)}, u32[]{:S(2)}, u32[]{:S(2)}) collective-permute-start(bf16[4,10,32,128]{3,2,1,0:T(8,128)(2,1)S(1)} %collective-permute-done.3.refs_0_), channel_id=1, source_target_pairs={{0,8},{4,60},{8,16},{12,4},{16,24},{20,12},{24,32},{28,20},{32,40}... | collective-permute-start | bytes 983048 | tf_op jit(solution)/shard_map/ppermute | solution.py:376
  49.6 1.9 %collective-permute-start.6 = (bf16[4,10,32,128]{3,2,1,0:T(8,128)(2,1)S(1)}, bf16[4,10,32,128]{3,2,1,0:T(8,128)(2,1)S(1)}, u32[]{:S(2)}, u32[]{:S(2)}) collective-permute-start(bf16[4,10,32,128]{3,2,1,0:T(8,128)(2,1)S(1)} %collective-permute-done.4.refs_1_), channel_id=1, source_target_pairs={{0,8},{4,60},{8,16},{12,4},{16,24},{20,12},{24,32},{28,20},{32,40}... | collective-permute-start | bytes 983048 | tf_op jit(solution)/shard_map/ppermute | solution.py:376
  56.3 3.5 %collective-permute-done.6.refs_1_ = bf16[4,10,32,128]{3,2,1,0:T(8,128)(2,1)S(1)} collective-permute-done((bf16[4,10,32,128]{3,2,1,0:T(8,128)(2,1)S(1)}, bf16[4,10,32,128]{3,2,1,0:T(8,128)(2,1)S(1)}, u32[]{:S(2)}, u32[]{:S(2)}) %collective-permute-start.6) | collective-permute-done | bytes 327712 | tf_op jit(solution)/shard_map/ppermute | solution.py:376
  60.5 2.0 %collective-permute-start.7 = (bf16[8,576,128]{2,1,0:T(8,128)(2,1)}, bf16[8,576,128]{2,1,0:T(8,128)(2,1)S(1)}, u32[]{:S(2)}, u32[]{:S(2)}) collective-permute-start(bf16[8,576,128]{2,1,0:T(8,128)(2,1)} %bitcast.14), channel_id=1, source_target_pairs={{0,4},{4,0},{8,12},{12,8},{16,20},{20,16},{24,28},{28,24},{32,36},... | collective-permute-start | bytes 3538952 | tf_op jit(solution)/shard_map/ppermute | solution.py:379
  62.5 1.9 %collective-permute-start.8 = (bf16[4,10,32,128]{3,2,1,0:T(8,128)(2,1)S(1)}, bf16[4,10,32,128]{3,2,1,0:T(8,128)(2,1)S(1)}, u32[]{:S(2)}, u32[]{:S(2)}) collective-permute-start(bf16[4,10,32,128]{3,2,1,0:T(8,128)(2,1)S(1)} %collective-permute-done.5.refs_0_), channel_id=1, source_target_pairs={{0,8},{4,60},{8,16},{12,4},{16,24},{20,12},{24,32},{28,20},{32,40}... | collective-permute-start | bytes 983048 | tf_op jit(solution)/shard_map/ppermute | solution.py:376
  66.8 2.8 %right.1.refs_2_.right_ref = bf16[8,512,256]{2,1,0:T(8,128)(2,1)S(1)} custom-call(s32[32]{0:T(128)S(1)} %stack.68.table_ref, bf16[8,576,128]{2,1,0:T(8,128)(2,1)S(1)} %bitcast.15, bf16[8,576,128]{2,1,0:T(8,128)(2,1)S(1)} %collective-permute-done.7.other_hbm), custom_call_target="tpu_custom_call" | custom-call | flops 40000000 | bytes 4194304 | tf_op jit(solution)/shard_map/right/pallas_call | solution.py:155
  69.6 4.5 %product.1 = (bf16[2,1024,512]{2,1,0:T(8,128)(2,1)S(1)}, f32[1024,256]{1,0:T(8,128)S(1)}) custom-call(s32[32]{0:T(128)S(1)} %stack.68.table_ref, s32[10,256]{1,0:T(8,128)S(1)} %get-tuple-element.18.places_ref, bf16[4,10,32,128]{3,2,1,0:T(8,128)(2,1)S(1)} %collective-permute-done.5.refs_0_, bf16[4,10,32,128]{3,2,1,0:T(8,128)(2,1)S(1)} %copy-done.10, ...), custom_call_target="tpu_custom_call" | custom-call | flops 1073741824 | bytes 12582912 | tf_op jit(solution)/shard_map/product/pallas_call | solution.py:236
  78.4 2.0 %collective-permute-start.14 = (f32[1024,128]{1,0:T(8,128)S(1)}, f32[1024,128]{1,0:T(8,128)S(1)}, u32[]{:S(2)}, u32[]{:S(2)}) collective-permute-start(f32[1024,128]{1,0:T(8,128)S(1)} %get-tuple-element.30), channel_id=1, source_target_pairs={{0,4},{4,0},{8,12},{12,8},{16,20},{20,16},{24,28},{28,24},{32,36},... | collective-permute-start | bytes 1572872 | tf_op jit(solution)/shard_map/ppermute | solution.py:379
  83.0 2.0 %collective-permute-start.10 = (bf16[2,1024,512]{2,1,0:T(8,128)(2,1)S(1)}, bf16[2,1024,512]{2,1,0:T(8,128)(2,1)S(1)}, u32[]{:S(2)}, u32[]{:S(2)}) collective-permute-start(bf16[2,1024,512]{2,1,0:T(8,128)(2,1)S(1)} %widen.4.refs_4_.refs_1_), channel_id=1, source_target_pairs={{0,4},{4,0},{8,12},{12,8},{16,20},{20,16},{24,28},{28,24},{32,36},... | collective-permute-start | bytes 6291464 | tf_op jit(solution)/shard_map/ppermute | solution.py:379
  85.1 2.3 %collective-permute-start.11 = (bf16[2,1024,512]{2,1,0:T(8,128)(2,1)}, bf16[2,1024,512]{2,1,0:T(8,128)(2,1)S(1)}, u32[]{:S(2)}, u32[]{:S(2)}) collective-permute-start(bf16[2,1024,512]{2,1,0:T(8,128)(2,1)} %copy-done.1), channel_id=1, source_target_pairs={{0,4},{4,0},{8,12},{12,8},{16,20},{20,16},{24,28},{28,24},{32,36},... | collective-permute-start | bytes 6291464 | tf_op jit(solution)/shard_map/ppermute | solution.py:379
  87.4 2.0 %collective-permute-start.12 = (bf16[2,1024,512]{2,1,0:T(8,128)(2,1)}, bf16[2,1024,512]{2,1,0:T(8,128)(2,1)}, u32[]{:S(2)}, u32[]{:S(2)}) collective-permute-start(bf16[2,1024,512]{2,1,0:T(8,128)(2,1)} %copy-done.4), channel_id=1, source_target_pairs={{0,4},{4,0},{8,12},{12,8},{16,20},{20,16},{24,28},{28,24},{32,36},... | collective-permute-start | bytes 6291464 | tf_op jit(solution)/shard_map/ppermute | solution.py:379
  89.4 2.3 %collective-permute-start.9 = (bf16[1,1024,512]{2,1,0:T(8,128)(2,1)S(1)}, bf16[1,1024,512]{2,1,0:T(8,128)(2,1)S(1)}, u32[]{:S(2)}, u32[]{:S(2)}) collective-permute-start(bf16[1,1024,512]{2,1,0:T(8,128)(2,1)S(1)} %widen.3.refs_3_.refs_0_), channel_id=1, source_target_pairs={{0,4},{4,0},{8,12},{12,8},{16,20},{20,16},{24,28},{28,24},{32,36},... | collective-permute-start | bytes 3145736 | tf_op jit(solution)/shard_map/ppermute | solution.py:379
  91.7 2.2 %collective-permute-start.13 = (bf16[1,1024,512]{2,1,0:T(8,128)(2,1)}, bf16[1,1024,512]{2,1,0:T(8,128)(2,1)S(1)}, u32[]{:S(2)}, u32[]{:S(2)}) collective-permute-start(bf16[1,1024,512]{2,1,0:T(8,128)(2,1)} %copy-done.7), channel_id=1, source_target_pairs={{0,4},{4,0},{8,12},{12,8},{16,20},{20,16},{24,28},{28,24},{32,36},... | collective-permute-start | bytes 3145736 | tf_op jit(solution)/shard_map/ppermute | solution.py:379
  94.0 4.1 %collective-permute-done.9.refs_5_ = bf16[1,1024,512]{2,1,0:T(8,128)(2,1)S(1)} collective-permute-done((bf16[1,1024,512]{2,1,0:T(8,128)(2,1)S(1)}, bf16[1,1024,512]{2,1,0:T(8,128)(2,1)S(1)}, u32[]{:S(2)}, u32[]{:S(2)}) %collective-permute-start.9) | collective-permute-done | bytes 1048608 | tf_op jit(solution)/shard_map/ppermute | solution.py:379
  101.8 26.4 %all-gather.7.cloned.1.call-done = bf16[8192,128]{1,0:T(8,128)(2,1)} async-done(((bf16[1024,128]{1,0:T(8,128)(2,1)}), bf16[8192,128]{1,0:T(8,128)(2,1)}) %all-gather.7.cloned.1.call-update) | async-done | bytes 2097168 | tf_op jit(solution)/shard_map/all_gather | solution.py:402
  128.2 13.0 %cube.1 = bf16[1024,128]{1,0:T(8,128)(2,1)} custom-call(s32[32]{0:T(128)} %copy-done.13, bf16[1,1024,512]{2,1,0:T(8,128)(2,1)} %copy-done.3, bf16[2,1024,512]{2,1,0:T(8,128)(2,1)} %copy-done, bf16[2,1024,512]{2,1,0:T(8,128)(2,1)} %copy-done.1, bf16[2,1024,512]{2,1,0:T(8,128)(2,1)} %copy-done.4, bf16[1,1024,512]{2,1,0:T(8,128)(2,1)} %copy-done.7, ...), custom_call_target="tpu_custom_call" | custom-call | flops 2147483648 | bytes 20971520 | tf_op jit(solution)/shard_map/cube/pallas_call | solution.py:339
  (64 shorter events, 31.0 us)
Async XLA Ops:
  6.5 54.0 %all-gather.5.cloned.1.call-start = ((), (), s32[]{:S(2)}) async-start(), calls=%async_computation.1 | async-start | bytes 1327104 | tf_op jit(solution)/shard_map/all_gather | solution.py:385
  9.6 118.6 %all-gather.7.cloned.1.call-start = ((), (), s32[]{:S(2)}) async-start(), calls=%async_computation.2 | async-start | bytes 2359296 | tf_op jit(solution)/shard_map/all_gather | solution.py:402
  23.5 3.8 %collective-permute-start.1 = (bf16[4,10,32,128]{3,2,1,0:T(8,128)(2,1)S(1)}, bf16[4,10,32,128]{3,2,1,0:T(8,128)(2,1)S(1)}, u32[]{:S(2)}, u32[]{:S(2)}) collective-permute-start(bf16[4,10,32,128]{3,2,1,0:T(8,128)(2,1)S(1)} %all_to_all.5.refs_0_), channel_id=1, source_target_pairs={{0,4},{4,0},{8,12},{12,8},{16,20},{20,16},{24,28},{28,24},{32,36},... | collective-permute-start | bytes 983048 | tf_op jit(solution)/shard_map/ppermute | solution.py:379
  25.4 10.3 %collective-permute-start = (bf16[4,10,32,128]{3,2,1,0:T(8,128)(2,1)S(1)}, bf16[4,10,32,128]{3,2,1,0:T(8,128)(2,1)}, u32[]{:S(2)}, u32[]{:S(2)}) collective-permute-start(bf16[4,10,32,128]{3,2,1,0:T(8,128)(2,1)S(1)} %all_to_all.5.refs_0_), channel_id=1, source_target_pairs={{0,8},{4,60},{8,16},{12,4},{16,24},{20,12},{24,32},{28,20},{32,40}... | collective-permute-start | bytes 983048 | tf_op jit(solution)/shard_map/ppermute | solution.py:376
  27.4 11.9 %collective-permute-start.2 = (bf16[4,10,32,128]{3,2,1,0:T(8,128)(2,1)S(1)}, bf16[4,10,32,128]{3,2,1,0:T(8,128)(2,1)}, u32[]{:S(2)}, u32[]{:S(2)}) collective-permute-start(bf16[4,10,32,128]{3,2,1,0:T(8,128)(2,1)S(1)} %collective-permute-done.1), channel_id=1, source_target_pairs={{0,8},{4,60},{8,16},{12,4},{16,24},{20,12},{24,32},{28,20},{32,40}... | collective-permute-start | bytes 983048 | tf_op jit(solution)/shard_map/ppermute | solution.py:376
  31.6 44.0 %copy-start.13 = (s32[32]{0:T(128)}, s32[32]{0:T(128)S(1)}, u32[]{:S(2)}) copy-start(s32[32]{0:T(128)S(1)} %stack.68.table_ref) | copy-start | bytes 388
  32.5 49.7 %copy-start.8 = (f32[3,32,128]{2,1,0:T(8,128)}, f32[3,32,128]{2,1,0:T(8,128)S(1)}, u32[]{:S(2)}) copy-start(f32[3,32,128]{2,1,0:T(8,128)S(1)} %masks.1.masks_ref.refs_12_) | copy-start | bytes 147460
  33.8 55.6 %copy-start.3 = (bf16[1,1024,512]{2,1,0:T(8,128)(2,1)}, bf16[1,1024,512]{2,1,0:T(8,128)(2,1)S(1)}, u32[]{:S(2)}) copy-start(bf16[1,1024,512]{2,1,0:T(8,128)(2,1)S(1)} %widen.3.refs_3_.refs_0_) | copy-start | bytes 3145732
  35.7 10.4 %collective-permute-start.3 = (bf16[4,10,32,128]{3,2,1,0:T(8,128)(2,1)}, bf16[4,10,32,128]{3,2,1,0:T(8,128)(2,1)S(1)}, u32[]{:S(2)}, u32[]{:S(2)}) collective-permute-start(bf16[4,10,32,128]{3,2,1,0:T(8,128)(2,1)} %collective-permute-done.refs_0_), channel_id=1, source_target_pairs={{0,8},{4,60},{8,16},{12,4},{16,24},{20,12},{24,32},{28,20},{32,40}... | collective-permute-start | bytes 983048 | tf_op jit(solution)/shard_map/ppermute | solution.py:376
  39.2 10.4 %collective-permute-start.4 = (bf16[4,10,32,128]{3,2,1,0:T(8,128)(2,1)}, bf16[4,10,32,128]{3,2,1,0:T(8,128)(2,1)S(1)}, u32[]{:S(2)}, u32[]{:S(2)}) collective-permute-start(bf16[4,10,32,128]{3,2,1,0:T(8,128)(2,1)} %collective-permute-done.2.refs_1_), channel_id=1, source_target_pairs={{0,8},{4,60},{8,16},{12,4},{16,24},{20,12},{24,32},{28,20},{32,40}... | collective-permute-start | bytes 983048 | tf_op jit(solution)/shard_map/ppermute | solution.py:376
  43.9 39.1 %copy-start = (bf16[2,1024,512]{2,1,0:T(8,128)(2,1)}, bf16[2,1024,512]{2,1,0:T(8,128)(2,1)S(1)}, u32[]{:S(2)}) copy-start(bf16[2,1024,512]{2,1,0:T(8,128)(2,1)S(1)} %widen.4.refs_4_.refs_1_) | copy-start | bytes 6291460
  46.1 10.2 %collective-permute-start.5 = (bf16[4,10,32,128]{3,2,1,0:T(8,128)(2,1)S(1)}, bf16[4,10,32,128]{3,2,1,0:T(8,128)(2,1)S(1)}, u32[]{:S(2)}, u32[]{:S(2)}) collective-permute-start(bf16[4,10,32,128]{3,2,1,0:T(8,128)(2,1)S(1)} %collective-permute-done.3.refs_0_), channel_id=1, source_target_pairs={{0,8},{4,60},{8,16},{12,4},{16,24},{20,12},{24,32},{28,20},{32,40}... | collective-permute-start | bytes 983048 | tf_op jit(solution)/shard_map/ppermute | solution.py:376
  49.6 10.2 %collective-permute-start.6 = (bf16[4,10,32,128]{3,2,1,0:T(8,128)(2,1)S(1)}, bf16[4,10,32,128]{3,2,1,0:T(8,128)(2,1)S(1)}, u32[]{:S(2)}, u32[]{:S(2)}) collective-permute-start(bf16[4,10,32,128]{3,2,1,0:T(8,128)(2,1)S(1)} %collective-permute-done.4.refs_1_), channel_id=1, source_target_pairs={{0,8},{4,60},{8,16},{12,4},{16,24},{20,12},{24,32},{28,20},{32,40}... | collective-permute-start | bytes 983048 | tf_op jit(solution)/shard_map/ppermute | solution.py:376
  60.5 9.1 %copy-start.2 = (bf16[2,1024,512]{2,1,0:T(8,128)(2,1)S(1)}, bf16[2,1024,512]{2,1,0:T(8,128)(2,1)}, u32[]{:S(2)}) copy-start(bf16[2,1024,512]{2,1,0:T(8,128)(2,1)} %copy-done.1) | copy-start | bytes 6291460
  60.5 5.1 %collective-permute-start.7 = (bf16[8,576,128]{2,1,0:T(8,128)(2,1)}, bf16[8,576,128]{2,1,0:T(8,128)(2,1)S(1)}, u32[]{:S(2)}, u32[]{:S(2)}) collective-permute-start(bf16[8,576,128]{2,1,0:T(8,128)(2,1)} %bitcast.14), channel_id=1, source_target_pairs={{0,4},{4,0},{8,12},{12,8},{16,20},{20,16},{24,28},{28,24},{32,36},... | collective-permute-start | bytes 3538952 | tf_op jit(solution)/shard_map/ppermute | solution.py:379
  62.5 13.0 %collective-permute-start.8 = (bf16[4,10,32,128]{3,2,1,0:T(8,128)(2,1)S(1)}, bf16[4,10,32,128]{3,2,1,0:T(8,128)(2,1)S(1)}, u32[]{:S(2)}, u32[]{:S(2)}) collective-permute-start(bf16[4,10,32,128]{3,2,1,0:T(8,128)(2,1)S(1)} %collective-permute-done.5.refs_0_), channel_id=1, source_target_pairs={{0,8},{4,60},{8,16},{12,4},{16,24},{20,12},{24,32},{28,20},{32,40}... | collective-permute-start | bytes 983048 | tf_op jit(solution)/shard_map/ppermute | solution.py:376
  66.8 2.8 %copy-start.10 = (bf16[4,10,32,128]{3,2,1,0:T(8,128)(2,1)S(1)}, bf16[4,10,32,128]{3,2,1,0:T(8,128)(2,1)}, u32[]{:S(2)}) copy-start(bf16[4,10,32,128]{3,2,1,0:T(8,128)(2,1)} %copy-done.9) | copy-start | bytes 983044
  78.4 3.8 %collective-permute-start.14 = (f32[1024,128]{1,0:T(8,128)S(1)}, f32[1024,128]{1,0:T(8,128)S(1)}, u32[]{:S(2)}, u32[]{:S(2)}) collective-permute-start(f32[1024,128]{1,0:T(8,128)S(1)} %get-tuple-element.30), channel_id=1, source_target_pairs={{0,4},{4,0},{8,12},{12,8},{16,20},{20,16},{24,28},{28,24},{32,36},... | collective-permute-start | bytes 1572872 | tf_op jit(solution)/shard_map/ppermute | solution.py:379
  83.0 15.1 %collective-permute-start.10 = (bf16[2,1024,512]{2,1,0:T(8,128)(2,1)S(1)}, bf16[2,1024,512]{2,1,0:T(8,128)(2,1)S(1)}, u32[]{:S(2)}, u32[]{:S(2)}) collective-permute-start(bf16[2,1024,512]{2,1,0:T(8,128)(2,1)S(1)} %widen.4.refs_4_.refs_1_), channel_id=1, source_target_pairs={{0,4},{4,0},{8,12},{12,8},{16,20},{20,16},{24,28},{28,24},{32,36},... | collective-permute-start | bytes 6291464 | tf_op jit(solution)/shard_map/ppermute | solution.py:379
  85.1 14.4 %collective-permute-start.11 = (bf16[2,1024,512]{2,1,0:T(8,128)(2,1)}, bf16[2,1024,512]{2,1,0:T(8,128)(2,1)S(1)}, u32[]{:S(2)}, u32[]{:S(2)}) collective-permute-start(bf16[2,1024,512]{2,1,0:T(8,128)(2,1)} %copy-done.1), channel_id=1, source_target_pairs={{0,4},{4,0},{8,12},{12,8},{16,20},{20,16},{24,28},{28,24},{32,36},... | collective-permute-start | bytes 6291464 | tf_op jit(solution)/shard_map/ppermute | solution.py:379
  87.4 14.5 %collective-permute-start.12 = (bf16[2,1024,512]{2,1,0:T(8,128)(2,1)}, bf16[2,1024,512]{2,1,0:T(8,128)(2,1)}, u32[]{:S(2)}, u32[]{:S(2)}) collective-permute-start(bf16[2,1024,512]{2,1,0:T(8,128)(2,1)} %copy-done.4), channel_id=1, source_target_pairs={{0,4},{4,0},{8,12},{12,8},{16,20},{20,16},{24,28},{28,24},{32,36},... | collective-permute-start | bytes 6291464 | tf_op jit(solution)/shard_map/ppermute | solution.py:379
  89.4 8.6 %collective-permute-start.9 = (bf16[1,1024,512]{2,1,0:T(8,128)(2,1)S(1)}, bf16[1,1024,512]{2,1,0:T(8,128)(2,1)S(1)}, u32[]{:S(2)}, u32[]{:S(2)}) collective-permute-start(bf16[1,1024,512]{2,1,0:T(8,128)(2,1)S(1)} %widen.3.refs_3_.refs_0_), channel_id=1, source_target_pairs={{0,4},{4,0},{8,12},{12,8},{16,20},{20,16},{24,28},{28,24},{32,36},... | collective-permute-start | bytes 3145736 | tf_op jit(solution)/shard_map/ppermute | solution.py:379
  91.7 9.1 %collective-permute-start.13 = (bf16[1,1024,512]{2,1,0:T(8,128)(2,1)}, bf16[1,1024,512]{2,1,0:T(8,128)(2,1)S(1)}, u32[]{:S(2)}, u32[]{:S(2)}) collective-permute-start(bf16[1,1024,512]{2,1,0:T(8,128)(2,1)} %copy-done.7), channel_id=1, source_target_pairs={{0,4},{4,0},{8,12},{12,8},{16,20},{20,16},{24,28},{28,24},{32,36},... | collective-permute-start | bytes 3145736 | tf_op jit(solution)/shard_map/ppermute | solution.py:379
  98.1 2.8 %copy-start.18 = (bf16[1,1024,512]{2,1,0:T(8,128)(2,1)}, bf16[1,1024,512]{2,1,0:T(8,128)(2,1)S(1)}, u32[]{:S(2)}) copy-start(bf16[1,1024,512]{2,1,0:T(8,128)(2,1)S(1)} %collective-permute-done.9.refs_5_) | copy-start | bytes 3145732
  (13 other events, 13.3 us)
Sparse Core Ops, SparseCore 0:
  9.7 46.9 all-gather.4
  83.1 45.0 all-gather.6

commit v8 on v7

--- a/solution.py
+++ b/solution.py
@@ -306,6 +306,9 @@
     )(mine, other, masks)
 
 
+AHEAD = 2
+
+
 def cube_kernel(table_ref, *refs):
     *lists, square_hbm, tile_ref, masks_ref, out_ref, acc, square_ref, held, sems = refs
     scale = (NB / (KX * KSQ * B)) ** 0.5
@@ -315,12 +318,15 @@
     for at, ref in enumerate(lists):
         count = ref.shape[0]
         fetches.append(pltpu.make_async_copy(ref, held.at[pl.ds(start, count)], sems.at[at]))
-        fetches[-1].start()
         begins.append(start)
         start += count
+    for fetch in fetches[:AHEAD]:
+        fetch.start()
     first.wait()
-    for ref, fetch, begin in zip(lists, fetches, begins):
+    for at, (ref, fetch, begin) in enumerate(zip(lists, fetches, begins)):
         fetch.wait()
+        if at + AHEAD < len(fetches):
+            fetches[at + AHEAD].start()
         for k in range(begin, begin + ref.shape[0]):
             g, core = table_ref[2 * k], table_ref[2 * k + 1]
             half = square_ref[g, pl.ds(pl.multiple_of(core * HALF, HALF), HALF), :]

time: 149 us -> 149 us (level)
  no operation moved by 1% of the time
where the time goes in v8:
time: 149 us; the launch traced here: 148 us
  waiting for transfers between devices  45.8 us (31%)
  starting transfers between devices  31 us (21%)
  Pallas kernels  30.6 us (21%)
  blocking collectives  13.9 us (9%)
  between operations  13.8 us (9%)
  local copies, waits for them, and re-layouts  13.4 us (9%)
    all_gather x1, waiting for transfers between devices, local(): squares = lax.all_gather(square, 'row', axis=0, tiled=False)  26.4 us
    ppermute x8, starting transfers between devices, across(): return lax.ppermute(piece, 'col', swap)  16.9 us
    ppermute x7, starting transfers between devices, along_y(): return lax.ppermute(piece, 'col', turn_y)  14.1 us
    all_to_all x1, blocking collectives, local(): a0 = lax.all_to_all(left, 'layer', 0, 0, tiled=True)  13.9 us
    pallas_call x1, Pallas kernels, cube(): pl.pallas_call(cube_kernel, out_shape=jax.ShapeDtypeStruct((ROWS, W), BF1...  13.3 us
    unnamed x40, local copies, waits for them, and re-layouts  13.3 us
    ppermute x7, waiting for transfers between devices, along_y(): return lax.ppermute(piece, 'col', turn_y)  12.4 us
    ppermute x8, waiting for transfers between devices, across(): return lax.ppermute(piece, 'col', swap)  6.99 us
  transfers between devices with their start and end apart: 17, of which 10 were waited for; matrix products, arithmetic and copies ran while one was open for 0% of the time, Pallas kernels for 9%

profile of v8, /device:TPU:2, one launch (start us, length us, event | category | flops | bytes accessed | tf_op | source)
XLA Modules:
  0.0 148.4 jit_solution(12314752398507028393)
XLA Ops:
  9.7 13.9 %all_to_all.5.refs_0_ = bf16[4,10,32,128]{3,2,1,0:T(8,128)(2,1)S(1)} all-to-all(bf16[4,10,32,128]{3,2,1,0:T(8,128)(2,1)S(1)} %get-tuple-element.19), channel_id=1, replica_groups=mesh['row'=8,'col'=16,'layer'=4] {'layer'}, dimensions={0} | all-to-all | bytes 655360 | tf_op jit(solution)/shard_map/all_to_all | solution.py:392
  23.5 1.9 %collective-permute-start.1 = (bf16[4,10,32,128]{3,2,1,0:T(8,128)(2,1)S(1)}, bf16[4,10,32,128]{3,2,1,0:T(8,128)(2,1)S(1)}, u32[]{:S(2)}, u32[]{:S(2)}) collective-permute-start(bf16[4,10,32,128]{3,2,1,0:T(8,128)(2,1)S(1)} %all_to_all.5.refs_0_), channel_id=1, source_target_pairs={{0,4},{4,0},{8,12},{12,8},{16,20},{20,16},{24,28},{28,24},{32,36},... | collective-permute-start | bytes 983048 | tf_op jit(solution)/shard_map/ppermute | solution.py:385
  25.4 1.9 %collective-permute-start = (bf16[4,10,32,128]{3,2,1,0:T(8,128)(2,1)S(1)}, bf16[4,10,32,128]{3,2,1,0:T(8,128)(2,1)}, u32[]{:S(2)}, u32[]{:S(2)}) collective-permute-start(bf16[4,10,32,128]{3,2,1,0:T(8,128)(2,1)S(1)} %all_to_all.5.refs_0_), channel_id=1, source_target_pairs={{0,8},{4,60},{8,16},{12,4},{16,24},{20,12},{24,32},{28,20},{32,40}... | collective-permute-start | bytes 983048 | tf_op jit(solution)/shard_map/ppermute | solution.py:382
  27.4 1.9 %collective-permute-start.2 = (bf16[4,10,32,128]{3,2,1,0:T(8,128)(2,1)S(1)}, bf16[4,10,32,128]{3,2,1,0:T(8,128)(2,1)}, u32[]{:S(2)}, u32[]{:S(2)}) collective-permute-start(bf16[4,10,32,128]{3,2,1,0:T(8,128)(2,1)S(1)} %collective-permute-done.1), channel_id=1, source_target_pairs={{0,8},{4,60},{8,16},{12,4},{16,24},{20,12},{24,32},{28,20},{32,40}... | collective-permute-start | bytes 983048 | tf_op jit(solution)/shard_map/ppermute | solution.py:382
  35.7 1.9 %collective-permute-start.3 = (bf16[4,10,32,128]{3,2,1,0:T(8,128)(2,1)}, bf16[4,10,32,128]{3,2,1,0:T(8,128)(2,1)S(1)}, u32[]{:S(2)}, u32[]{:S(2)}) collective-permute-start(bf16[4,10,32,128]{3,2,1,0:T(8,128)(2,1)} %collective-permute-done.refs_0_), channel_id=1, source_target_pairs={{0,8},{4,60},{8,16},{12,4},{16,24},{20,12},{24,32},{28,20},{32,40}... | collective-permute-start | bytes 983048 | tf_op jit(solution)/shard_map/ppermute | solution.py:382
  39.2 2.6 %collective-permute-start.4 = (bf16[4,10,32,128]{3,2,1,0:T(8,128)(2,1)}, bf16[4,10,32,128]{3,2,1,0:T(8,128)(2,1)S(1)}, u32[]{:S(2)}, u32[]{:S(2)}) collective-permute-start(bf16[4,10,32,128]{3,2,1,0:T(8,128)(2,1)} %collective-permute-done.2.refs_1_), channel_id=1, source_target_pairs={{0,8},{4,60},{8,16},{12,4},{16,24},{20,12},{24,32},{28,20},{32,40}... | collective-permute-start | bytes 983048 | tf_op jit(solution)/shard_map/ppermute | solution.py:382
  41.9 2.1 %widen.4.refs_4_.refs_1_ = bf16[2,1024,512]{2,1,0:T(8,128)(2,1)S(1)} custom-call(s32[32]{0:T(128)S(1)} %stack.68.table_ref, s32[10,256]{1,0:T(8,128)S(1)} %get-tuple-element.18.places_ref, bf16[4,10,32,128]{3,2,1,0:T(8,128)(2,1)} %collective-permute-done.refs_0_, bf16[4,10,32,128]{3,2,1,0:T(8,128)(2,1)} %collective-permute-done.2.refs_1_), custom_call_target="tpu_custom_call" | custom-call | flops 536870912 | bytes 6291456 | tf_op jit(solution)/shard_map/widen/pallas_call | solution.py:198
  43.9 2.2 %collective-permute-done.3.refs_0_ = bf16[4,10,32,128]{3,2,1,0:T(8,128)(2,1)S(1)} collective-permute-done((bf16[4,10,32,128]{3,2,1,0:T(8,128)(2,1)}, bf16[4,10,32,128]{3,2,1,0:T(8,128)(2,1)S(1)}, u32[]{:S(2)}, u32[]{:S(2)}) %collective-permute-start.3) | collective-permute-done | bytes 327712 | tf_op jit(solution)/shard_map/ppermute | solution.py:382
  46.1 1.9 %collective-permute-start.5 = (bf16[4,10,32,128]{3,2,1,0:T(8,128)(2,1)S(1)}, bf16[4,10,32,128]{3,2,1,0:T(8,128)(2,1)S(1)}, u32[]{:S(2)}, u32[]{:S(2)}) collective-permute-start(bf16[4,10,32,128]{3,2,1,0:T(8,128)(2,1)S(1)} %collective-permute-done.3.refs_0_), channel_id=1, source_target_pairs={{0,8},{4,60},{8,16},{12,4},{16,24},{20,12},{24,32},{28,20},{32,40}... | collective-permute-start | bytes 983048 | tf_op jit(solution)/shard_map/ppermute | solution.py:382
  49.6 1.9 %collective-permute-start.6 = (bf16[4,10,32,128]{3,2,1,0:T(8,128)(2,1)S(1)}, bf16[4,10,32,128]{3,2,1,0:T(8,128)(2,1)S(1)}, u32[]{:S(2)}, u32[]{:S(2)}) collective-permute-start(bf16[4,10,32,128]{3,2,1,0:T(8,128)(2,1)S(1)} %collective-permute-done.4.refs_1_), channel_id=1, source_target_pairs={{0,8},{4,60},{8,16},{12,4},{16,24},{20,12},{24,32},{28,20},{32,40}... | collective-permute-start | bytes 983048 | tf_op jit(solution)/shard_map/ppermute | solution.py:382
  56.3 3.5 %collective-permute-done.6.refs_1_ = bf16[4,10,32,128]{3,2,1,0:T(8,128)(2,1)S(1)} collective-permute-done((bf16[4,10,32,128]{3,2,1,0:T(8,128)(2,1)S(1)}, bf16[4,10,32,128]{3,2,1,0:T(8,128)(2,1)S(1)}, u32[]{:S(2)}, u32[]{:S(2)}) %collective-permute-start.6) | collective-permute-done | bytes 327712 | tf_op jit(solution)/shard_map/ppermute | solution.py:382
  60.5 2.0 %collective-permute-start.7 = (bf16[8,576,128]{2,1,0:T(8,128)(2,1)}, bf16[8,576,128]{2,1,0:T(8,128)(2,1)S(1)}, u32[]{:S(2)}, u32[]{:S(2)}) collective-permute-start(bf16[8,576,128]{2,1,0:T(8,128)(2,1)} %bitcast.14), channel_id=1, source_target_pairs={{0,4},{4,0},{8,12},{12,8},{16,20},{20,16},{24,28},{28,24},{32,36},... | collective-permute-start | bytes 3538952 | tf_op jit(solution)/shard_map/ppermute | solution.py:385
  62.5 1.9 %collective-permute-start.8 = (bf16[4,10,32,128]{3,2,1,0:T(8,128)(2,1)S(1)}, bf16[4,10,32,128]{3,2,1,0:T(8,128)(2,1)S(1)}, u32[]{:S(2)}, u32[]{:S(2)}) collective-permute-start(bf16[4,10,32,128]{3,2,1,0:T(8,128)(2,1)S(1)} %collective-permute-done.5.refs_0_), channel_id=1, source_target_pairs={{0,8},{4,60},{8,16},{12,4},{16,24},{20,12},{24,32},{28,20},{32,40}... | collective-permute-start | bytes 983048 | tf_op jit(solution)/shard_map/ppermute | solution.py:382
  66.8 2.8 %right.1.refs_2_.right_ref = bf16[8,512,256]{2,1,0:T(8,128)(2,1)S(1)} custom-call(s32[32]{0:T(128)S(1)} %stack.68.table_ref, bf16[8,576,128]{2,1,0:T(8,128)(2,1)S(1)} %bitcast.15, bf16[8,576,128]{2,1,0:T(8,128)(2,1)S(1)} %collective-permute-done.7.other_hbm), custom_call_target="tpu_custom_call" | custom-call | flops 40000000 | bytes 4194304 | tf_op jit(solution)/shard_map/right/pallas_call | solution.py:155
  69.6 4.5 %product.1 = (bf16[2,1024,512]{2,1,0:T(8,128)(2,1)S(1)}, f32[1024,256]{1,0:T(8,128)S(1)}) custom-call(s32[32]{0:T(128)S(1)} %stack.68.table_ref, s32[10,256]{1,0:T(8,128)S(1)} %get-tuple-element.18.places_ref, bf16[4,10,32,128]{3,2,1,0:T(8,128)(2,1)S(1)} %collective-permute-done.5.refs_0_, bf16[4,10,32,128]{3,2,1,0:T(8,128)(2,1)S(1)} %copy-done.10, ...), custom_call_target="tpu_custom_call" | custom-call | flops 1073741824 | bytes 12582912 | tf_op jit(solution)/shard_map/product/pallas_call | solution.py:236
  78.4 2.0 %collective-permute-start.14 = (f32[1024,128]{1,0:T(8,128)S(1)}, f32[1024,128]{1,0:T(8,128)S(1)}, u32[]{:S(2)}, u32[]{:S(2)}) collective-permute-start(f32[1024,128]{1,0:T(8,128)S(1)} %get-tuple-element.30), channel_id=1, source_target_pairs={{0,4},{4,0},{8,12},{12,8},{16,20},{20,16},{24,28},{28,24},{32,36},... | collective-permute-start | bytes 1572872 | tf_op jit(solution)/shard_map/ppermute | solution.py:385
  83.0 2.0 %collective-permute-start.10 = (bf16[2,1024,512]{2,1,0:T(8,128)(2,1)S(1)}, bf16[2,1024,512]{2,1,0:T(8,128)(2,1)S(1)}, u32[]{:S(2)}, u32[]{:S(2)}) collective-permute-start(bf16[2,1024,512]{2,1,0:T(8,128)(2,1)S(1)} %widen.4.refs_4_.refs_1_), channel_id=1, source_target_pairs={{0,4},{4,0},{8,12},{12,8},{16,20},{20,16},{24,28},{28,24},{32,36},... | collective-permute-start | bytes 6291464 | tf_op jit(solution)/shard_map/ppermute | solution.py:385
  85.1 2.3 %collective-permute-start.11 = (bf16[2,1024,512]{2,1,0:T(8,128)(2,1)}, bf16[2,1024,512]{2,1,0:T(8,128)(2,1)S(1)}, u32[]{:S(2)}, u32[]{:S(2)}) collective-permute-start(bf16[2,1024,512]{2,1,0:T(8,128)(2,1)} %copy-done.1), channel_id=1, source_target_pairs={{0,4},{4,0},{8,12},{12,8},{16,20},{20,16},{24,28},{28,24},{32,36},... | collective-permute-start | bytes 6291464 | tf_op jit(solution)/shard_map/ppermute | solution.py:385
  87.4 2.0 %collective-permute-start.12 = (bf16[2,1024,512]{2,1,0:T(8,128)(2,1)}, bf16[2,1024,512]{2,1,0:T(8,128)(2,1)}, u32[]{:S(2)}, u32[]{:S(2)}) collective-permute-start(bf16[2,1024,512]{2,1,0:T(8,128)(2,1)} %copy-done.4), channel_id=1, source_target_pairs={{0,4},{4,0},{8,12},{12,8},{16,20},{20,16},{24,28},{28,24},{32,36},... | collective-permute-start | bytes 6291464 | tf_op jit(solution)/shard_map/ppermute | solution.py:385
  89.4 2.3 %collective-permute-start.9 = (bf16[1,1024,512]{2,1,0:T(8,128)(2,1)S(1)}, bf16[1,1024,512]{2,1,0:T(8,128)(2,1)S(1)}, u32[]{:S(2)}, u32[]{:S(2)}) collective-permute-start(bf16[1,1024,512]{2,1,0:T(8,128)(2,1)S(1)} %widen.3.refs_3_.refs_0_), channel_id=1, source_target_pairs={{0,4},{4,0},{8,12},{12,8},{16,20},{20,16},{24,28},{28,24},{32,36},... | collective-permute-start | bytes 3145736 | tf_op jit(solution)/shard_map/ppermute | solution.py:385
  91.7 2.2 %collective-permute-start.13 = (bf16[1,1024,512]{2,1,0:T(8,128)(2,1)}, bf16[1,1024,512]{2,1,0:T(8,128)(2,1)S(1)}, u32[]{:S(2)}, u32[]{:S(2)}) collective-permute-start(bf16[1,1024,512]{2,1,0:T(8,128)(2,1)} %copy-done.7), channel_id=1, source_target_pairs={{0,4},{4,0},{8,12},{12,8},{16,20},{20,16},{24,28},{28,24},{32,36},... | collective-permute-start | bytes 3145736 | tf_op jit(solution)/shard_map/ppermute | solution.py:385
  94.0 4.1 %collective-permute-done.9.refs_5_ = bf16[1,1024,512]{2,1,0:T(8,128)(2,1)S(1)} collective-permute-done((bf16[1,1024,512]{2,1,0:T(8,128)(2,1)S(1)}, bf16[1,1024,512]{2,1,0:T(8,128)(2,1)S(1)}, u32[]{:S(2)}, u32[]{:S(2)}) %collective-permute-start.9) | collective-permute-done | bytes 1048608 | tf_op jit(solution)/shard_map/ppermute | solution.py:385
  101.8 26.4 %all-gather.7.cloned.1.call-done = bf16[8192,128]{1,0:T(8,128)(2,1)} async-done(((bf16[1024,128]{1,0:T(8,128)(2,1)}), bf16[8192,128]{1,0:T(8,128)(2,1)}) %all-gather.7.cloned.1.call-update) | async-done | bytes 2097168 | tf_op jit(solution)/shard_map/all_gather | solution.py:408
  128.2 13.3 %cube.1 = bf16[1024,128]{1,0:T(8,128)(2,1)} custom-call(s32[32]{0:T(128)} %copy-done.13, bf16[1,1024,512]{2,1,0:T(8,128)(2,1)} %copy-done.3, bf16[2,1024,512]{2,1,0:T(8,128)(2,1)} %copy-done, bf16[2,1024,512]{2,1,0:T(8,128)(2,1)} %copy-done.1, bf16[2,1024,512]{2,1,0:T(8,128)(2,1)} %copy-done.4, bf16[1,1024,512]{2,1,0:T(8,128)(2,1)} %copy-done.7, ...), custom_call_target="tpu_custom_call" | custom-call | flops 2147483648 | bytes 20971520 | tf_op jit(solution)/shard_map/cube/pallas_call | solution.py:345
  (64 shorter events, 31.0 us)
Async XLA Ops:
  6.5 54.0 %all-gather.5.cloned.1.call-start = ((), (), s32[]{:S(2)}) async-start(), calls=%async_computation.1 | async-start | bytes 1327104 | tf_op jit(solution)/shard_map/all_gather | solution.py:391
  9.6 118.6 %all-gather.7.cloned.1.call-start = ((), (), s32[]{:S(2)}) async-start(), calls=%async_computation.2 | async-start | bytes 2359296 | tf_op jit(solution)/shard_map/all_gather | solution.py:408
  23.5 3.8 %collective-permute-start.1 = (bf16[4,10,32,128]{3,2,1,0:T(8,128)(2,1)S(1)}, bf16[4,10,32,128]{3,2,1,0:T(8,128)(2,1)S(1)}, u32[]{:S(2)}, u32[]{:S(2)}) collective-permute-start(bf16[4,10,32,128]{3,2,1,0:T(8,128)(2,1)S(1)} %all_to_all.5.refs_0_), channel_id=1, source_target_pairs={{0,4},{4,0},{8,12},{12,8},{16,20},{20,16},{24,28},{28,24},{32,36},... | collective-permute-start | bytes 983048 | tf_op jit(solution)/shard_map/ppermute | solution.py:385
  25.4 10.3 %collective-permute-start = (bf16[4,10,32,128]{3,2,1,0:T(8,128)(2,1)S(1)}, bf16[4,10,32,128]{3,2,1,0:T(8,128)(2,1)}, u32[]{:S(2)}, u32[]{:S(2)}) collective-permute-start(bf16[4,10,32,128]{3,2,1,0:T(8,128)(2,1)S(1)} %all_to_all.5.refs_0_), channel_id=1, source_target_pairs={{0,8},{4,60},{8,16},{12,4},{16,24},{20,12},{24,32},{28,20},{32,40}... | collective-permute-start | bytes 983048 | tf_op jit(solution)/shard_map/ppermute | solution.py:382
  27.4 11.9 %collective-permute-start.2 = (bf16[4,10,32,128]{3,2,1,0:T(8,128)(2,1)S(1)}, bf16[4,10,32,128]{3,2,1,0:T(8,128)(2,1)}, u32[]{:S(2)}, u32[]{:S(2)}) collective-permute-start(bf16[4,10,32,128]{3,2,1,0:T(8,128)(2,1)S(1)} %collective-permute-done.1), channel_id=1, source_target_pairs={{0,8},{4,60},{8,16},{12,4},{16,24},{20,12},{24,32},{28,20},{32,40}... | collective-permute-start | bytes 983048 | tf_op jit(solution)/shard_map/ppermute | solution.py:382
  31.6 44.0 %copy-start.13 = (s32[32]{0:T(128)}, s32[32]{0:T(128)S(1)}, u32[]{:S(2)}) copy-start(s32[32]{0:T(128)S(1)} %stack.68.table_ref) | copy-start | bytes 388
  32.5 49.7 %copy-start.8 = (f32[3,32,128]{2,1,0:T(8,128)}, f32[3,32,128]{2,1,0:T(8,128)S(1)}, u32[]{:S(2)}) copy-start(f32[3,32,128]{2,1,0:T(8,128)S(1)} %masks.1.masks_ref.refs_12_) | copy-start | bytes 147460
  33.8 55.6 %copy-start.3 = (bf16[1,1024,512]{2,1,0:T(8,128)(2,1)}, bf16[1,1024,512]{2,1,0:T(8,128)(2,1)S(1)}, u32[]{:S(2)}) copy-start(bf16[1,1024,512]{2,1,0:T(8,128)(2,1)S(1)} %widen.3.refs_3_.refs_0_) | copy-start | bytes 3145732
  35.7 10.4 %collective-permute-start.3 = (bf16[4,10,32,128]{3,2,1,0:T(8,128)(2,1)}, bf16[4,10,32,128]{3,2,1,0:T(8,128)(2,1)S(1)}, u32[]{:S(2)}, u32[]{:S(2)}) collective-permute-start(bf16[4,10,32,128]{3,2,1,0:T(8,128)(2,1)} %collective-permute-done.refs_0_), channel_id=1, source_target_pairs={{0,8},{4,60},{8,16},{12,4},{16,24},{20,12},{24,32},{28,20},{32,40}... | collective-permute-start | bytes 983048 | tf_op jit(solution)/shard_map/ppermute | solution.py:382
  39.2 10.4 %collective-permute-start.4 = (bf16[4,10,32,128]{3,2,1,0:T(8,128)(2,1)}, bf16[4,10,32,128]{3,2,1,0:T(8,128)(2,1)S(1)}, u32[]{:S(2)}, u32[]{:S(2)}) collective-permute-start(bf16[4,10,32,128]{3,2,1,0:T(8,128)(2,1)} %collective-permute-done.2.refs_1_), channel_id=1, source_target_pairs={{0,8},{4,60},{8,16},{12,4},{16,24},{20,12},{24,32},{28,20},{32,40}... | collective-permute-start | bytes 983048 | tf_op jit(solution)/shard_map/ppermute | solution.py:382
  43.9 39.1 %copy-start = (bf16[2,1024,512]{2,1,0:T(8,128)(2,1)}, bf16[2,1024,512]{2,1,0:T(8,128)(2,1)S(1)}, u32[]{:S(2)}) copy-start(bf16[2,1024,512]{2,1,0:T(8,128)(2,1)S(1)} %widen.4.refs_4_.refs_1_) | copy-start | bytes 6291460
  46.1 10.2 %collective-permute-start.5 = (bf16[4,10,32,128]{3,2,1,0:T(8,128)(2,1)S(1)}, bf16[4,10,32,128]{3,2,1,0:T(8,128)(2,1)S(1)}, u32[]{:S(2)}, u32[]{:S(2)}) collective-permute-start(bf16[4,10,32,128]{3,2,1,0:T(8,128)(2,1)S(1)} %collective-permute-done.3.refs_0_), channel_id=1, source_target_pairs={{0,8},{4,60},{8,16},{12,4},{16,24},{20,12},{24,32},{28,20},{32,40}... | collective-permute-start | bytes 983048 | tf_op jit(solution)/shard_map/ppermute | solution.py:382
  49.6 10.2 %collective-permute-start.6 = (bf16[4,10,32,128]{3,2,1,0:T(8,128)(2,1)S(1)}, bf16[4,10,32,128]{3,2,1,0:T(8,128)(2,1)S(1)}, u32[]{:S(2)}, u32[]{:S(2)}) collective-permute-start(bf16[4,10,32,128]{3,2,1,0:T(8,128)(2,1)S(1)} %collective-permute-done.4.refs_1_), channel_id=1, source_target_pairs={{0,8},{4,60},{8,16},{12,4},{16,24},{20,12},{24,32},{28,20},{32,40}... | collective-permute-start | bytes 983048 | tf_op jit(solution)/shard_map/ppermute | solution.py:382
  60.5 9.1 %copy-start.2 = (bf16[2,1024,512]{2,1,0:T(8,128)(2,1)S(1)}, bf16[2,1024,512]{2,1,0:T(8,128)(2,1)}, u32[]{:S(2)}) copy-start(bf16[2,1024,512]{2,1,0:T(8,128)(2,1)} %copy-done.1) | copy-start | bytes 6291460
  60.5 5.1 %collective-permute-start.7 = (bf16[8,576,128]{2,1,0:T(8,128)(2,1)}, bf16[8,576,128]{2,1,0:T(8,128)(2,1)S(1)}, u32[]{:S(2)}, u32[]{:S(2)}) collective-permute-start(bf16[8,576,128]{2,1,0:T(8,128)(2,1)} %bitcast.14), channel_id=1, source_target_pairs={{0,4},{4,0},{8,12},{12,8},{16,20},{20,16},{24,28},{28,24},{32,36},... | collective-permute-start | bytes 3538952 | tf_op jit(solution)/shard_map/ppermute | solution.py:385
  62.5 13.0 %collective-permute-start.8 = (bf16[4,10,32,128]{3,2,1,0:T(8,128)(2,1)S(1)}, bf16[4,10,32,128]{3,2,1,0:T(8,128)(2,1)S(1)}, u32[]{:S(2)}, u32[]{:S(2)}) collective-permute-start(bf16[4,10,32,128]{3,2,1,0:T(8,128)(2,1)S(1)} %collective-permute-done.5.refs_0_), channel_id=1, source_target_pairs={{0,8},{4,60},{8,16},{12,4},{16,24},{20,12},{24,32},{28,20},{32,40}... | collective-permute-start | bytes 983048 | tf_op jit(solution)/shard_map/ppermute | solution.py:382
  66.8 2.8 %copy-start.10 = (bf16[4,10,32,128]{3,2,1,0:T(8,128)(2,1)S(1)}, bf16[4,10,32,128]{3,2,1,0:T(8,128)(2,1)}, u32[]{:S(2)}) copy-start(bf16[4,10,32,128]{3,2,1,0:T(8,128)(2,1)} %copy-done.9) | copy-start | bytes 983044
  78.4 3.8 %collective-permute-start.14 = (f32[1024,128]{1,0:T(8,128)S(1)}, f32[1024,128]{1,0:T(8,128)S(1)}, u32[]{:S(2)}, u32[]{:S(2)}) collective-permute-start(f32[1024,128]{1,0:T(8,128)S(1)} %get-tuple-element.30), channel_id=1, source_target_pairs={{0,4},{4,0},{8,12},{12,8},{16,20},{20,16},{24,28},{28,24},{32,36},... | collective-permute-start | bytes 1572872 | tf_op jit(solution)/shard_map/ppermute | solution.py:385
  83.0 15.1 %collective-permute-start.10 = (bf16[2,1024,512]{2,1,0:T(8,128)(2,1)S(1)}, bf16[2,1024,512]{2,1,0:T(8,128)(2,1)S(1)}, u32[]{:S(2)}, u32[]{:S(2)}) collective-permute-start(bf16[2,1024,512]{2,1,0:T(8,128)(2,1)S(1)} %widen.4.refs_4_.refs_1_), channel_id=1, source_target_pairs={{0,4},{4,0},{8,12},{12,8},{16,20},{20,16},{24,28},{28,24},{32,36},... | collective-permute-start | bytes 6291464 | tf_op jit(solution)/shard_map/ppermute | solution.py:385
  85.1 14.4 %collective-permute-start.11 = (bf16[2,1024,512]{2,1,0:T(8,128)(2,1)}, bf16[2,1024,512]{2,1,0:T(8,128)(2,1)S(1)}, u32[]{:S(2)}, u32[]{:S(2)}) collective-permute-start(bf16[2,1024,512]{2,1,0:T(8,128)(2,1)} %copy-done.1), channel_id=1, source_target_pairs={{0,4},{4,0},{8,12},{12,8},{16,20},{20,16},{24,28},{28,24},{32,36},... | collective-permute-start | bytes 6291464 | tf_op jit(solution)/shard_map/ppermute | solution.py:385
  87.4 14.5 %collective-permute-start.12 = (bf16[2,1024,512]{2,1,0:T(8,128)(2,1)}, bf16[2,1024,512]{2,1,0:T(8,128)(2,1)}, u32[]{:S(2)}, u32[]{:S(2)}) collective-permute-start(bf16[2,1024,512]{2,1,0:T(8,128)(2,1)} %copy-done.4), channel_id=1, source_target_pairs={{0,4},{4,0},{8,12},{12,8},{16,20},{20,16},{24,28},{28,24},{32,36},... | collective-permute-start | bytes 6291464 | tf_op jit(solution)/shard_map/ppermute | solution.py:385
  89.4 8.6 %collective-permute-start.9 = (bf16[1,1024,512]{2,1,0:T(8,128)(2,1)S(1)}, bf16[1,1024,512]{2,1,0:T(8,128)(2,1)S(1)}, u32[]{:S(2)}, u32[]{:S(2)}) collective-permute-start(bf16[1,1024,512]{2,1,0:T(8,128)(2,1)S(1)} %widen.3.refs_3_.refs_0_), channel_id=1, source_target_pairs={{0,4},{4,0},{8,12},{12,8},{16,20},{20,16},{24,28},{28,24},{32,36},... | collective-permute-start | bytes 3145736 | tf_op jit(solution)/shard_map/ppermute | solution.py:385
  91.7 9.1 %collective-permute-start.13 = (bf16[1,1024,512]{2,1,0:T(8,128)(2,1)}, bf16[1,1024,512]{2,1,0:T(8,128)(2,1)S(1)}, u32[]{:S(2)}, u32[]{:S(2)}) collective-permute-start(bf16[1,1024,512]{2,1,0:T(8,128)(2,1)} %copy-done.7), channel_id=1, source_target_pairs={{0,4},{4,0},{8,12},{12,8},{16,20},{20,16},{24,28},{28,24},{32,36},... | collective-permute-start | bytes 3145736 | tf_op jit(solution)/shard_map/ppermute | solution.py:385
  98.1 2.8 %copy-start.18 = (bf16[1,1024,512]{2,1,0:T(8,128)(2,1)}, bf16[1,1024,512]{2,1,0:T(8,128)(2,1)S(1)}, u32[]{:S(2)}) copy-start(bf16[1,1024,512]{2,1,0:T(8,128)(2,1)S(1)} %collective-permute-done.9.refs_5_) | copy-start | bytes 3145732
  (13 other events, 13.3 us)
Sparse Core Ops, SparseCore 0:
  9.7 46.9 all-gather.4
  83.1 45.0 all-gather.6

commit v9 on v7

--- a/solution.py
+++ b/solution.py
@@ -306,6 +306,9 @@
     )(mine, other, masks)
 
 
+KEPT = 2
+
+
 def cube_kernel(table_ref, *refs):
     *lists, square_hbm, tile_ref, masks_ref, out_ref, acc, square_ref, held, sems = refs
     scale = (NB / (KX * KSQ * B)) ** 0.5
@@ -314,17 +317,21 @@
     fetches, begins, start = [], [], 0
     for at, ref in enumerate(lists):
         count = ref.shape[0]
-        fetches.append(pltpu.make_async_copy(ref, held.at[pl.ds(start, count)], sems.at[at]))
-        fetches[-1].start()
+        fetch = pltpu.make_async_copy(ref, held.at[pl.ds(start, count)], sems.at[at])
+        if at >= KEPT:
+            fetch.start()
+        fetches.append(fetch)
         begins.append(start)
         start += count
     first.wait()
-    for ref, fetch, begin in zip(lists, fetches, begins):
-        fetch.wait()
+    for at, (ref, fetch, begin) in enumerate(zip(lists, fetches, begins)):
+        if at >= KEPT:
+            fetch.wait()
         for k in range(begin, begin + ref.shape[0]):
             g, core = table_ref[2 * k], table_ref[2 * k + 1]
             half = square_ref[g, pl.ds(pl.multiple_of(core * HALF, HALF), HALF), :]
-            term = jnp.dot(held[k], half, preferred_element_type=F32)
+            left = held[k] if at >= KEPT else ref[k - begin]
+            term = jnp.dot(left, half, preferred_element_type=F32)
             acc[...] = term if k == 0 else acc[...] + term
     for k in range(BR):
         rows = pl.ds(k * B, B)
@@ -339,7 +346,7 @@
     return pl.pallas_call(
         cube_kernel,
         out_shape=jax.ShapeDtypeStruct((ROWS, W), BF16),
-        in_specs=[SMEM] + [HBM] * (len(lists) + 1) + [VMEM] * 2,
+        in_specs=[SMEM] + [VMEM] * KEPT + [HBM] * (len(lists) + 1 - KEPT) + [VMEM] * 2,
         out_specs=VMEM,
         scratch_shapes=[
             pltpu.VMEM((ROWS, W), F32),
@@ -347,7 +354,7 @@
             pltpu.VMEM((2 * (FIRST + 1), ROWS, HALF), BF16),
             pltpu.SemaphoreType.DMA((len(lists) + 1,)),
         ],
-        compiler_params=params(60),
+        compiler_params=params(52),
         cost_estimate=cost(2 * GROUPS * ROWS * ROWS * W, 20 * MIB),
         name="cube",
     )(table, *lists, squares, tile, masks)

time: 149 us -> 149 us (level)
    unnamed x40 -> x38, local copies, waits for them, and re-layouts: 13.3 us -> 14 us
where the time goes in v9:
time: 149 us; the launch traced here: 148 us
  waiting for transfers between devices  45.8 us (31%)
  starting transfers between devices  31 us (21%)
  Pallas kernels  29.8 us (20%)
  local copies, waits for them, and re-layouts  14.1 us (9%)
  blocking collectives  13.9 us (9%)
  between operations  13.7 us (9%)
    all_gather x1, waiting for transfers between devices, local(): squares = lax.all_gather(square, 'row', axis=0, tiled=False)  26.4 us
    ppermute x8, starting transfers between devices, across(): return lax.ppermute(piece, 'col', swap)  16.9 us
    ppermute x7, starting transfers between devices, along_y(): return lax.ppermute(piece, 'col', turn_y)  14.1 us
    unnamed x38, local copies, waits for them, and re-layouts  14 us
    all_to_all x1, blocking collectives, local(): a0 = lax.all_to_all(left, 'layer', 0, 0, tiled=True)  13.9 us
    pallas_call x1, Pallas kernels, cube(): pl.pallas_call(cube_kernel, out_shape=jax.ShapeDtypeStruct((ROWS, W), BF1...  13.2 us
    ppermute x7, waiting for transfers between devices, along_y(): return lax.ppermute(piece, 'col', turn_y)  12.4 us
    ppermute x8, waiting for transfers between devices, across(): return lax.ppermute(piece, 'col', swap)  6.99 us
  transfers between devices with their start and end apart: 17, of which 10 were waited for; matrix products, arithmetic and copies ran while one was open for 0% of the time, Pallas kernels for 9%

profile of v9, /device:TPU:2, one launch (start us, length us, event | category | flops | bytes accessed | tf_op | source)
XLA Modules:
  0.0 148.3 jit_solution(7066909982708533156)
XLA Ops:
  9.7 13.9 %all_to_all.5.refs_0_ = bf16[4,10,32,128]{3,2,1,0:T(8,128)(2,1)S(1)} all-to-all(bf16[4,10,32,128]{3,2,1,0:T(8,128)(2,1)S(1)} %get-tuple-element.19), channel_id=1, replica_groups=mesh['row'=8,'col'=16,'layer'=4] {'layer'}, dimensions={0} | all-to-all | bytes 655360 | tf_op jit(solution)/shard_map/all_to_all | solution.py:393
  23.5 1.9 %collective-permute-start.1 = (bf16[4,10,32,128]{3,2,1,0:T(8,128)(2,1)S(1)}, bf16[4,10,32,128]{3,2,1,0:T(8,128)(2,1)S(1)}, u32[]{:S(2)}, u32[]{:S(2)}) collective-permute-start(bf16[4,10,32,128]{3,2,1,0:T(8,128)(2,1)S(1)} %all_to_all.5.refs_0_), channel_id=1, source_target_pairs={{0,4},{4,0},{8,12},{12,8},{16,20},{20,16},{24,28},{28,24},{32,36},... | collective-permute-start | bytes 983048 | tf_op jit(solution)/shard_map/ppermute | solution.py:386
  25.4 1.9 %collective-permute-start = (bf16[4,10,32,128]{3,2,1,0:T(8,128)(2,1)S(1)}, bf16[4,10,32,128]{3,2,1,0:T(8,128)(2,1)}, u32[]{:S(2)}, u32[]{:S(2)}) collective-permute-start(bf16[4,10,32,128]{3,2,1,0:T(8,128)(2,1)S(1)} %all_to_all.5.refs_0_), channel_id=1, source_target_pairs={{0,8},{4,60},{8,16},{12,4},{16,24},{20,12},{24,32},{28,20},{32,40}... | collective-permute-start | bytes 983048 | tf_op jit(solution)/shard_map/ppermute | solution.py:383
  27.4 1.9 %collective-permute-start.2 = (bf16[4,10,32,128]{3,2,1,0:T(8,128)(2,1)S(1)}, bf16[4,10,32,128]{3,2,1,0:T(8,128)(2,1)}, u32[]{:S(2)}, u32[]{:S(2)}) collective-permute-start(bf16[4,10,32,128]{3,2,1,0:T(8,128)(2,1)S(1)} %collective-permute-done.1), channel_id=1, source_target_pairs={{0,8},{4,60},{8,16},{12,4},{16,24},{20,12},{24,32},{28,20},{32,40}... | collective-permute-start | bytes 983048 | tf_op jit(solution)/shard_map/ppermute | solution.py:383
  33.8 1.9 %collective-permute-done.refs_0_ = bf16[4,10,32,128]{3,2,1,0:T(8,128)(2,1)} collective-permute-done((bf16[4,10,32,128]{3,2,1,0:T(8,128)(2,1)S(1)}, bf16[4,10,32,128]{3,2,1,0:T(8,128)(2,1)}, u32[]{:S(2)}, u32[]{:S(2)}) %collective-permute-start) | collective-permute-done | bytes 327712 | tf_op jit(solution)/shard_map/ppermute | solution.py:383
  39.2 2.6 %collective-permute-start.4 = (bf16[4,10,32,128]{3,2,1,0:T(8,128)(2,1)}, bf16[4,10,32,128]{3,2,1,0:T(8,128)(2,1)S(1)}, u32[]{:S(2)}, u32[]{:S(2)}) collective-permute-start(bf16[4,10,32,128]{3,2,1,0:T(8,128)(2,1)} %collective-permute-done.2.refs_1_), channel_id=1, source_target_pairs={{0,8},{4,60},{8,16},{12,4},{16,24},{20,12},{24,32},{28,20},{32,40}... | collective-permute-start | bytes 983048 | tf_op jit(solution)/shard_map/ppermute | solution.py:383
  41.8 2.1 %widen.4.refs_4_.refs_1_ = bf16[2,1024,512]{2,1,0:T(8,128)(2,1)S(1)} custom-call(s32[32]{0:T(128)S(1)} %stack.68.table_ref, s32[10,256]{1,0:T(8,128)S(1)} %get-tuple-element.18.places_ref, bf16[4,10,32,128]{3,2,1,0:T(8,128)(2,1)} %collective-permute-done.refs_0_, bf16[4,10,32,128]{3,2,1,0:T(8,128)(2,1)} %collective-permute-done.2.refs_1_), custom_call_target="tpu_custom_call" | custom-call | flops 536870912 | bytes 6291456 | tf_op jit(solution)/shard_map/widen/pallas_call | solution.py:198
  43.9 2.2 %collective-permute-done.3.refs_0_ = bf16[4,10,32,128]{3,2,1,0:T(8,128)(2,1)S(1)} collective-permute-done((bf16[4,10,32,128]{3,2,1,0:T(8,128)(2,1)}, bf16[4,10,32,128]{3,2,1,0:T(8,128)(2,1)S(1)}, u32[]{:S(2)}, u32[]{:S(2)}) %collective-permute-start.3) | collective-permute-done | bytes 327712 | tf_op jit(solution)/shard_map/ppermute | solution.py:383
  46.1 1.9 %collective-permute-start.5 = (bf16[4,10,32,128]{3,2,1,0:T(8,128)(2,1)S(1)}, bf16[4,10,32,128]{3,2,1,0:T(8,128)(2,1)S(1)}, u32[]{:S(2)}, u32[]{:S(2)}) collective-permute-start(bf16[4,10,32,128]{3,2,1,0:T(8,128)(2,1)S(1)} %collective-permute-done.3.refs_0_), channel_id=1, source_target_pairs={{0,8},{4,60},{8,16},{12,4},{16,24},{20,12},{24,32},{28,20},{32,40}... | collective-permute-start | bytes 983048 | tf_op jit(solution)/shard_map/ppermute | solution.py:383
  49.6 1.9 %collective-permute-start.6 = (bf16[4,10,32,128]{3,2,1,0:T(8,128)(2,1)S(1)}, bf16[4,10,32,128]{3,2,1,0:T(8,128)(2,1)S(1)}, u32[]{:S(2)}, u32[]{:S(2)}) collective-permute-start(bf16[4,10,32,128]{3,2,1,0:T(8,128)(2,1)S(1)} %collective-permute-done.4.refs_1_), channel_id=1, source_target_pairs={{0,8},{4,60},{8,16},{12,4},{16,24},{20,12},{24,32},{28,20},{32,40}... | collective-permute-start | bytes 983048 | tf_op jit(solution)/shard_map/ppermute | solution.py:383
  56.3 3.5 %collective-permute-done.6.refs_1_ = bf16[4,10,32,128]{3,2,1,0:T(8,128)(2,1)S(1)} collective-permute-done((bf16[4,10,32,128]{3,2,1,0:T(8,128)(2,1)S(1)}, bf16[4,10,32,128]{3,2,1,0:T(8,128)(2,1)S(1)}, u32[]{:S(2)}, u32[]{:S(2)}) %collective-permute-start.6) | collective-permute-done | bytes 327712 | tf_op jit(solution)/shard_map/ppermute | solution.py:383
  60.5 2.0 %collective-permute-start.7 = (bf16[8,576,128]{2,1,0:T(8,128)(2,1)}, bf16[8,576,128]{2,1,0:T(8,128)(2,1)S(1)}, u32[]{:S(2)}, u32[]{:S(2)}) collective-permute-start(bf16[8,576,128]{2,1,0:T(8,128)(2,1)} %bitcast.14), channel_id=1, source_target_pairs={{0,4},{4,0},{8,12},{12,8},{16,20},{20,16},{24,28},{28,24},{32,36},... | collective-permute-start | bytes 3538952 | tf_op jit(solution)/shard_map/ppermute | solution.py:386
  62.6 1.9 %collective-permute-start.8 = (bf16[4,10,32,128]{3,2,1,0:T(8,128)(2,1)S(1)}, bf16[4,10,32,128]{3,2,1,0:T(8,128)(2,1)S(1)}, u32[]{:S(2)}, u32[]{:S(2)}) collective-permute-start(bf16[4,10,32,128]{3,2,1,0:T(8,128)(2,1)S(1)} %collective-permute-done.5.refs_0_), channel_id=1, source_target_pairs={{0,8},{4,60},{8,16},{12,4},{16,24},{20,12},{24,32},{28,20},{32,40}... | collective-permute-start | bytes 983048 | tf_op jit(solution)/shard_map/ppermute | solution.py:383
  66.9 2.8 %right.1.refs_2_.right_ref = bf16[8,512,256]{2,1,0:T(8,128)(2,1)S(1)} custom-call(s32[32]{0:T(128)S(1)} %stack.68.table_ref, bf16[8,576,128]{2,1,0:T(8,128)(2,1)S(1)} %bitcast.15, bf16[8,576,128]{2,1,0:T(8,128)(2,1)S(1)} %collective-permute-done.7.other_hbm), custom_call_target="tpu_custom_call" | custom-call | flops 40000000 | bytes 4194304 | tf_op jit(solution)/shard_map/right/pallas_call | solution.py:155
  69.7 4.5 %product.1 = (bf16[2,1024,512]{2,1,0:T(8,128)(2,1)S(1)}, f32[1024,256]{1,0:T(8,128)S(1)}) custom-call(s32[32]{0:T(128)S(1)} %stack.68.table_ref, s32[10,256]{1,0:T(8,128)S(1)} %get-tuple-element.18.places_ref, bf16[4,10,32,128]{3,2,1,0:T(8,128)(2,1)S(1)} %collective-permute-done.5.refs_0_, bf16[4,10,32,128]{3,2,1,0:T(8,128)(2,1)S(1)} %copy-done.10, ...), custom_call_target="tpu_custom_call" | custom-call | flops 1073741824 | bytes 12582912 | tf_op jit(solution)/shard_map/product/pallas_call | solution.py:236
  78.4 2.0 %collective-permute-start.14 = (f32[1024,128]{1,0:T(8,128)S(1)}, f32[1024,128]{1,0:T(8,128)S(1)}, u32[]{:S(2)}, u32[]{:S(2)}) collective-permute-start(f32[1024,128]{1,0:T(8,128)S(1)} %get-tuple-element.30), channel_id=1, source_target_pairs={{0,4},{4,0},{8,12},{12,8},{16,20},{20,16},{24,28},{28,24},{32,36},... | collective-permute-start | bytes 1572872 | tf_op jit(solution)/shard_map/ppermute | solution.py:386
  83.1 2.0 %collective-permute-start.10 = (bf16[2,1024,512]{2,1,0:T(8,128)(2,1)S(1)}, bf16[2,1024,512]{2,1,0:T(8,128)(2,1)S(1)}, u32[]{:S(2)}, u32[]{:S(2)}) collective-permute-start(bf16[2,1024,512]{2,1,0:T(8,128)(2,1)S(1)} %widen.4.refs_4_.refs_1_), channel_id=1, source_target_pairs={{0,4},{4,0},{8,12},{12,8},{16,20},{20,16},{24,28},{28,24},{32,36},... | collective-permute-start | bytes 6291464 | tf_op jit(solution)/shard_map/ppermute | solution.py:386
  85.1 2.3 %collective-permute-start.11 = (bf16[2,1024,512]{2,1,0:T(8,128)(2,1)}, bf16[2,1024,512]{2,1,0:T(8,128)(2,1)S(1)}, u32[]{:S(2)}, u32[]{:S(2)}) collective-permute-start(bf16[2,1024,512]{2,1,0:T(8,128)(2,1)} %copy-done.1), channel_id=1, source_target_pairs={{0,4},{4,0},{8,12},{12,8},{16,20},{20,16},{24,28},{28,24},{32,36},... | collective-permute-start | bytes 6291464 | tf_op jit(solution)/shard_map/ppermute | solution.py:386
  87.4 2.0 %collective-permute-start.12 = (bf16[2,1024,512]{2,1,0:T(8,128)(2,1)}, bf16[2,1024,512]{2,1,0:T(8,128)(2,1)}, u32[]{:S(2)}, u32[]{:S(2)}) collective-permute-start(bf16[2,1024,512]{2,1,0:T(8,128)(2,1)} %copy-done.3), channel_id=1, source_target_pairs={{0,4},{4,0},{8,12},{12,8},{16,20},{20,16},{24,28},{28,24},{32,36},... | collective-permute-start | bytes 6291464 | tf_op jit(solution)/shard_map/ppermute | solution.py:386
  89.5 2.3 %collective-permute-start.9 = (bf16[1,1024,512]{2,1,0:T(8,128)(2,1)S(1)}, bf16[1,1024,512]{2,1,0:T(8,128)(2,1)S(1)}, u32[]{:S(2)}, u32[]{:S(2)}) collective-permute-start(bf16[1,1024,512]{2,1,0:T(8,128)(2,1)S(1)} %widen.3.refs_3_.refs_0_), channel_id=1, source_target_pairs={{0,4},{4,0},{8,12},{12,8},{16,20},{20,16},{24,28},{28,24},{32,36},... | collective-permute-start | bytes 3145736 | tf_op jit(solution)/shard_map/ppermute | solution.py:386
  91.7 2.2 %collective-permute-start.13 = (bf16[1,1024,512]{2,1,0:T(8,128)(2,1)}, bf16[1,1024,512]{2,1,0:T(8,128)(2,1)S(1)}, u32[]{:S(2)}, u32[]{:S(2)}) collective-permute-start(bf16[1,1024,512]{2,1,0:T(8,128)(2,1)} %copy-done.7), channel_id=1, source_target_pairs={{0,4},{4,0},{8,12},{12,8},{16,20},{20,16},{24,28},{28,24},{32,36},... | collective-permute-start | bytes 3145736 | tf_op jit(solution)/shard_map/ppermute | solution.py:386
  94.0 4.1 %collective-permute-done.9.refs_5_ = bf16[1,1024,512]{2,1,0:T(8,128)(2,1)S(1)} collective-permute-done((bf16[1,1024,512]{2,1,0:T(8,128)(2,1)S(1)}, bf16[1,1024,512]{2,1,0:T(8,128)(2,1)S(1)}, u32[]{:S(2)}, u32[]{:S(2)}) %collective-permute-start.9) | collective-permute-done | bytes 1048608 | tf_op jit(solution)/shard_map/ppermute | solution.py:386
  101.9 26.4 %all-gather.7.cloned.1.call-done = bf16[8192,128]{1,0:T(8,128)(2,1)} async-done(((bf16[1024,128]{1,0:T(8,128)(2,1)}), bf16[8192,128]{1,0:T(8,128)(2,1)}) %all-gather.7.cloned.1.call-update) | async-done | bytes 2097168 | tf_op jit(solution)/shard_map/all_gather | solution.py:409
  128.2 13.2 %cube.1 = bf16[1024,128]{1,0:T(8,128)(2,1)} custom-call(s32[32]{0:T(128)S(1)} %stack.68.table_ref, bf16[1,1024,512]{2,1,0:T(8,128)(2,1)S(1)} %widen.3.refs_3_.refs_0_, bf16[2,1024,512]{2,1,0:T(8,128)(2,1)} %copy-done, bf16[2,1024,512]{2,1,0:T(8,128)(2,1)} %copy-done.1, bf16[2,1024,512]{2,1,0:T(8,128)(2,1)} %copy-done.3, bf16[1,1024,512]{2,1,0:T(8,128)(2,1)} %copy-done.7, ...), custom_call_target="tpu_custom_call" | custom-call | flops 2147483648 | bytes 20971520 | tf_op jit(solution)/shard_map/cube/pallas_call | solution.py:346
  (62 shorter events, 31.0 us)
Async XLA Ops:
  6.5 54.0 %all-gather.5.cloned.1.call-start = ((), (), s32[]{:S(2)}) async-start(), calls=%async_computation.1 | async-start | bytes 1327104 | tf_op jit(solution)/shard_map/all_gather | solution.py:392
  9.6 118.6 %all-gather.7.cloned.1.call-start = ((), (), s32[]{:S(2)}) async-start(), calls=%async_computation.2 | async-start | bytes 2359296 | tf_op jit(solution)/shard_map/all_gather | solution.py:409
  23.5 3.8 %collective-permute-start.1 = (bf16[4,10,32,128]{3,2,1,0:T(8,128)(2,1)S(1)}, bf16[4,10,32,128]{3,2,1,0:T(8,128)(2,1)S(1)}, u32[]{:S(2)}, u32[]{:S(2)}) collective-permute-start(bf16[4,10,32,128]{3,2,1,0:T(8,128)(2,1)S(1)} %all_to_all.5.refs_0_), channel_id=1, source_target_pairs={{0,4},{4,0},{8,12},{12,8},{16,20},{20,16},{24,28},{28,24},{32,36},... | collective-permute-start | bytes 983048 | tf_op jit(solution)/shard_map/ppermute | solution.py:386
  25.4 10.3 %collective-permute-start = (bf16[4,10,32,128]{3,2,1,0:T(8,128)(2,1)S(1)}, bf16[4,10,32,128]{3,2,1,0:T(8,128)(2,1)}, u32[]{:S(2)}, u32[]{:S(2)}) collective-permute-start(bf16[4,10,32,128]{3,2,1,0:T(8,128)(2,1)S(1)} %all_to_all.5.refs_0_), channel_id=1, source_target_pairs={{0,8},{4,60},{8,16},{12,4},{16,24},{20,12},{24,32},{28,20},{32,40}... | collective-permute-start | bytes 983048 | tf_op jit(solution)/shard_map/ppermute | solution.py:383
  27.4 11.9 %collective-permute-start.2 = (bf16[4,10,32,128]{3,2,1,0:T(8,128)(2,1)S(1)}, bf16[4,10,32,128]{3,2,1,0:T(8,128)(2,1)}, u32[]{:S(2)}, u32[]{:S(2)}) collective-permute-start(bf16[4,10,32,128]{3,2,1,0:T(8,128)(2,1)S(1)} %collective-permute-done.1), channel_id=1, source_target_pairs={{0,8},{4,60},{8,16},{12,4},{16,24},{20,12},{24,32},{28,20},{32,40}... | collective-permute-start | bytes 983048 | tf_op jit(solution)/shard_map/ppermute | solution.py:383
  35.7 10.4 %collective-permute-start.3 = (bf16[4,10,32,128]{3,2,1,0:T(8,128)(2,1)}, bf16[4,10,32,128]{3,2,1,0:T(8,128)(2,1)S(1)}, u32[]{:S(2)}, u32[]{:S(2)}) collective-permute-start(bf16[4,10,32,128]{3,2,1,0:T(8,128)(2,1)} %collective-permute-done.refs_0_), channel_id=1, source_target_pairs={{0,8},{4,60},{8,16},{12,4},{16,24},{20,12},{24,32},{28,20},{32,40}... | collective-permute-start | bytes 983048 | tf_op jit(solution)/shard_map/ppermute | solution.py:383
  39.2 10.4 %collective-permute-start.4 = (bf16[4,10,32,128]{3,2,1,0:T(8,128)(2,1)}, bf16[4,10,32,128]{3,2,1,0:T(8,128)(2,1)S(1)}, u32[]{:S(2)}, u32[]{:S(2)}) collective-permute-start(bf16[4,10,32,128]{3,2,1,0:T(8,128)(2,1)} %collective-permute-done.2.refs_1_), channel_id=1, source_target_pairs={{0,8},{4,60},{8,16},{12,4},{16,24},{20,12},{24,32},{28,20},{32,40}... | collective-permute-start | bytes 983048 | tf_op jit(solution)/shard_map/ppermute | solution.py:383
  43.9 39.1 %copy-start = (bf16[2,1024,512]{2,1,0:T(8,128)(2,1)}, bf16[2,1024,512]{2,1,0:T(8,128)(2,1)S(1)}, u32[]{:S(2)}) copy-start(bf16[2,1024,512]{2,1,0:T(8,128)(2,1)S(1)} %widen.4.refs_4_.refs_1_) | copy-start | bytes 6291460
  46.1 10.2 %collective-permute-start.5 = (bf16[4,10,32,128]{3,2,1,0:T(8,128)(2,1)S(1)}, bf16[4,10,32,128]{3,2,1,0:T(8,128)(2,1)S(1)}, u32[]{:S(2)}, u32[]{:S(2)}) collective-permute-start(bf16[4,10,32,128]{3,2,1,0:T(8,128)(2,1)S(1)} %collective-permute-done.3.refs_0_), channel_id=1, source_target_pairs={{0,8},{4,60},{8,16},{12,4},{16,24},{20,12},{24,32},{28,20},{32,40}... | collective-permute-start | bytes 983048 | tf_op jit(solution)/shard_map/ppermute | solution.py:383
  49.6 10.2 %collective-permute-start.6 = (bf16[4,10,32,128]{3,2,1,0:T(8,128)(2,1)S(1)}, bf16[4,10,32,128]{3,2,1,0:T(8,128)(2,1)S(1)}, u32[]{:S(2)}, u32[]{:S(2)}) collective-permute-start(bf16[4,10,32,128]{3,2,1,0:T(8,128)(2,1)S(1)} %collective-permute-done.4.refs_1_), channel_id=1, source_target_pairs={{0,8},{4,60},{8,16},{12,4},{16,24},{20,12},{24,32},{28,20},{32,40}... | collective-permute-start | bytes 983048 | tf_op jit(solution)/shard_map/ppermute | solution.py:383
  60.5 9.1 %copy-start.2 = (bf16[2,1024,512]{2,1,0:T(8,128)(2,1)S(1)}, bf16[2,1024,512]{2,1,0:T(8,128)(2,1)}, u32[]{:S(2)}) copy-start(bf16[2,1024,512]{2,1,0:T(8,128)(2,1)} %copy-done.1) | copy-start | bytes 6291460
  60.5 5.1 %collective-permute-start.7 = (bf16[8,576,128]{2,1,0:T(8,128)(2,1)}, bf16[8,576,128]{2,1,0:T(8,128)(2,1)S(1)}, u32[]{:S(2)}, u32[]{:S(2)}) collective-permute-start(bf16[8,576,128]{2,1,0:T(8,128)(2,1)} %bitcast.14), channel_id=1, source_target_pairs={{0,4},{4,0},{8,12},{12,8},{16,20},{20,16},{24,28},{28,24},{32,36},... | collective-permute-start | bytes 3538952 | tf_op jit(solution)/shard_map/ppermute | solution.py:386
  62.6 13.0 %collective-permute-start.8 = (bf16[4,10,32,128]{3,2,1,0:T(8,128)(2,1)S(1)}, bf16[4,10,32,128]{3,2,1,0:T(8,128)(2,1)S(1)}, u32[]{:S(2)}, u32[]{:S(2)}) collective-permute-start(bf16[4,10,32,128]{3,2,1,0:T(8,128)(2,1)S(1)} %collective-permute-done.5.refs_0_), channel_id=1, source_target_pairs={{0,8},{4,60},{8,16},{12,4},{16,24},{20,12},{24,32},{28,20},{32,40}... | collective-permute-start | bytes 983048 | tf_op jit(solution)/shard_map/ppermute | solution.py:383
  66.9 2.8 %copy-start.10 = (bf16[4,10,32,128]{3,2,1,0:T(8,128)(2,1)S(1)}, bf16[4,10,32,128]{3,2,1,0:T(8,128)(2,1)}, u32[]{:S(2)}) copy-start(bf16[4,10,32,128]{3,2,1,0:T(8,128)(2,1)} %copy-done.9) | copy-start | bytes 983044
  74.2 1.4 copy-start.3
  75.6 52.6 %copy-start.6 = (bf16[1024,128]{1,0:T(8,128)(2,1)S(1)}, bf16[1024,128]{1,0:T(8,128)(2,1)}, u32[]{:S(2)}) copy-start(bf16[1024,128]{1,0:T(8,128)(2,1)} %refs_11_.1) | copy-start | bytes 786436
  78.4 3.8 %collective-permute-start.14 = (f32[1024,128]{1,0:T(8,128)S(1)}, f32[1024,128]{1,0:T(8,128)S(1)}, u32[]{:S(2)}, u32[]{:S(2)}) collective-permute-start(f32[1024,128]{1,0:T(8,128)S(1)} %get-tuple-element.30), channel_id=1, source_target_pairs={{0,4},{4,0},{8,12},{12,8},{16,20},{20,16},{24,28},{28,24},{32,36},... | collective-permute-start | bytes 1572872 | tf_op jit(solution)/shard_map/ppermute | solution.py:386
  83.1 15.1 %collective-permute-start.10 = (bf16[2,1024,512]{2,1,0:T(8,128)(2,1)S(1)}, bf16[2,1024,512]{2,1,0:T(8,128)(2,1)S(1)}, u32[]{:S(2)}, u32[]{:S(2)}) collective-permute-start(bf16[2,1024,512]{2,1,0:T(8,128)(2,1)S(1)} %widen.4.refs_4_.refs_1_), channel_id=1, source_target_pairs={{0,4},{4,0},{8,12},{12,8},{16,20},{20,16},{24,28},{28,24},{32,36},... | collective-permute-start | bytes 6291464 | tf_op jit(solution)/shard_map/ppermute | solution.py:386
  85.1 14.4 %collective-permute-start.11 = (bf16[2,1024,512]{2,1,0:T(8,128)(2,1)}, bf16[2,1024,512]{2,1,0:T(8,128)(2,1)S(1)}, u32[]{:S(2)}, u32[]{:S(2)}) collective-permute-start(bf16[2,1024,512]{2,1,0:T(8,128)(2,1)} %copy-done.1), channel_id=1, source_target_pairs={{0,4},{4,0},{8,12},{12,8},{16,20},{20,16},{24,28},{28,24},{32,36},... | collective-permute-start | bytes 6291464 | tf_op jit(solution)/shard_map/ppermute | solution.py:386
  87.4 14.5 %collective-permute-start.12 = (bf16[2,1024,512]{2,1,0:T(8,128)(2,1)}, bf16[2,1024,512]{2,1,0:T(8,128)(2,1)}, u32[]{:S(2)}, u32[]{:S(2)}) collective-permute-start(bf16[2,1024,512]{2,1,0:T(8,128)(2,1)} %copy-done.3), channel_id=1, source_target_pairs={{0,4},{4,0},{8,12},{12,8},{16,20},{20,16},{24,28},{28,24},{32,36},... | collective-permute-start | bytes 6291464 | tf_op jit(solution)/shard_map/ppermute | solution.py:386
  89.5 8.7 %collective-permute-start.9 = (bf16[1,1024,512]{2,1,0:T(8,128)(2,1)S(1)}, bf16[1,1024,512]{2,1,0:T(8,128)(2,1)S(1)}, u32[]{:S(2)}, u32[]{:S(2)}) collective-permute-start(bf16[1,1024,512]{2,1,0:T(8,128)(2,1)S(1)} %widen.3.refs_3_.refs_0_), channel_id=1, source_target_pairs={{0,4},{4,0},{8,12},{12,8},{16,20},{20,16},{24,28},{28,24},{32,36},... | collective-permute-start | bytes 3145736 | tf_op jit(solution)/shard_map/ppermute | solution.py:386
  91.7 9.1 %collective-permute-start.13 = (bf16[1,1024,512]{2,1,0:T(8,128)(2,1)}, bf16[1,1024,512]{2,1,0:T(8,128)(2,1)S(1)}, u32[]{:S(2)}, u32[]{:S(2)}) collective-permute-start(bf16[1,1024,512]{2,1,0:T(8,128)(2,1)} %copy-done.7), channel_id=1, source_target_pairs={{0,4},{4,0},{8,12},{12,8},{16,20},{20,16},{24,28},{28,24},{32,36},... | collective-permute-start | bytes 3145736 | tf_op jit(solution)/shard_map/ppermute | solution.py:386
  98.1 2.8 %copy-start.17 = (bf16[1,1024,512]{2,1,0:T(8,128)(2,1)}, bf16[1,1024,512]{2,1,0:T(8,128)(2,1)S(1)}, u32[]{:S(2)}) copy-start(bf16[1,1024,512]{2,1,0:T(8,128)(2,1)S(1)} %collective-permute-done.9.refs_5_) | copy-start | bytes 3145732
  99.5 1.4 copy-start.16
  (12 other events, 11.2 us)
Sparse Core Ops, SparseCore 0:
  9.7 46.9 all-gather.4
  83.2 45.0 all-gather.6
